TPU v7x, 256 devices: a whole 4x4x8 slice. The times are simulated.
256 devices in a mesh: pre: 16 (over y, x), seq: 8 (over z), dec: 2 (over core).
Axes of the slice: x: 4, y: 4, z: 8, core: 2. Of those that a mesh axis runs over, the one named last changes fastest.
Arguments:
- block_pool: bfloat16 [16, 8, 2, 80, 128, 576], P('pre', 'seq', 'dec'), may hold values from -6 to 6
- block_table: int32 [16, 8, 2, 128], P('pre', 'seq', 'dec'), may hold values from 0 to 79, as said below
- lengths: int32 [16, 16], P('pre'), may hold values from 1 to 16384, as said below
- destination: int32 [16, 16], P('pre'), may hold values from 0 to 15, each once within a row
- query_latent: bfloat16 [16, 16, 2, 128, 576], P('pre', None, None, ('seq', 'dec'))
- new_latent: bfloat16 [16, 16, 2, 576], P('pre')
- value_proj: bfloat16 [128, 512, 128], P(('seq', 'dec')), may hold values from -0.25 to 0.25
Outputs:
- attended: bfloat16 [16, 16, 2, 16384], P('pre', None, None, ('seq', 'dec'))
Inputs may be any that keep to these rules, and one draw needn't show every extreme that they name: `block_table`: on each device, the slots of a request that hold positions below its length name distinct pool blocks; other slots name any block. `destination`: each prefill device's row names every code 0 to 15 once. Each prefill device's lengths sum to 131072, and one of them is 16384.
All inputs are finite; a program needn't handle non-finite values.
Results may differ from a plain program's by a relative error of at most 0.0051.
Values may be sent and summed in bfloat16 or wider, within the bound.
No kernel may reach another device: no remote copies, remote signals or barrier semaphores. Data moves between devices by JAX's collectives and lax.ppermute only.
A program may use at most 192 MiB of HBM per device.

v0:
```python
import jax
import jax.numpy as jnp
from jax import lax
from jax.sharding import PartitionSpec as P

score_scale = 192.0 ** (-0.5)


def attend(blocks, req_lengths, query_part, new_keys, value_proj):
    split_index = lax.axis_index(("seq", "dec"))
    split_count = lax.axis_size(("seq", "dec"))
    requests, slots, block_len, width = blocks.shape
    head_part = value_proj.shape[0]
    latent_width = value_proj.shape[1]
    value_width = value_proj.shape[2]
    queries = lax.all_gather(query_part, ("seq", "dec"), axis=2, tiled=True)
    steps = queries.shape[1]
    heads = queries.shape[2]
    query_rows = queries.reshape(requests, steps * heads, width)
    cached = blocks.reshape(requests, slots * block_len, width)
    token_ids = jnp.arange(slots * block_len, dtype=jnp.int32)
    position = (
        token_ids // block_len * split_count + split_index
    ) * block_len + token_ids % block_len

    def score_one(items):
        rows, keys, length = items
        raw = jnp.dot(rows, keys.T, preferred_element_type=jnp.float32) * score_scale
        raw = jnp.where((position < length)[None, :], raw, -jnp.inf)
        return (raw, jnp.max(raw, axis=-1))

    scores, cache_top = lax.map(score_one, (query_rows, cached, req_lengths))
    new_scores = (
        jnp.einsum("rqc,rkc->rqk", query_rows, new_keys, preferred_element_type=jnp.float32)
        * score_scale
    )
    row_step = jnp.arange(steps * heads, dtype=jnp.int32) // heads
    causal = jnp.arange(steps, dtype=jnp.int32)[None, :] <= row_step[:, None]
    new_scores = jnp.where(causal[None], new_scores, -jnp.inf)
    local_top = jnp.maximum(cache_top, jnp.max(new_scores, axis=-1))
    global_top = lax.pmax(local_top, ("seq", "dec"))

    def weigh_one(items):
        raw, keys, top = items
        weights = jnp.exp(raw - top[:, None])
        total = jnp.sum(weights, axis=-1)
        partial_sum = jnp.dot(
            weights.astype(jnp.bfloat16), keys[:, :latent_width], preferred_element_type=jnp.float32
        )
        return (total, partial_sum)

    denominator, numerator = lax.map(weigh_one, (scores, cached, global_top))
    denominator = denominator.reshape(requests, steps, heads)
    numerator = numerator.reshape(requests, steps, heads, latent_width)
    numerator, denominator = (
        lax.psum_scatter(numerator, ("seq", "dec"), scatter_dimension=2, tiled=True),
        lax.psum_scatter(denominator, ("seq", "dec"), scatter_dimension=2, tiled=True),
    )
    first_head = split_index * head_part
    own_new = lax.dynamic_slice_in_dim(
        new_scores.reshape(requests, steps, heads, steps), first_head, head_part, 2
    )
    own_top = lax.dynamic_slice_in_dim(
        global_top.reshape(requests, steps, heads), first_head, head_part, 2
    )
    new_weights = jnp.exp(own_new - own_top[..., None])
    denominator = denominator + jnp.sum(new_weights, axis=-1)
    numerator = numerator + jnp.einsum(
        "rshj,rjc->rshc",
        new_weights.astype(jnp.bfloat16),
        new_keys[:, :, :latent_width],
        preferred_element_type=jnp.float32,
    )
    latent = (numerator / denominator[..., None]).astype(jnp.bfloat16)
    values = jnp.einsum(
        "rshc,hcv->rshv", latent, value_proj, preferred_element_type=jnp.float32
    ).astype(jnp.bfloat16)
    return values.reshape(requests, steps, head_part * value_width)


def shards(block_pool, block_table, lengths, destination, query_latent, new_latent, value_proj):
    requests = destination.shape[1]
    slots = block_table.shape[3] // requests
    dest_row = destination[0]
    request_ids = jnp.arange(requests, dtype=jnp.int32)
    matches = (dest_row[:, None] == request_ids[None, :]).astype(jnp.int32)
    send_order = jnp.sum(matches * request_ids[:, None], axis=0)
    block_rows = block_table[0, 0, 0].reshape(requests, slots)
    own_pool = block_pool[0, 0, 0]
    picked = own_pool[block_rows[send_order]]
    got_blocks, got_lengths = (
        lax.all_to_all(picked, "pre", split_axis=0, concat_axis=0, tiled=True),
        lax.all_to_all(lengths[0][send_order], "pre", split_axis=0, concat_axis=0, tiled=True),
    )
    result = attend(got_blocks, got_lengths, query_latent[0], new_latent[0], value_proj)
    return result[None]


def solution(mesh):
    return jax.shard_map(
        shards,
        mesh=mesh,
        in_specs=(
            P("pre", "seq", "dec", None, None, None),
            P("pre", "seq", "dec", None),
            P("pre", None),
            P("pre", None),
            P("pre", None, None, ("seq", "dec"), None),
            P("pre", None, None, None),
            P(("seq", "dec"), None, None),
        ),
        out_specs=P("pre", None, None, ("seq", "dec")),
        check_vma=False,
    )
```

profile of v0, /device:TPU:2, one launch (start us, length us, event | category | flops | bytes accessed | tf_op | source)
XLA Modules:
  0.0 632.9 jit_solution(18402123183261251889)
XLA Ops:
  9.4 7.5 %all-to-all-start = ((s32[16,1,1]{2,1,0:T(1,128)}), s32[16,1,1]{2,1,0:T(1,128)S(1)}, u32[]{:S(2)}, u32[]{:S(2)}) async-start(s32[16,1,1]{2,1,0:T(1,128)} %copy.62), calls=%async_computation | async-start | bytes 16384 | tf_op jit(solution)/shard_map/all_to_all | solution.py:93
  19.7 13.5 %gather_fusion.2 = bf16[128,128,576]{1,2,0:T(8,128)(2,1)} fusion(bf16[80,128,576]{1,2,0:T(8,128)(2,1)} %bitcast.94, s32[1024]{0:T(1024)S(1)} %pad_clamp_fusion), kind=kCustom, calls=%fused_computation.2 | custom fusion | bytes 37749248 | tf_op jit(solution)/shard_map/gather | solution.py:90
  33.3 7.4 %all-to-all-start.1 = ((bf16[16,8,128,576]{2,3,1,0:T(8,128)(2,1)}), bf16[16,8,128,576]{2,3,1,0:T(8,128)(2,1)}, u32[]{:S(2)}, u32[]{:S(2)}) async-start(bf16[16,8,128,576]{2,3,1,0:T(8,128)(2,1)} %bitcast.92), calls=%async_computation.1 | async-start | bytes 37748736 | tf_op jit(solution)/shard_map/all_to_all | solution.py:92
  41.9 48.1 %all-gather.3.cloned.1.call-done = bf16[1,16,2,128,576]{4,3,2,1,0:T(8,128)(2,1)} async-done(((bf16[1,16,2,8,576]{4,3,2,1,0:T(8,128)(2,1)}), bf16[1,16,2,128,576]{4,3,2,1,0:T(8,128)(2,1)}) %all-gather.3.cloned.1.call-update) | async-done | bytes 4718608 | tf_op jit(solution)/shard_map/all_gather | solution.py:16
  90.0 4.0 fusion.39
  94.0 221.1 %all-to-all-done.1 = bf16[16,8,128,576]{2,3,1,0:T(8,128)(2,1)} async-done(((bf16[16,8,128,576]{2,3,1,0:T(8,128)(2,1)}), bf16[16,8,128,576]{2,3,1,0:T(8,128)(2,1)}, u32[]{:S(2)}, u32[]{:S(2)}) %all-to-all-start.1) | async-done | bytes 18874400 | tf_op jit(solution)/shard_map/all_to_all | solution.py:92
  315.1 26.7 %copy.80 = bf16[16,8,128,576]{3,2,1,0:T(8,128)(2,1)} copy(bf16[16,8,128,576]{2,3,1,0:T(8,128)(2,1)} %all-to-all-done.1) | data formatting | bytes 37748736
  341.7 71.7 %while.26 = (s32[]{:T(128)}, f32[16,256,1024]{2,1,0:T(8,128)}, f32[16,256]{1,0:T(8,128)S(1)}, s32[16]{0:T(128)S(1)}, bf16[16,256,576]{2,1,0:T(8,128)(2,1)}, /*in...) while((s32[]{:T(128)}, f32[16,256,1024]{2,1,0:T(8,128)}, ...), condition=%wide.region_3.4_spmd.clone, body=%wide.region_1.3_spmd.clone.sunk | while | flops 302793472 | bytes 4790913 | solution.py:32
  343.0 3.1 bitcast_dynamic-update-slice_fusion.2
  347.4 3.0 bitcast_dynamic-update-slice_fusion.2
  351.9 3.0 bitcast_dynamic-update-slice_fusion.2
  356.4 3.1 bitcast_dynamic-update-slice_fusion.2
  360.9 3.1 bitcast_dynamic-update-slice_fusion.2
  365.4 3.0 bitcast_dynamic-update-slice_fusion.2
  369.8 3.0 bitcast_dynamic-update-slice_fusion.2
  374.3 3.1 bitcast_dynamic-update-slice_fusion.2
  378.8 3.1 bitcast_dynamic-update-slice_fusion.2
  383.3 3.0 bitcast_dynamic-update-slice_fusion.2
  387.8 3.0 bitcast_dynamic-update-slice_fusion.2
  392.3 3.1 bitcast_dynamic-update-slice_fusion.2
  396.7 3.0 bitcast_dynamic-update-slice_fusion.2
  401.2 3.1 bitcast_dynamic-update-slice_fusion.2
  405.7 3.0 bitcast_dynamic-update-slice_fusion.2
  410.2 3.0 bitcast_dynamic-update-slice_fusion.2
  413.4 49.2 %pmax.7 = f32[16,256]{1,0:T(8,128)S(1)} all-reduce(f32[16,256]{1,0:T(8,128)S(1)} %max.5), channel_id=1, replica_groups=mesh['pre'=16,'seq'=8,'dec'=2] {'seq','dec'}, use_global_device_ids=true, to_apply=%region_5.6 | all-reduce | flops 4096 | bytes 32768 | tf_op jit(solution)/shard_map/pmax | solution.py:41
  462.6 89.4 %while.25 = (s32[]{:T(128)}, f32[16,256]{1,0:T(8,128)S(1)}, f32[16,256,512]{2,1,0:T(8,128)}, f32[16,256,1024]{2,1,0:T(8,128)}, f32[16,256]{1,0:T(8,128)S(1)}, /*...) while((s32[]{:T(128)}, f32[16,256]{1,0:T(8,128)S(1)}, f32[16,256,512]{2,1,0:T(8,128)}, ...), condition=%wide.region_8.9_spmd, body=%wide.region_6.8_spmd.sunk | while | flops 269483776 | bytes 6037605 | solution.py:52
  464.1 2.6 fusion.49
  466.7 1.5 fusion.48
  469.7 2.6 fusion.49
  472.3 1.5 fusion.48
  475.3 2.5 fusion.49
  477.8 1.5 fusion.48
  479.4 1.4 dynamic-slice_bitcast_fusion.2
  480.9 2.5 fusion.49
  483.4 1.5 fusion.48
  486.5 2.6 fusion.49
  489.0 1.5 fusion.48
  492.1 2.5 fusion.49
  494.6 1.5 fusion.48
  496.2 1.4 dynamic-slice_bitcast_fusion.2
  497.6 2.5 fusion.49
  500.2 1.5 fusion.48
  501.8 1.4 dynamic-slice_bitcast_fusion.2
  503.2 2.5 fusion.49
  505.8 1.5 fusion.48
  508.8 2.5 fusion.49
  511.4 1.5 fusion.48
  514.4 2.5 fusion.49
  516.9 1.5 fusion.48
  520.0 2.5 fusion.49
  522.5 1.5 fusion.48
  525.5 2.5 fusion.49
  528.1 1.5 fusion.48
  531.1 2.6 fusion.49
  533.7 1.5 fusion.48
  536.7 2.6 fusion.49
  539.3 1.5 fusion.48
  542.3 2.6 fusion.49
  544.9 1.5 fusion.48
  547.9 2.6 fusion.49
  550.5 1.5 fusion.48
  553.5 47.1 %all-reduce = f32[16,2,128]{0,1,2:T(2,128)S(1)} all-reduce(f32[16,2,128]{0,1,2:T(2,128)S(1)} %copy.71), channel_id=4, replica_groups=mesh['pre'=16,'seq'=8,'dec'=2] {'seq','dec'}, use_global_device_ids=true, to_apply=%region_10.11.clone | all-reduce | flops 4096 | bytes 32768
  600.9 22.4 %reduce-scatter.2.cloned.1.call-done = f32[16,2,8,512]{3,2,1,0:T(8,128)} async-done(((f32[16,2,128,512]{3,2,1,0:T(8,128)}), f32[16,2,8,512]{3,2,1,0:T(8,128)}) %reduce-scatter.2.cloned.1.call-update) | async-done | bytes 524304 | tf_op jit(solution)/shard_map/reduce_scatter | solution.py:56
  623.4 1.6 fusion.29
  (154 shorter events, 51.0 us)
Async XLA Ops:
  6.5 618.4 %copy-start = (bf16[8,512,128]{2,1,0:T(8,128)(2,1)S(1)}, bf16[8,512,128]{2,1,0:T(8,128)(2,1)}, u32[]{:S(2)}) copy-start(bf16[8,512,128]{2,1,0:T(8,128)(2,1)} %param.17) | copy-start | bytes 3145732
  9.4 23.9 %all-to-all-start = ((s32[16,1,1]{2,1,0:T(1,128)}), s32[16,1,1]{2,1,0:T(1,128)S(1)}, u32[]{:S(2)}, u32[]{:S(2)}) async-start(s32[16,1,1]{2,1,0:T(1,128)} %copy.62), calls=%async_computation | async-start | bytes 16384 | tf_op jit(solution)/shard_map/all_to_all | solution.py:93
  33.3 56.7 %copy-start.1 = (bf16[1,16,2,576]{3,2,1,0:T(2,128)(2,1)S(1)}, bf16[1,16,2,576]{3,2,1,0:T(2,128)(2,1)}, u32[]{:S(2)}) copy-start(bf16[1,16,2,576]{3,2,1,0:T(2,128)(2,1)} %param.16) | copy-start | bytes 110596
  33.3 281.8 %all-to-all-start.1 = ((bf16[16,8,128,576]{2,3,1,0:T(8,128)(2,1)}), bf16[16,8,128,576]{2,3,1,0:T(8,128)(2,1)}, u32[]{:S(2)}, u32[]{:S(2)}) async-start(bf16[16,8,128,576]{2,3,1,0:T(8,128)(2,1)} %bitcast.92), calls=%async_computation.1 | async-start | bytes 37748736 | tf_op jit(solution)/shard_map/all_to_all | solution.py:92
  40.6 49.4 %all-gather.3.cloned.1.call-start = ((), (), s32[]{:S(2)}) async-start(), calls=%async_computation.4 | async-start | bytes 5570560 | tf_op jit(solution)/shard_map/all_gather | solution.py:16
  41.4 582.0 %reduce-scatter.2.cloned.1.call-start = ((), (), s32[]{:S(2)}) async-start(), calls=%async_computation.3 | async-start | bytes 8912896 | tf_op jit(solution)/shard_map/reduce_scatter | solution.py:56
  462.6 89.5 %copy-start.2 = (u32[256]{0:T(256)S(1)}, u32[256]{0:T(256)}, u32[]{:S(2)}) copy-start(u32[256]{0:T(256)} %constant.114) | copy-start | bytes 3076
Sparse Core Ops, SparseCore 0:
  43.3 46.6 all-gather.2
  552.2 71.0 reduce-scatter.1
where the time goes:
time: 637 us; the launch traced here: 633 us
  waiting for transfers between devices  292 us (46%)
  blocking collectives  96.3 us (15%)
  matrix products  95.5 us (15%)
  local copies, waits for them, and re-layouts  79.6 us (12%)
  other arithmetic  39.1 us (6%)
  starting transfers between devices  14.9 us (2%)
  between operations  14.2 us (2%)
    all_to_all x1, waiting for transfers between devices, shards(): lax.all_to_all(picked, 'pre', split_axis=0, concat_axis=0, tiled=True)  221 us
    pmax x1, blocking collectives, attend(): global_top = lax.pmax(local_top, ('seq', 'dec'))  49.2 us
    dot_general x16, matrix products, score_one(): jnp.dot(rows, keys.T, preferred_element_type=jnp.float32) * score_scale  48.7 us
    all_gather x1, waiting for transfers between devices, attend(): queries = lax.all_gather(query_part, ('seq', 'dec'), axis=2, tiled=True)  48.1 us
    unnamed x1, blocking collectives  47.1 us
    dot_general x16, matrix products, weigh_one(): jnp.dot(weights.astype(jnp.bfloat16), keys[:, :latent_width], preferred_e...  40.8 us
    unnamed x10, local copies, waits for them, and re-layouts  27.9 us
    reduce_sum x16, other arithmetic, weigh_one(): total = jnp.sum(weights, axis=-1)  24.3 us
  transfers between devices with their start and end apart: 4, of which 3 were waited for; matrix products, arithmetic and copies ran while one was open for 3% of the time, Pallas kernels for 0%

commit v1 on v0

v1 whole, which is shorter than its diff:
```python
import functools

import jax
import jax.numpy as jnp
from jax import lax
from jax.experimental import pallas as pl
from jax.experimental.pallas import tpu as pltpu
from jax.sharding import PartitionSpec as P

score_scale = 192.0 ** (-0.5) * 1.4426950408889634
EMPTY = -(2.0**127)
F32 = jnp.float32
BF16 = jnp.bfloat16
MIB = 1024 * 1024
GROUP = 4


def pack_stat(stat):
    high = stat.astype(BF16)
    rest = stat - high.astype(F32)
    mid = rest.astype(BF16)
    low = (rest - mid.astype(F32)).astype(BF16)
    return high, mid, low


def read_stat(ref):
    requests = ref.shape[0] - 1
    parts = [ref[requests, :, i * 128 : (i + 1) * 128].astype(F32) for i in range(3)]
    return parts[0] + parts[1] + parts[2]


def write_stat(ref, stat):
    requests = ref.shape[0] - 1
    for i, part in enumerate(pack_stat(stat)):
        ref[requests, :, i * 128 : (i + 1) * 128] = part
    used = 3 * 128
    if ref.shape[2] > used:
        ref[requests, :, used:] = jnp.zeros((ref.shape[1], ref.shape[2] - used), BF16)


def plan_kernel(split_count, block, dest_ref, len_ref, table_ref, split_ref, out_ref, next_ref):
    requests = dest_ref.shape[1]
    slots = table_ref.shape[3] // requests
    split = split_ref[0]
    counts = []
    for i in range(requests):
        total = lax.div(len_ref[0, i] + (block - 1), block)
        counts.append(lax.div(total - split + (split_count - 1), split_count))
    pairs = [lax.div(count + 1, 2) for count in counts]
    for c in range(slots // 2 + 1):
        longer = [(p > c).astype(jnp.int32) for p in pairs]
        next_ref[c] = functools.reduce(jnp.add, longer)
    for i in range(requests):
        at = next_ref[pairs[i]]
        next_ref[pairs[i]] = at + 1
        start = (counts[i] - 1) * split_count + split
        used = (counts[i] - 1) * block + jnp.minimum(block, len_ref[0, i] - start * block)
        out_ref[at, 0] = dest_ref[0, i]
        out_ref[at, 1] = pairs[i]
        out_ref[at, 2] = jnp.where(counts[i] > 0, used, 0)
        for j in range(slots):
            out_ref[at, 3 + j] = table_ref[0, 0, 0, i * slots + j]


def attention_kernel(n_pieces, plan_ref, *refs):
    q_refs = refs[:n_pieces]
    pool_ref = refs[n_pieces]
    o_refs = refs[n_pieces + 1 : 2 * n_pieces + 1]
    kbuf, stat_ref, sems = refs[2 * n_pieces + 1 :]
    requests, rows, _ = q_refs[0].shape
    slots = plan_ref.shape[1] - 3
    block = pool_ref.shape[2]
    latent = o_refs[0].shape[2]
    groups = requests // GROUP

    def each(g, act):
        pairs = plan_ref[g * GROUP, 1]
        half = lax.rem(g, 2)
        for m in range(GROUP):
            for j in range(slots):

                @pl.when(j // 2 < pairs)
                def _():
                    act(
                        pltpu.make_async_copy(
                            pool_ref.at[plan_ref[g * GROUP + m, 3 + j]],
                            kbuf.at[half, m, j],
                            sems.at[half, m, j],
                        )
                    )

    each(0, lambda c: c.start())
    stat_ref[...] = jnp.zeros_like(stat_ref)
    lane = lax.broadcasted_iota(jnp.int32, stat_ref.shape, 1)
    pair = 2 * block
    column = lax.broadcasted_iota(jnp.int32, (1, pair), 1)

    def compute(g, pairs):
        half = lax.rem(g, 2)
        whos = [plan_ref[g * GROUP + m, 0] for m in range(GROUP)]
        keys, scores, tops = [], [], []
        for m, who in enumerate(whos):
            used = plan_ref[g * GROUP + m, 2]
            q = jnp.concatenate([ref[who] for ref in q_refs], axis=0)
            keys.append(
                [
                    jnp.concatenate([kbuf[half, m, 2 * c], kbuf[half, m, 2 * c + 1]], axis=1)
                    for c in range(pairs)
                ]
            )
            row = []
            for c in range(pairs):
                s = jnp.dot(q, keys[m][c], preferred_element_type=F32) * score_scale
                row.append(jnp.where(column < used - c * pair, s, -jnp.inf))
            scores.append(row)
        for row in scores:
            top = functools.reduce(jnp.maximum, row)
            tops.append(jnp.maximum(jnp.max(top, axis=1, keepdims=True), EMPTY))
        for m, who in enumerate(whos):
            total, out = None, None
            for c in range(pairs):
                e = jnp.exp2(scores[m][c] - tops[m])
                total = e if total is None else total + e
                part = lax.dot_general(
                    e.astype(BF16),
                    keys[m][c][:latent],
                    (((1,), (1,)), ((), ())),
                    preferred_element_type=F32,
                )
                out = part if out is None else out + part
            total = jnp.sum(total, axis=1, keepdims=True)
            some = total > 0
            out = (out * jnp.where(some, 1.0 / total, 0.0)).astype(BF16)
            for n, ref in enumerate(o_refs):
                ref[who] = out[n * rows : (n + 1) * rows]
            stat = jnp.where(some, tops[m] + jnp.log2(total), EMPTY)
            stat_ref[...] = jnp.where(lane == who, stat, stat_ref[...])

    def step(g, carry):
        @pl.when(g + 1 < groups)
        def _():
            each(g + 1, lambda c: c.start())

        each(g, lambda c: c.wait())
        pairs_here = plan_ref[g * GROUP, 1]
        for pairs in range(1, slots // 2 + 1):

            @pl.when(pairs_here == pairs)
            def _():
                compute(g, pairs)

        @pl.when(pairs_here == 0)
        def _():
            for m in range(GROUP):
                who = plan_ref[g * GROUP + m, 0]
                for ref in o_refs:
                    ref[who] = jnp.zeros((rows, latent), BF16)
                stat_ref[...] = jnp.where(lane == who, EMPTY, stat_ref[...])

        return carry

    lax.fori_loop(0, groups, step, 0)
    for n, ref in enumerate(o_refs):
        write_stat(ref, stat_ref[n * rows : (n + 1) * rows, :])


def weights_of(refs):
    stats = [read_stat(ref) for ref in refs]
    top = functools.reduce(jnp.maximum, stats)
    parts = [jnp.exp2(stat - top) for stat in stats]
    total = functools.reduce(jnp.add, parts)
    share = 1.0 / total
    return [part * share for part in parts], top + jnp.log2(total)


def combined(refs, weights, who):
    out = None
    for ref, weight in zip(refs, weights):
        part = ref[who].astype(F32) * weight[:, who : who + 1]
        out = part if out is None else out + part
    return out


def combine_kernel(*refs):
    *pieces, out_ref = refs
    weights, stat = weights_of(pieces)
    write_stat(out_ref, stat)
    for who in range(out_ref.shape[0] - 1):
        out_ref[who] = combined(pieces, weights, who).astype(BF16)


def project(latents, stats, proj_ref, out_ref):
    requests, steps, _ = out_ref.shape
    heads, _, width = proj_ref.shape
    latent = jnp.concatenate(latents, axis=0)
    stat = jnp.concatenate(stats, axis=0)
    shape = (latent.shape[0], width)
    head_of = lax.broadcasted_iota(jnp.int32, shape, 0) % heads

    def by_row(value):
        return value.reshape(requests * steps, heads, width).sum(axis=1)

    def put(value, at):
        for who in range(requests):
            out_ref[who, :, at : at + width] = value[who * steps : (who + 1) * steps]

    for h in range(heads):
        value = jnp.dot(latent, proj_ref[h], preferred_element_type=F32)
        put(by_row(jnp.where(head_of == h, value, 0.0)), h * width)
    lane = lax.broadcasted_iota(jnp.int32, shape, 1)
    put(by_row(jnp.where(head_of == lane, stat, 0.0)), heads * width)


def new_keys_kernel(q_ref, key_ref, proj_ref, out_ref):
    requests, rows, _ = q_ref.shape
    latent = proj_ref.shape[1]
    steps = key_ref.shape[1]
    heads = rows // steps
    step_of = lax.broadcasted_iota(jnp.int32, (rows, 1), 0) // heads
    latents, stats = [], []
    for who in range(requests):
        q = q_ref[who].astype(F32)
        keys = key_ref[who].astype(F32)
        scores = []
        for j in range(steps):
            s = jnp.sum(q * keys[j : j + 1, :], axis=1, keepdims=True) * score_scale
            scores.append(jnp.where(step_of >= j, s, -jnp.inf))
        top = functools.reduce(jnp.maximum, scores)
        parts = [jnp.exp2(s - top) for s in scores]
        total = functools.reduce(jnp.add, parts)
        out = None
        for j in range(steps):
            part = parts[j].astype(BF16).astype(F32) * keys[j : j + 1, :latent]
            out = part if out is None else out + part
        latents.append((out / total).astype(BF16))
        stats.append(top + jnp.log2(total))
    project(latents, stats, proj_ref, out_ref)


def finish_kernel(*refs):
    *pieces, proj_ref, out_ref = refs
    requests = out_ref.shape[0]
    weights, stat = weights_of(pieces)
    latents = [combined(pieces, weights, who).astype(BF16) for who in range(requests)]
    stats = [stat[:, who : who + 1] for who in range(requests)]
    project(latents, stats, proj_ref, out_ref)


def merge_kernel(cache_ref, new_ref, out_ref):
    width = out_ref.shape[2]
    heads = width // 128
    cache_stat = cache_ref[:, :, width:]
    new_stat = new_ref[:, :, width:]
    top = jnp.maximum(cache_stat, new_stat)
    cache_part = jnp.exp2(cache_stat - top)
    new_part = jnp.exp2(new_stat - top)
    share = 1.0 / (cache_part + new_part)
    cache_part = cache_part * share
    new_part = new_part * share
    for h in range(heads):
        at = slice(h * 128, (h + 1) * 128)
        value = cache_ref[:, :, at] * cache_part[:, :, h : h + 1]
        value = value + new_ref[:, :, at] * new_part[:, :, h : h + 1]
        out_ref[:, :, at] = value.astype(BF16)


def call(kernel, out_shape, *args, mib=12, **extra):
    return pl.pallas_call(
        kernel,
        out_shape=out_shape,
        compiler_params=pltpu.CompilerParams(vmem_limit_bytes=mib * MIB),
        **extra,
    )(*args)


def vmem(count):
    return [pl.BlockSpec(memory_space=pltpu.VMEM)] * count


def smem(count):
    return [pl.BlockSpec(memory_space=pltpu.SMEM)] * count


def combine(pieces):
    return call(
        combine_kernel,
        jax.ShapeDtypeStruct(pieces[0].shape, BF16),
        *pieces,
        in_specs=vmem(len(pieces)),
        out_specs=vmem(1)[0],
    )


def shards(block_pool, block_table, lengths, destination, query_latent, new_latent, value_proj):
    ring = lax.axis_size("seq")
    split_count = ring * lax.axis_size("dec")
    split_index = lax.axis_index(("seq", "dec"))
    requests = destination.shape[1]
    _, _, steps, heads, width = query_latent.shape
    rows = steps * heads
    latent, value_width = value_proj.shape[1:]
    block = block_pool.shape[4]
    slots = block_table.shape[3] // requests
    far, near = ring // 2, (ring - 1) // 2
    pool = jnp.swapaxes(block_pool[0, 0, 0], 1, 2)

    up = [(i, (i + 1) % ring) for i in range(ring)]
    down = [(i, (i - 1) % ring) for i in range(ring)]

    def swap(x):
        return lax.ppermute(x, "dec", [(0, 1), (1, 0)])

    decode_q = query_latent[0].reshape(requests, rows, width)
    own_q = lax.all_to_all(decode_q, "pre", split_axis=0, concat_axis=0, tiled=True)
    plan = call(
        functools.partial(plan_kernel, split_count, block),
        jax.ShapeDtypeStruct((requests, 3 + slots), jnp.int32),
        destination,
        lengths,
        block_table,
        split_index.reshape(1),
        in_specs=smem(4),
        out_specs=smem(1)[0],
        scratch_shapes=[pltpu.SMEM((slots // 2 + 1,), jnp.int32)],
    )
    values_shape = jax.ShapeDtypeStruct(
        (requests, steps, heads * value_width + 128), F32
    )
    new_values = call(
        new_keys_kernel,
        values_shape,
        decode_q,
        new_latent[0],
        value_proj,
        in_specs=vmem(3),
        out_specs=vmem(1)[0],
    )

    queries = {0: own_q}
    for s in range(1, far + 1):
        queries[-s] = lax.ppermute(queries[1 - s], "seq", up)
        if s <= near:
            queries[s] = lax.ppermute(queries[s - 1], "seq", down)
        if s == 1:
            queries[-s], plan = lax.optimization_barrier((queries[-s], plan))
        if s == 2:
            queries[-s], new_values = lax.optimization_barrier((queries[-s], new_values))
    order = sorted(queries)
    q_list = [queries[r] for r in order] + [swap(queries[r]) for r in order]
    n_pieces = len(q_list)
    piece = jax.ShapeDtypeStruct((requests + 1, rows, latent), BF16)
    outs = call(
        functools.partial(attention_kernel, n_pieces),
        [piece] * n_pieces,
        plan,
        *q_list,
        pool,
        in_specs=smem(1) + vmem(n_pieces) + [pl.BlockSpec(memory_space=pltpu.HBM)],
        out_specs=vmem(n_pieces),
        scratch_shapes=[
            pltpu.VMEM((2, GROUP, slots, width, block), BF16),
            pltpu.VMEM((n_pieces * rows, 128), F32),
            pltpu.SemaphoreType.DMA((2, GROUP, slots)),
        ],
        mib=50,
    )
    mine = dict(zip(order, outs[: len(order)]))
    others = {r: swap(x) for r, x in zip(order, outs[len(order) :])}

    from_up, from_down = [], []
    for s in range(far, 0, -1):
        sent = combine([mine[-s], others[-s]] + from_up)
        from_up = [lax.ppermute(sent, "seq", down)]
        if s <= near:
            sent = combine([mine[s], others[s]] + from_down)
            from_down = [lax.ppermute(sent, "seq", up)]
    pieces = [mine[0], others[0]] + from_up + from_down
    values = call(
        finish_kernel,
        values_shape,
        *pieces,
        value_proj,
        in_specs=vmem(len(pieces) + 1),
        out_specs=vmem(1)[0],
    )
    got = lax.all_to_all(values, "pre", split_axis=0, concat_axis=0, tiled=True)
    result = call(
        merge_kernel,
        jax.ShapeDtypeStruct((requests, steps, heads * value_width), BF16),
        got,
        new_values,
        in_specs=vmem(2),
        out_specs=vmem(1)[0],
    )
    return result[None]


def solution(mesh):
    return jax.shard_map(
        shards,
        mesh=mesh,
        in_specs=(
            P("pre", "seq", "dec", None, None, None),
            P("pre", "seq", "dec", None),
            P("pre", None),
            P("pre", None),
            P("pre", None, None, ("seq", "dec"), None),
            P("pre", None, None, None),
            P(("seq", "dec"), None, None),
        ),
        out_specs=P("pre", None, None, ("seq", "dec")),
        check_vma=False,
    )
```

time: 637 us -> 122 us (0.19)
  waiting for transfers between devices: 292 us -> 37.8 us
  matrix products: 95.5 us -> 0 us
  local copies, waits for them, and re-layouts: 79.6 us -> 5.71 us
  blocking collectives: 96.3 us -> 25.9 us
  other arithmetic: 39.1 us -> 0 us
  Pallas kernels: 0 us -> 23.6 us
  between operations: 14.2 us -> 0.36 us
  starting transfers between devices: 14.9 us -> 27.4 us
    all_to_all x2 -> x0, waiting for transfers between devices: 221 us -> none  [the longest x1 221 us: shards(): lax.all_to_all(picked, 'pre', split_axis=0, concat_axis=0, tiled=True)]
    dot_general x35 -> x0, matrix products: 95.5 us -> none  [the longest x16 48.7 us: score_one(): jnp.dot(rows, keys.T, preferred_element_type=jnp.float32) * score_scale]
    pmax x1 -> x0, blocking collectives: 49.2 us -> none  [attend(): global_top = lax.pmax(local_top, ('seq', 'dec'))]
    all_gather x1 -> x0, waiting for transfers between devices: 48.1 us -> none  [attend(): queries = lax.all_gather(query_part, ('seq', 'dec'), axis=2, tiled=True)]
    unnamed x1 -> x0, blocking collectives: 47.1 us -> none
    ppermute x0 -> x30, waiting for transfers between devices: none -> 37.8 us  [the longest x4 16.5 us: shards(): from_up = [lax.ppermute(sent, 'seq', down)]]
    ppermute x0 -> x30, starting transfers between devices: none -> 27.4 us  [the longest x3 10.9 us: shards(): queries[s] = lax.ppermute(queries[s - 1], 'seq', down)]
    all_to_all x0 -> x2, blocking collectives: none -> 25.9 us  [the longest x1 15.5 us: shards(): lax.all_to_all(decode_q, 'pre', split_axis=0, concat_axis=0, tiled=True)]
  transfers between devices with their start and end apart: 4 -> 30, of which waited for: 3 -> 14; matrix products, arithmetic and copies ran while one was open for 3% -> 0% of each run, Pallas kernels for 0% -> 3%
where the time goes in v1:
time: 122 us; the launch traced here: 121 us
  waiting for transfers between devices  37.8 us (31%)
  starting transfers between devices  27.4 us (22%)
  blocking collectives  25.9 us (21%)
  Pallas kernels  23.6 us (19%)
  local copies, waits for them, and re-layouts  5.71 us (5%)
    pallas_call x12, Pallas kernels, call(): pl.pallas_call(kernel, out_shape=out_shape, compiler_params=pltpu.Compile...  23.6 us
    ppermute x4, waiting for transfers between devices, shards(): from_up = [lax.ppermute(sent, 'seq', down)]  16.5 us
    all_to_all x1, blocking collectives, shards(): lax.all_to_all(decode_q, 'pre', split_axis=0, concat_axis=0, tiled=True)  15.5 us
    ppermute x4, waiting for transfers between devices, shards(): queries[-s] = lax.ppermute(queries[1 - s], 'seq', up)  11 us
    ppermute x3, starting transfers between devices, shards(): queries[s] = lax.ppermute(queries[s - 1], 'seq', down)  10.9 us
    all_to_all x1, blocking collectives, shards(): got = lax.all_to_all(values, 'pre', split_axis=0, concat_axis=0, tiled=True)  10.4 us
    ppermute x4, starting transfers between devices, shards(): from_up = [lax.ppermute(sent, 'seq', down)]  8.52 us
    unnamed x46, local copies, waits for them, and re-layouts  5.71 us
  transfers between devices with their start and end apart: 30, of which 14 were waited for; matrix products, arithmetic and copies ran while one was open for 0% of the time, Pallas kernels for 3%

profile of v1, /device:TPU:2, one launch (start us, length us, event | category | flops | bytes accessed | tf_op | source)
XLA Modules:
  0.0 120.6 jit_solution(3573257069282309316)
XLA Ops:
  0.0 15.5 %all_to_all.10.refs_4_ = bf16[16,16,576]{2,1,0:T(8,128)(2,1)S(1)} all-to-all(bf16[16,16,576]{2,1,0:T(8,128)(2,1)} %bitcast.7), channel_id=1, replica_groups=mesh['pre'=16,'seq'=8,'dec'=2] {'pre'}, dimensions={0} | all-to-all | bytes 589824 | tf_op jit(solution)/shard_map/all_to_all | solution.py:314
  15.5 1.9 %collective-permute-start = (bf16[16,16,576]{2,1,0:T(8,128)(2,1)S(1)}, bf16[16,16,576]{2,1,0:T(8,128)(2,1)S(1)}, u32[]{:S(2)}, u32[]{:S(2)}) collective-permute-start(bf16[16,16,576]{2,1,0:T(8,128)(2,1)S(1)} %all_to_all.10.refs_4_), channel_id=1, source_target_pairs={{0,2},{2,4},{4,6},{6,8},{8,10},{10,12},{12,14},{14,0},{1,3},{3,5},... | collective-permute-start | bytes 884744 | tf_op jit(solution)/shard_map/ppermute | solution.py:341
  17.4 0.7 copy-done.4
  18.1 0.7 copy-done.5
  18.7 0.7 copy-done.6
  19.4 1.7 %shard_map.73.plan_ref = s32[16,11]{1,0:T(8,128)S(1)} custom-call(s32[1,16]{1,0:T(1,128)S(1)} %copy-done.4, s32[1,16]{1,0:T(1,128)S(1)} %copy-done.5, s32[1,1,1,128]{3,2,1,0:T(1,128)S(1)} %copy-done.6, s32[1]{0:T(128)} %bitcast.1.split_ref), custom_call_target="tpu_custom_call" | custom-call | tf_op jit(solution)/shard_map/pallas_call | solution.py:268
  21.1 4.0 %collective-permute-start.4 = (bf16[16,16,576]{2,1,0:T(8,128)(2,1)S(1)}, bf16[16,16,576]{2,1,0:T(8,128)(2,1)S(1)}, u32[]{:S(2)}, u32[]{:S(2)}) collective-permute-start(bf16[16,16,576]{2,1,0:T(8,128)(2,1)S(1)} %all_to_all.10.refs_4_), channel_id=1, source_target_pairs={{0,14},{2,0},{4,2},{6,4},{8,6},{10,8},{12,10},{14,12},{1,15},{3,1}... | collective-permute-start | bytes 884744 | tf_op jit(solution)/shard_map/ppermute | solution.py:343
  25.1 2.8 %collective-permute-done.refs_3_ = bf16[16,16,576]{2,1,0:T(8,128)(2,1)S(1)} collective-permute-done((bf16[16,16,576]{2,1,0:T(8,128)(2,1)S(1)}, bf16[16,16,576]{2,1,0:T(8,128)(2,1)S(1)}, u32[]{:S(2)}, u32[]{:S(2)}) %collective-permute-start) | collective-permute-done | bytes 294944 | tf_op jit(solution)/shard_map/ppermute | solution.py:341
  27.9 0.0 collective-permute-start.1
  27.9 1.3 %copy-done = bf16[8,512,128]{2,1,0:T(8,128)(2,1)S(1)} copy-done((bf16[8,512,128]{2,1,0:T(8,128)(2,1)S(1)}, bf16[8,512,128]{2,1,0:T(8,128)(2,1)}, u32[]{:S(2)}) %copy-start) | copy-done | bytes 1048600
  29.2 1.0 copy-done.2
  30.2 0.8 copy-done.3
  31.0 0.9 shard_map.74.new_ref
  31.9 3.2 %collective-permute-start.5 = (bf16[16,16,576]{2,1,0:T(8,128)(2,1)S(1)}, bf16[16,16,576]{2,1,0:T(8,128)(2,1)S(1)}, u32[]{:S(2)}, u32[]{:S(2)}) collective-permute-start(bf16[16,16,576]{2,1,0:T(8,128)(2,1)S(1)} %collective-permute-done.4.refs_5_), channel_id=1, source_target_pairs={{0,14},{2,0},{4,2},{6,4},{8,6},{10,8},{12,10},{14,12},{1,15},{3,1}... | collective-permute-start | bytes 884744 | tf_op jit(solution)/shard_map/ppermute | solution.py:343
  35.1 1.6 %collective-permute-done.1.refs_2_ = bf16[16,16,576]{2,1,0:T(8,128)(2,1)S(1)} collective-permute-done((bf16[16,16,576]{2,1,0:T(8,128)(2,1)S(1)}, bf16[16,16,576]{2,1,0:T(8,128)(2,1)S(1)}, u32[]{:S(2)}, u32[]{:S(2)}) %collective-permute-start.1) | collective-permute-done | bytes 294944 | tf_op jit(solution)/shard_map/ppermute | solution.py:341
  36.7 0.0 collective-permute-start.2
  36.7 0.0 collective-permute-start.11
  36.7 0.5 collective-permute-start.12
  37.2 0.1 collective-permute-start.10
  37.3 2.7 %collective-permute-done.5.refs_6_ = bf16[16,16,576]{2,1,0:T(8,128)(2,1)S(1)} collective-permute-done((bf16[16,16,576]{2,1,0:T(8,128)(2,1)S(1)}, bf16[16,16,576]{2,1,0:T(8,128)(2,1)S(1)}, u32[]{:S(2)}, u32[]{:S(2)}) %collective-permute-start.5) | collective-permute-done | bytes 294944 | tf_op jit(solution)/shard_map/ppermute | solution.py:343
  40.0 3.7 %collective-permute-start.6 = (bf16[16,16,576]{2,1,0:T(8,128)(2,1)S(1)}, bf16[16,16,576]{2,1,0:T(8,128)(2,1)S(1)}, u32[]{:S(2)}, u32[]{:S(2)}) collective-permute-start(bf16[16,16,576]{2,1,0:T(8,128)(2,1)S(1)} %collective-permute-done.5.refs_6_), channel_id=1, source_target_pairs={{0,14},{2,0},{4,2},{6,4},{8,6},{10,8},{12,10},{14,12},{1,15},{3,1}... | collective-permute-start | bytes 884744 | tf_op jit(solution)/shard_map/ppermute | solution.py:343
  43.7 1.5 %collective-permute-done.2.refs_1_ = bf16[16,16,576]{2,1,0:T(8,128)(2,1)S(1)} collective-permute-done((bf16[16,16,576]{2,1,0:T(8,128)(2,1)S(1)}, bf16[16,16,576]{2,1,0:T(8,128)(2,1)S(1)}, u32[]{:S(2)}, u32[]{:S(2)}) %collective-permute-start.2) | collective-permute-done | bytes 294944 | tf_op jit(solution)/shard_map/ppermute | solution.py:341
  45.2 0.1 collective-permute-start.9
  45.3 0.0 collective-permute-done.12.refs_13_
  45.3 0.5 collective-permute-start.13
  45.8 0.0 collective-permute-done.10.refs_11_
  45.8 0.1 collective-permute-start.8
  45.9 2.4 %collective-permute-done.6.refs_7_ = bf16[16,16,576]{2,1,0:T(8,128)(2,1)S(1)} collective-permute-done((bf16[16,16,576]{2,1,0:T(8,128)(2,1)S(1)}, bf16[16,16,576]{2,1,0:T(8,128)(2,1)S(1)}, u32[]{:S(2)}, u32[]{:S(2)}) %collective-permute-start.6) | collective-permute-done | bytes 294944 | tf_op jit(solution)/shard_map/ppermute | solution.py:343
  48.3 5.2 %collective-permute-done.3.refs_0_ = bf16[16,16,576]{2,1,0:T(8,128)(2,1)S(1)} collective-permute-done((bf16[16,16,576]{2,1,0:T(8,128)(2,1)S(1)}, bf16[16,16,576]{2,1,0:T(8,128)(2,1)S(1)}, u32[]{:S(2)}, u32[]{:S(2)}) %collective-permute-start.3) | collective-permute-done | bytes 294944 | tf_op jit(solution)/shard_map/ppermute | solution.py:341
  53.5 0.0 collective-permute-start.7
  53.5 0.0 collective-permute-done.8.refs_9_
  53.6 1.5 %collective-permute-done.7.refs_8_ = bf16[16,16,576]{2,1,0:T(8,128)(2,1)S(1)} collective-permute-done((bf16[16,16,576]{2,1,0:T(8,128)(2,1)S(1)}, bf16[16,16,576]{2,1,0:T(8,128)(2,1)S(1)}, u32[]{:S(2)}, u32[]{:S(2)}) %collective-permute-start.7) | collective-permute-done | bytes 294944 | tf_op jit(solution)/shard_map/ppermute | solution.py:311
  55.2 0.6 copy-done.22
  55.8 17.4 %shard_map.75 = (bf16[17,16,512]{2,1,0:T(8,128)(2,1)S(1)}, bf16[17,16,512]{2,1,0:T(8,128)(2,1)S(1)}, bf16[17,16,512]{2,1,0:T(8,128)(2,1)S(1)}, bf16[17,16,512]{2...) custom-call(s32[16,11]{1,0:T(8,128)S(1)} %shard_map.73.plan_ref, ...), custom_call_target="tpu_custom_call" | custom-call | tf_op jit(solution)/shard_map/pallas_call | solution.py:268
  73.3 0.1 collective-permute-start.19
  73.4 0.5 collective-permute-start.26
  73.8 0.1 collective-permute-start.18
  74.0 0.9 collective-permute-done.19.refs_1_
  74.9 0.2 shard_map.76
  75.1 0.1 collective-permute-start.20
  75.2 0.2 collective-permute-start.17
  75.4 0.4 collective-permute-start.25
  75.8 0.2 shard_map.80
  76.0 2.2 %collective-permute-start.27 = (bf16[17,16,512]{2,1,0:T(8,128)(2,1)S(1)}, bf16[17,16,512]{2,1,0:T(8,128)(2,1)S(1)}, u32[]{:S(2)}, u32[]{:S(2)}) collective-permute-start(bf16[17,16,512]{2,1,0:T(8,128)(2,1)S(1)} %shard_map.80), channel_id=1, source_target_pairs={{0,2},{2,4},{4,6},{6,8},{8,10},{10,12},{12,14},{14,0},{1,3},{3,5},... | collective-permute-start | bytes 835592 | tf_op jit(solution)/shard_map/ppermute | solution.py:376
  78.2 5.7 %collective-permute-done.20.refs_2_ = bf16[17,16,512]{2,1,0:T(8,128)(2,1)S(1)} collective-permute-done((bf16[17,16,512]{2,1,0:T(8,128)(2,1)S(1)}, bf16[17,16,512]{2,1,0:T(8,128)(2,1)S(1)}, u32[]{:S(2)}, u32[]{:S(2)}) %collective-permute-start.20) | collective-permute-done | bytes 278560 | tf_op jit(solution)/shard_map/ppermute | solution.py:373
  83.9 0.2 shard_map.77
  84.1 1.6 %collective-permute-start.21 = (bf16[17,16,512]{2,1,0:T(8,128)(2,1)S(1)}, bf16[17,16,512]{2,1,0:T(8,128)(2,1)S(1)}, u32[]{:S(2)}, u32[]{:S(2)}) collective-permute-start(bf16[17,16,512]{2,1,0:T(8,128)(2,1)S(1)} %shard_map.77), channel_id=1, source_target_pairs={{0,14},{2,0},{4,2},{6,4},{8,6},{10,8},{12,10},{14,12},{1,15},{3,1}... | collective-permute-start | bytes 835592 | tf_op jit(solution)/shard_map/ppermute | solution.py:373
  85.7 0.5 collective-permute-start.24
  86.2 0.2 shard_map.81
  86.4 0.6 collective-permute-start.28
  87.1 5.0 %collective-permute-done.21.refs_2_ = bf16[17,16,512]{2,1,0:T(8,128)(2,1)S(1)} collective-permute-done((bf16[17,16,512]{2,1,0:T(8,128)(2,1)S(1)}, bf16[17,16,512]{2,1,0:T(8,128)(2,1)S(1)}, u32[]{:S(2)}, u32[]{:S(2)}) %collective-permute-start.21) | collective-permute-done | bytes 278560 | tf_op jit(solution)/shard_map/ppermute | solution.py:373
  92.1 0.2 shard_map.78
  92.3 3.1 %collective-permute-start.22 = (bf16[17,16,512]{2,1,0:T(8,128)(2,1)S(1)}, bf16[17,16,512]{2,1,0:T(8,128)(2,1)S(1)}, u32[]{:S(2)}, u32[]{:S(2)}) collective-permute-start(bf16[17,16,512]{2,1,0:T(8,128)(2,1)S(1)} %shard_map.78), channel_id=1, source_target_pairs={{0,14},{2,0},{4,2},{6,4},{8,6},{10,8},{12,10},{14,12},{1,15},{3,1}... | collective-permute-start | bytes 835592 | tf_op jit(solution)/shard_map/ppermute | solution.py:373
  95.4 0.9 collective-permute-done.28.refs_2_
  96.3 0.2 shard_map.82
  96.6 0.1 collective-permute-start.29
  96.7 3.6 %collective-permute-done.22.refs_2_ = bf16[17,16,512]{2,1,0:T(8,128)(2,1)S(1)} collective-permute-done((bf16[17,16,512]{2,1,0:T(8,128)(2,1)S(1)}, bf16[17,16,512]{2,1,0:T(8,128)(2,1)S(1)}, u32[]{:S(2)}, u32[]{:S(2)}) %collective-permute-start.22) | collective-permute-done | bytes 278560 | tf_op jit(solution)/shard_map/ppermute | solution.py:373
  100.2 0.2 shard_map.79
  100.5 3.8 %collective-permute-start.23 = (bf16[17,16,512]{2,1,0:T(8,128)(2,1)S(1)}, bf16[17,16,512]{2,1,0:T(8,128)(2,1)S(1)}, u32[]{:S(2)}, u32[]{:S(2)}) collective-permute-start(bf16[17,16,512]{2,1,0:T(8,128)(2,1)S(1)} %shard_map.79), channel_id=1, source_target_pairs={{0,14},{2,0},{4,2},{6,4},{8,6},{10,8},{12,10},{14,12},{1,15},{3,1}... | collective-permute-start | bytes 835592 | tf_op jit(solution)/shard_map/ppermute | solution.py:373
  104.2 1.8 %collective-permute-done.29.refs_3_ = bf16[17,16,512]{2,1,0:T(8,128)(2,1)S(1)} collective-permute-done((bf16[17,16,512]{2,1,0:T(8,128)(2,1)S(1)}, bf16[17,16,512]{2,1,0:T(8,128)(2,1)S(1)}, u32[]{:S(2)}, u32[]{:S(2)}) %collective-permute-start.29) | collective-permute-done | bytes 278560 | tf_op jit(solution)/shard_map/ppermute | solution.py:376
  106.0 2.3 %collective-permute-done.23.refs_2_ = bf16[17,16,512]{2,1,0:T(8,128)(2,1)S(1)} collective-permute-done((bf16[17,16,512]{2,1,0:T(8,128)(2,1)S(1)}, bf16[17,16,512]{2,1,0:T(8,128)(2,1)S(1)}, u32[]{:S(2)}, u32[]{:S(2)}) %collective-permute-start.23) | collective-permute-done | bytes 278560 | tf_op jit(solution)/shard_map/ppermute | solution.py:373
  108.3 0.9 shard_map.83
  109.2 10.4 %all_to_all.11.cache_ref = f32[16,2,1152]{2,1,0:T(2,128)S(1)} all-to-all(f32[16,2,1152]{2,1,0:T(2,128)S(1)} %shard_map.83), channel_id=1, replica_groups=mesh['pre'=16,'seq'=8,'dec'=2] {'pre'}, dimensions={0} | all-to-all | bytes 294912 | tf_op jit(solution)/shard_map/all_to_all | solution.py:386
  119.6 1.0 shard_map.84
  (56 shorter events, 0.1 us)
Async XLA Ops:
  15.5 39.6 %copy-start.7 = (bf16[16,16,576]{2,1,0:T(8,128)(2,1)}, bf16[16,16,576]{2,1,0:T(8,128)(2,1)S(1)}, u32[]{:S(2)}) copy-start(bf16[16,16,576]{2,1,0:T(8,128)(2,1)S(1)} %all_to_all.10.refs_4_) | copy-start | bytes 884740
  15.5 12.4 %collective-permute-start = (bf16[16,16,576]{2,1,0:T(8,128)(2,1)S(1)}, bf16[16,16,576]{2,1,0:T(8,128)(2,1)S(1)}, u32[]{:S(2)}, u32[]{:S(2)}) collective-permute-start(bf16[16,16,576]{2,1,0:T(8,128)(2,1)S(1)} %all_to_all.10.refs_4_), channel_id=1, source_target_pairs={{0,2},{2,4},{4,6},{6,8},{8,10},{10,12},{12,14},{14,0},{1,3},{3,5},... | collective-permute-start | bytes 884744 | tf_op jit(solution)/shard_map/ppermute | solution.py:341
  17.4 0.7 copy-start.4
  18.1 0.7 copy-start.5
  18.7 0.7 copy-start.6
  21.1 10.9 %collective-permute-start.4 = (bf16[16,16,576]{2,1,0:T(8,128)(2,1)S(1)}, bf16[16,16,576]{2,1,0:T(8,128)(2,1)S(1)}, u32[]{:S(2)}, u32[]{:S(2)}) collective-permute-start(bf16[16,16,576]{2,1,0:T(8,128)(2,1)S(1)} %all_to_all.10.refs_4_), channel_id=1, source_target_pairs={{0,14},{2,0},{4,2},{6,4},{8,6},{10,8},{12,10},{14,12},{1,15},{3,1}... | collective-permute-start | bytes 884744 | tf_op jit(solution)/shard_map/ppermute | solution.py:343
  27.9 27.2 %copy-start.8 = (bf16[16,16,576]{2,1,0:T(8,128)(2,1)}, bf16[16,16,576]{2,1,0:T(8,128)(2,1)S(1)}, u32[]{:S(2)}) copy-start(bf16[16,16,576]{2,1,0:T(8,128)(2,1)S(1)} %collective-permute-done.refs_3_) | copy-start | bytes 884740
  27.9 8.8 %collective-permute-start.1 = (bf16[16,16,576]{2,1,0:T(8,128)(2,1)S(1)}, bf16[16,16,576]{2,1,0:T(8,128)(2,1)S(1)}, u32[]{:S(2)}, u32[]{:S(2)}) collective-permute-start(bf16[16,16,576]{2,1,0:T(8,128)(2,1)S(1)} %collective-permute-done.refs_3_), channel_id=1, source_target_pairs={{0,2},{2,4},{4,6},{6,8},{8,10},{10,12},{12,14},{14,0},{1,3},{3,5},... | collective-permute-start | bytes 884744 | tf_op jit(solution)/shard_map/ppermute | solution.py:341
  27.9 1.3 %copy-start = (bf16[8,512,128]{2,1,0:T(8,128)(2,1)S(1)}, bf16[8,512,128]{2,1,0:T(8,128)(2,1)}, u32[]{:S(2)}) copy-start(bf16[8,512,128]{2,1,0:T(8,128)(2,1)} %refs_4_.1) | copy-start | bytes 3145732
  29.2 1.0 copy-start.2
  30.2 0.8 copy-start.3
  31.9 23.2 %copy-start.9 = (bf16[16,16,576]{2,1,0:T(8,128)(2,1)}, bf16[16,16,576]{2,1,0:T(8,128)(2,1)S(1)}, u32[]{:S(2)}) copy-start(bf16[16,16,576]{2,1,0:T(8,128)(2,1)S(1)} %collective-permute-done.4.refs_5_) | copy-start | bytes 884740
  31.9 8.0 %collective-permute-start.5 = (bf16[16,16,576]{2,1,0:T(8,128)(2,1)S(1)}, bf16[16,16,576]{2,1,0:T(8,128)(2,1)S(1)}, u32[]{:S(2)}, u32[]{:S(2)}) collective-permute-start(bf16[16,16,576]{2,1,0:T(8,128)(2,1)S(1)} %collective-permute-done.4.refs_5_), channel_id=1, source_target_pairs={{0,14},{2,0},{4,2},{6,4},{8,6},{10,8},{12,10},{14,12},{1,15},{3,1}... | collective-permute-start | bytes 884744 | tf_op jit(solution)/shard_map/ppermute | solution.py:343
  36.7 18.4 %copy-start.10 = (bf16[16,16,576]{2,1,0:T(8,128)(2,1)}, bf16[16,16,576]{2,1,0:T(8,128)(2,1)S(1)}, u32[]{:S(2)}) copy-start(bf16[16,16,576]{2,1,0:T(8,128)(2,1)S(1)} %collective-permute-done.1.refs_2_) | copy-start | bytes 884740
  36.7 8.5 %collective-permute-start.2 = (bf16[16,16,576]{2,1,0:T(8,128)(2,1)S(1)}, bf16[16,16,576]{2,1,0:T(8,128)(2,1)S(1)}, u32[]{:S(2)}, u32[]{:S(2)}) collective-permute-start(bf16[16,16,576]{2,1,0:T(8,128)(2,1)S(1)} %collective-permute-done.1.refs_2_), channel_id=1, source_target_pairs={{0,2},{2,4},{4,6},{6,8},{8,10},{10,12},{12,14},{14,0},{1,3},{3,5},... | collective-permute-start | bytes 884744 | tf_op jit(solution)/shard_map/ppermute | solution.py:341
  36.7 8.5 %collective-permute-start.11 = (bf16[16,16,576]{2,1,0:T(8,128)(2,1)S(1)}, bf16[16,16,576]{2,1,0:T(8,128)(2,1)S(1)}, u32[]{:S(2)}, u32[]{:S(2)}) collective-permute-start(bf16[16,16,576]{2,1,0:T(8,128)(2,1)S(1)} %all_to_all.10.refs_4_), channel_id=1, source_target_pairs={{0,1},{1,0},{2,3},{3,2},{4,5},{5,4},{6,7},{7,6},{8,9},{9,8},{10,11... | collective-permute-start | bytes 884744 | tf_op jit(solution)/shard_map/ppermute | solution.py:311
  36.7 8.6 %collective-permute-start.12 = (bf16[16,16,576]{2,1,0:T(8,128)(2,1)S(1)}, bf16[16,16,576]{2,1,0:T(8,128)(2,1)S(1)}, u32[]{:S(2)}, u32[]{:S(2)}) collective-permute-start(bf16[16,16,576]{2,1,0:T(8,128)(2,1)S(1)} %collective-permute-done.4.refs_5_), channel_id=1, source_target_pairs={{0,1},{1,0},{2,3},{3,2},{4,5},{5,4},{6,7},{7,6},{8,9},{9,8},{10,11... | collective-permute-start | bytes 884744 | tf_op jit(solution)/shard_map/ppermute | solution.py:311
  37.2 8.6 %collective-permute-start.10 = (bf16[16,16,576]{2,1,0:T(8,128)(2,1)S(1)}, bf16[16,16,576]{2,1,0:T(8,128)(2,1)S(1)}, u32[]{:S(2)}, u32[]{:S(2)}) collective-permute-start(bf16[16,16,576]{2,1,0:T(8,128)(2,1)S(1)} %collective-permute-done.refs_3_), channel_id=1, source_target_pairs={{0,1},{1,0},{2,3},{3,2},{4,5},{5,4},{6,7},{7,6},{8,9},{9,8},{10,11... | collective-permute-start | bytes 884744 | tf_op jit(solution)/shard_map/ppermute | solution.py:311
  40.0 15.1 %copy-start.11 = (bf16[16,16,576]{2,1,0:T(8,128)(2,1)}, bf16[16,16,576]{2,1,0:T(8,128)(2,1)S(1)}, u32[]{:S(2)}) copy-start(bf16[16,16,576]{2,1,0:T(8,128)(2,1)S(1)} %collective-permute-done.5.refs_6_) | copy-start | bytes 884740
  40.0 8.3 %collective-permute-start.6 = (bf16[16,16,576]{2,1,0:T(8,128)(2,1)S(1)}, bf16[16,16,576]{2,1,0:T(8,128)(2,1)S(1)}, u32[]{:S(2)}, u32[]{:S(2)}) collective-permute-start(bf16[16,16,576]{2,1,0:T(8,128)(2,1)S(1)} %collective-permute-done.5.refs_6_), channel_id=1, source_target_pairs={{0,14},{2,0},{4,2},{6,4},{8,6},{10,8},{12,10},{14,12},{1,15},{3,1}... | collective-permute-start | bytes 884744 | tf_op jit(solution)/shard_map/ppermute | solution.py:343
  45.2 10.0 %copy-start.12 = (bf16[16,16,576]{2,1,0:T(8,128)(2,1)}, bf16[16,16,576]{2,1,0:T(8,128)(2,1)S(1)}, u32[]{:S(2)}) copy-start(bf16[16,16,576]{2,1,0:T(8,128)(2,1)S(1)} %collective-permute-done.2.refs_1_) | copy-start | bytes 884740
  45.2 8.3 %collective-permute-start.3 = (bf16[16,16,576]{2,1,0:T(8,128)(2,1)S(1)}, bf16[16,16,576]{2,1,0:T(8,128)(2,1)S(1)}, u32[]{:S(2)}, u32[]{:S(2)}) collective-permute-start(bf16[16,16,576]{2,1,0:T(8,128)(2,1)S(1)} %collective-permute-done.2.refs_1_), channel_id=1, source_target_pairs={{0,2},{2,4},{4,6},{6,8},{8,10},{10,12},{12,14},{14,0},{1,3},{3,5},... | collective-permute-start | bytes 884744 | tf_op jit(solution)/shard_map/ppermute | solution.py:341
  45.2 10.0 %copy-start.13 = (bf16[16,16,576]{2,1,0:T(8,128)(2,1)}, bf16[16,16,576]{2,1,0:T(8,128)(2,1)S(1)}, u32[]{:S(2)}) copy-start(bf16[16,16,576]{2,1,0:T(8,128)(2,1)S(1)} %collective-permute-done.11.refs_12_) | copy-start | bytes 884740
  45.2 8.3 %collective-permute-start.9 = (bf16[16,16,576]{2,1,0:T(8,128)(2,1)S(1)}, bf16[16,16,576]{2,1,0:T(8,128)(2,1)S(1)}, u32[]{:S(2)}, u32[]{:S(2)}) collective-permute-start(bf16[16,16,576]{2,1,0:T(8,128)(2,1)S(1)} %collective-permute-done.1.refs_2_), channel_id=1, source_target_pairs={{0,1},{1,0},{2,3},{3,2},{4,5},{5,4},{6,7},{7,6},{8,9},{9,8},{10,11... | collective-permute-start | bytes 884744 | tf_op jit(solution)/shard_map/ppermute | solution.py:311
  45.3 9.8 %copy-start.14 = (bf16[16,16,576]{2,1,0:T(8,128)(2,1)}, bf16[16,16,576]{2,1,0:T(8,128)(2,1)S(1)}, u32[]{:S(2)}) copy-start(bf16[16,16,576]{2,1,0:T(8,128)(2,1)S(1)} %collective-permute-done.12.refs_13_) | copy-start | bytes 884740
  45.3 8.2 %collective-permute-start.13 = (bf16[16,16,576]{2,1,0:T(8,128)(2,1)S(1)}, bf16[16,16,576]{2,1,0:T(8,128)(2,1)S(1)}, u32[]{:S(2)}, u32[]{:S(2)}) collective-permute-start(bf16[16,16,576]{2,1,0:T(8,128)(2,1)S(1)} %collective-permute-done.5.refs_6_), channel_id=1, source_target_pairs={{0,1},{1,0},{2,3},{3,2},{4,5},{5,4},{6,7},{7,6},{8,9},{9,8},{10,11... | collective-permute-start | bytes 884744 | tf_op jit(solution)/shard_map/ppermute | solution.py:311
  45.8 9.4 %copy-start.15 = (bf16[16,16,576]{2,1,0:T(8,128)(2,1)}, bf16[16,16,576]{2,1,0:T(8,128)(2,1)S(1)}, u32[]{:S(2)}) copy-start(bf16[16,16,576]{2,1,0:T(8,128)(2,1)S(1)} %collective-permute-done.10.refs_11_) | copy-start | bytes 884740
  45.8 7.7 %collective-permute-start.8 = (bf16[16,16,576]{2,1,0:T(8,128)(2,1)S(1)}, bf16[16,16,576]{2,1,0:T(8,128)(2,1)S(1)}, u32[]{:S(2)}, u32[]{:S(2)}) collective-permute-start(bf16[16,16,576]{2,1,0:T(8,128)(2,1)S(1)} %collective-permute-done.2.refs_1_), channel_id=1, source_target_pairs={{0,1},{1,0},{2,3},{3,2},{4,5},{5,4},{6,7},{7,6},{8,9},{9,8},{10,11... | collective-permute-start | bytes 884744 | tf_op jit(solution)/shard_map/ppermute | solution.py:311
  48.3 6.9 %copy-start.16 = (bf16[16,16,576]{2,1,0:T(8,128)(2,1)}, bf16[16,16,576]{2,1,0:T(8,128)(2,1)S(1)}, u32[]{:S(2)}) copy-start(bf16[16,16,576]{2,1,0:T(8,128)(2,1)S(1)} %collective-permute-done.6.refs_7_) | copy-start | bytes 884740
  48.3 5.2 %collective-permute-start.14 = (bf16[16,16,576]{2,1,0:T(8,128)(2,1)S(1)}, bf16[16,16,576]{2,1,0:T(8,128)(2,1)S(1)}, u32[]{:S(2)}, u32[]{:S(2)}) collective-permute-start(bf16[16,16,576]{2,1,0:T(8,128)(2,1)S(1)} %collective-permute-done.6.refs_7_), channel_id=1, source_target_pairs={{0,1},{1,0},{2,3},{3,2},{4,5},{5,4},{6,7},{7,6},{8,9},{9,8},{10,11... | collective-permute-start | bytes 884744 | tf_op jit(solution)/shard_map/ppermute | solution.py:311
  53.5 1.7 %copy-start.17 = (bf16[16,16,576]{2,1,0:T(8,128)(2,1)}, bf16[16,16,576]{2,1,0:T(8,128)(2,1)S(1)}, u32[]{:S(2)}) copy-start(bf16[16,16,576]{2,1,0:T(8,128)(2,1)S(1)} %collective-permute-done.3.refs_0_) | copy-start | bytes 884740
  53.5 1.6 %collective-permute-start.7 = (bf16[16,16,576]{2,1,0:T(8,128)(2,1)S(1)}, bf16[16,16,576]{2,1,0:T(8,128)(2,1)S(1)}, u32[]{:S(2)}, u32[]{:S(2)}) collective-permute-start(bf16[16,16,576]{2,1,0:T(8,128)(2,1)S(1)} %collective-permute-done.3.refs_0_), channel_id=1, source_target_pairs={{0,1},{1,0},{2,3},{3,2},{4,5},{5,4},{6,7},{7,6},{8,9},{9,8},{10,11... | collective-permute-start | bytes 884744 | tf_op jit(solution)/shard_map/ppermute | solution.py:311
  53.5 1.7 %copy-start.19 = (bf16[16,16,576]{2,1,0:T(8,128)(2,1)}, bf16[16,16,576]{2,1,0:T(8,128)(2,1)S(1)}, u32[]{:S(2)}) copy-start(bf16[16,16,576]{2,1,0:T(8,128)(2,1)S(1)} %collective-permute-done.13.refs_14_) | copy-start | bytes 884740
  53.5 1.7 %copy-start.18 = (bf16[16,16,576]{2,1,0:T(8,128)(2,1)}, bf16[16,16,576]{2,1,0:T(8,128)(2,1)S(1)}, u32[]{:S(2)}) copy-start(bf16[16,16,576]{2,1,0:T(8,128)(2,1)S(1)} %collective-permute-done.9.refs_10_) | copy-start | bytes 884740
  53.5 1.7 %copy-start.21 = (bf16[16,16,576]{2,1,0:T(8,128)(2,1)}, bf16[16,16,576]{2,1,0:T(8,128)(2,1)S(1)}, u32[]{:S(2)}) copy-start(bf16[16,16,576]{2,1,0:T(8,128)(2,1)S(1)} %collective-permute-done.14.refs_15_) | copy-start | bytes 884740
  53.5 1.7 %copy-start.20 = (bf16[16,16,576]{2,1,0:T(8,128)(2,1)}, bf16[16,16,576]{2,1,0:T(8,128)(2,1)S(1)}, u32[]{:S(2)}) copy-start(bf16[16,16,576]{2,1,0:T(8,128)(2,1)S(1)} %collective-permute-done.8.refs_9_) | copy-start | bytes 884740
  55.1 0.7 copy-start.22
  55.8 52.5 %copy-start.1 = (bf16[8,512,128]{2,1,0:T(8,128)(2,1)S(1)}, bf16[8,512,128]{2,1,0:T(8,128)(2,1)}, u32[]{:S(2)}) copy-start(bf16[8,512,128]{2,1,0:T(8,128)(2,1)} %refs_4_.1) | copy-start | bytes 3145732
  73.3 1.6 %collective-permute-start.19 = (bf16[17,16,512]{2,1,0:T(8,128)(2,1)S(1)}, bf16[17,16,512]{2,1,0:T(8,128)(2,1)S(1)}, u32[]{:S(2)}, u32[]{:S(2)}) collective-permute-start(bf16[17,16,512]{2,1,0:T(8,128)(2,1)S(1)} %get-tuple-element.37), channel_id=1, source_target_pairs={{0,1},{1,0},{2,3},{3,2},{4,5},{5,4},{6,7},{7,6},{8,9},{9,8},{10,11... | collective-permute-start | bytes 835592 | tf_op jit(solution)/shard_map/ppermute | solution.py:311
  73.4 2.4 %collective-permute-start.26 = (bf16[17,16,512]{2,1,0:T(8,128)(2,1)}, bf16[17,16,512]{2,1,0:T(8,128)(2,1)S(1)}, u32[]{:S(2)}, u32[]{:S(2)}) collective-permute-start(bf16[17,16,512]{2,1,0:T(8,128)(2,1)} %get-tuple-element.43), channel_id=1, source_target_pairs={{0,1},{1,0},{2,3},{3,2},{4,5},{5,4},{6,7},{7,6},{8,9},{9,8},{10,11... | collective-permute-start | bytes 835592 | tf_op jit(solution)/shard_map/ppermute | solution.py:311
  73.8 4.3 %collective-permute-start.18 = (bf16[17,16,512]{2,1,0:T(8,128)(2,1)S(1)}, bf16[17,16,512]{2,1,0:T(8,128)(2,1)S(1)}, u32[]{:S(2)}, u32[]{:S(2)}) collective-permute-start(bf16[17,16,512]{2,1,0:T(8,128)(2,1)S(1)} %get-tuple-element.35), channel_id=1, source_target_pairs={{0,1},{1,0},{2,3},{3,2},{4,5},{5,4},{6,7},{7,6},{8,9},{9,8},{10,11... | collective-permute-start | bytes 835592 | tf_op jit(solution)/shard_map/ppermute | solution.py:311
  75.1 8.8 %collective-permute-start.20 = (bf16[17,16,512]{2,1,0:T(8,128)(2,1)S(1)}, bf16[17,16,512]{2,1,0:T(8,128)(2,1)S(1)}, u32[]{:S(2)}, u32[]{:S(2)}) collective-permute-start(bf16[17,16,512]{2,1,0:T(8,128)(2,1)S(1)} %shard_map.76), channel_id=1, source_target_pairs={{0,14},{2,0},{4,2},{6,4},{8,6},{10,8},{12,10},{14,12},{1,15},{3,1}... | collective-permute-start | bytes 835592 | tf_op jit(solution)/shard_map/ppermute | solution.py:373
  75.2 11.9 %collective-permute-start.17 = (bf16[17,16,512]{2,1,0:T(8,128)(2,1)S(1)}, bf16[17,16,512]{2,1,0:T(8,128)(2,1)S(1)}, u32[]{:S(2)}, u32[]{:S(2)}) collective-permute-start(bf16[17,16,512]{2,1,0:T(8,128)(2,1)S(1)} %get-tuple-element.33), channel_id=1, source_target_pairs={{0,1},{1,0},{2,3},{3,2},{4,5},{5,4},{6,7},{7,6},{8,9},{9,8},{10,11... | collective-permute-start | bytes 835592 | tf_op jit(solution)/shard_map/ppermute | solution.py:311
  75.4 10.3 %collective-permute-start.25 = (bf16[17,16,512]{2,1,0:T(8,128)(2,1)}, bf16[17,16,512]{2,1,0:T(8,128)(2,1)S(1)}, u32[]{:S(2)}, u32[]{:S(2)}) collective-permute-start(bf16[17,16,512]{2,1,0:T(8,128)(2,1)} %get-tuple-element.41), channel_id=1, source_target_pairs={{0,1},{1,0},{2,3},{3,2},{4,5},{5,4},{6,7},{7,6},{8,9},{9,8},{10,11... | collective-permute-start | bytes 835592 | tf_op jit(solution)/shard_map/ppermute | solution.py:311
  76.0 10.2 %collective-permute-start.27 = (bf16[17,16,512]{2,1,0:T(8,128)(2,1)S(1)}, bf16[17,16,512]{2,1,0:T(8,128)(2,1)S(1)}, u32[]{:S(2)}, u32[]{:S(2)}) collective-permute-start(bf16[17,16,512]{2,1,0:T(8,128)(2,1)S(1)} %shard_map.80), channel_id=1, source_target_pairs={{0,2},{2,4},{4,6},{6,8},{8,10},{10,12},{12,14},{14,0},{1,3},{3,5},... | collective-permute-start | bytes 835592 | tf_op jit(solution)/shard_map/ppermute | solution.py:376
  84.1 7.9 %collective-permute-start.21 = (bf16[17,16,512]{2,1,0:T(8,128)(2,1)S(1)}, bf16[17,16,512]{2,1,0:T(8,128)(2,1)S(1)}, u32[]{:S(2)}, u32[]{:S(2)}) collective-permute-start(bf16[17,16,512]{2,1,0:T(8,128)(2,1)S(1)} %shard_map.77), channel_id=1, source_target_pairs={{0,14},{2,0},{4,2},{6,4},{8,6},{10,8},{12,10},{14,12},{1,15},{3,1}... | collective-permute-start | bytes 835592 | tf_op jit(solution)/shard_map/ppermute | solution.py:373
  85.7 11.0 %collective-permute-start.16 = (bf16[17,16,512]{2,1,0:T(8,128)(2,1)S(1)}, bf16[17,16,512]{2,1,0:T(8,128)(2,1)S(1)}, u32[]{:S(2)}, u32[]{:S(2)}) collective-permute-start(bf16[17,16,512]{2,1,0:T(8,128)(2,1)S(1)} %get-tuple-element.31), channel_id=1, source_target_pairs={{0,1},{1,0},{2,3},{3,2},{4,5},{5,4},{6,7},{7,6},{8,9},{9,8},{10,11... | collective-permute-start | bytes 835592 | tf_op jit(solution)/shard_map/ppermute | solution.py:311
  85.7 9.7 %collective-permute-start.24 = (bf16[17,16,512]{2,1,0:T(8,128)(2,1)S(1)}, bf16[17,16,512]{2,1,0:T(8,128)(2,1)S(1)}, u32[]{:S(2)}, u32[]{:S(2)}) collective-permute-start(bf16[17,16,512]{2,1,0:T(8,128)(2,1)S(1)} %get-tuple-element.39), channel_id=1, source_target_pairs={{0,1},{1,0},{2,3},{3,2},{4,5},{5,4},{6,7},{7,6},{8,9},{9,8},{10,11... | collective-permute-start | bytes 835592 | tf_op jit(solution)/shard_map/ppermute | solution.py:311
  86.4 9.9 %collective-permute-start.28 = (bf16[17,16,512]{2,1,0:T(8,128)(2,1)S(1)}, bf16[17,16,512]{2,1,0:T(8,128)(2,1)S(1)}, u32[]{:S(2)}, u32[]{:S(2)}) collective-permute-start(bf16[17,16,512]{2,1,0:T(8,128)(2,1)S(1)} %shard_map.81), channel_id=1, source_target_pairs={{0,2},{2,4},{4,6},{6,8},{8,10},{10,12},{12,14},{14,0},{1,3},{3,5},... | collective-permute-start | bytes 835592 | tf_op jit(solution)/shard_map/ppermute | solution.py:376
  92.3 7.9 %collective-permute-start.22 = (bf16[17,16,512]{2,1,0:T(8,128)(2,1)S(1)}, bf16[17,16,512]{2,1,0:T(8,128)(2,1)S(1)}, u32[]{:S(2)}, u32[]{:S(2)}) collective-permute-start(bf16[17,16,512]{2,1,0:T(8,128)(2,1)S(1)} %shard_map.78), channel_id=1, source_target_pairs={{0,14},{2,0},{4,2},{6,4},{8,6},{10,8},{12,10},{14,12},{1,15},{3,1}... | collective-permute-start | bytes 835592 | tf_op jit(solution)/shard_map/ppermute | solution.py:373
  95.4 8.8 %collective-permute-start.15 = (bf16[17,16,512]{2,1,0:T(8,128)(2,1)S(1)}, bf16[17,16,512]{2,1,0:T(8,128)(2,1)S(1)}, u32[]{:S(2)}, u32[]{:S(2)}) collective-permute-start(bf16[17,16,512]{2,1,0:T(8,128)(2,1)S(1)} %get-tuple-element.29), channel_id=1, source_target_pairs={{0,1},{1,0},{2,3},{3,2},{4,5},{5,4},{6,7},{7,6},{8,9},{9,8},{10,11... | collective-permute-start | bytes 835592 | tf_op jit(solution)/shard_map/ppermute | solution.py:311
  96.6 9.5 %collective-permute-start.29 = (bf16[17,16,512]{2,1,0:T(8,128)(2,1)S(1)}, bf16[17,16,512]{2,1,0:T(8,128)(2,1)S(1)}, u32[]{:S(2)}, u32[]{:S(2)}) collective-permute-start(bf16[17,16,512]{2,1,0:T(8,128)(2,1)S(1)} %shard_map.82), channel_id=1, source_target_pairs={{0,2},{2,4},{4,6},{6,8},{8,10},{10,12},{12,14},{14,0},{1,3},{3,5},... | collective-permute-start | bytes 835592 | tf_op jit(solution)/shard_map/ppermute | solution.py:376
  100.5 7.8 %collective-permute-start.23 = (bf16[17,16,512]{2,1,0:T(8,128)(2,1)S(1)}, bf16[17,16,512]{2,1,0:T(8,128)(2,1)S(1)}, u32[]{:S(2)}, u32[]{:S(2)}) collective-permute-start(bf16[17,16,512]{2,1,0:T(8,128)(2,1)S(1)} %shard_map.79), channel_id=1, source_target_pairs={{0,14},{2,0},{4,2},{6,4},{8,6},{10,8},{12,10},{14,12},{1,15},{3,1}... | collective-permute-start | bytes 835592 | tf_op jit(solution)/shard_map/ppermute | solution.py:373

commit v2 on v1

--- a/solution.py
+++ b/solution.py
@@ -12,7 +12,7 @@
 F32 = jnp.float32
 BF16 = jnp.bfloat16
 MIB = 1024 * 1024
-GROUP = 4
+GROUP = 2
 
 
 def pack_stat(stat):
@@ -48,8 +48,8 @@
         counts.append(lax.div(total - split + (split_count - 1), split_count))
     pairs = [lax.div(count + 1, 2) for count in counts]
     for c in range(slots // 2 + 1):
-        longer = [(p > c).astype(jnp.int32) for p in pairs]
-        next_ref[c] = functools.reduce(jnp.add, longer)
+        shorter = [(p < c).astype(jnp.int32) for p in pairs]
+        next_ref[c] = functools.reduce(jnp.add, shorter)
     for i in range(requests):
         at = next_ref[pairs[i]]
         next_ref[pairs[i]] = at + 1
@@ -74,7 +74,7 @@
     groups = requests // GROUP
 
     def each(g, act):
-        pairs = plan_ref[g * GROUP, 1]
+        pairs = plan_ref[g * GROUP + GROUP - 1, 1]
         half = lax.rem(g, 2)
         for m in range(GROUP):
             for j in range(slots):
@@ -142,7 +142,7 @@
             each(g + 1, lambda c: c.start())
 
         each(g, lambda c: c.wait())
-        pairs_here = plan_ref[g * GROUP, 1]
+        pairs_here = plan_ref[g * GROUP + GROUP - 1, 1]
         for pairs in range(1, slots // 2 + 1):
 
             @pl.when(pairs_here == pairs)
@@ -336,15 +336,13 @@
         out_specs=vmem(1)[0],
     )
 
+    own_q, plan, new_values = lax.optimization_barrier((own_q, plan, new_values))
+
     queries = {0: own_q}
     for s in range(1, far + 1):
         queries[-s] = lax.ppermute(queries[1 - s], "seq", up)
         if s <= near:
             queries[s] = lax.ppermute(queries[s - 1], "seq", down)
-        if s == 1:
-            queries[-s], plan = lax.optimization_barrier((queries[-s], plan))
-        if s == 2:
-            queries[-s], new_values = lax.optimization_barrier((queries[-s], new_values))
     order = sorted(queries)
     q_list = [queries[r] for r in order] + [swap(queries[r]) for r in order]
     n_pieces = len(q_list)
@@ -362,7 +360,7 @@
             pltpu.VMEM((n_pieces * rows, 128), F32),
             pltpu.SemaphoreType.DMA((2, GROUP, slots)),
         ],
-        mib=50,
+        mib=44,
     )
     mine = dict(zip(order, outs[: len(order)]))
     others = {r: swap(x) for r, x in zip(order, outs[len(order) :])}

time: 122 us -> 121 us (level)
  blocking collectives: 25.9 us -> 14.9 us
  waiting for transfers between devices: 37.8 us -> 47.3 us
  starting transfers between devices: 27.4 us -> 34.2 us
  Pallas kernels: 23.6 us -> 18.6 us
    all_to_all x1 -> x0, blocking collectives: 15.5 us -> none  [shards(): lax.all_to_all(decode_q, 'pre', split_axis=0, concat_axis=0, tiled=True)]
    ppermute x4, waiting for transfers between devices: 11 us -> 22.4 us  [shards(): queries[-s] = lax.ppermute(queries[1 - s], 'seq', up)]
    all_to_all x0 -> x1, starting transfers between devices: none -> 7.48 us  [shards(): lax.all_to_all(decode_q, 'pre', split_axis=0, concat_axis=0, tiled=True)]
    pallas_call x12, Pallas kernels: 23.6 us -> 18.6 us  [call(): pl.pallas_call(kernel, out_shape=out_shape, compiler_params=pltpu.Compile...]
    all_to_all x1, blocking collectives: 10.4 us -> 14.9 us  [shards(): got = lax.all_to_all(values, 'pre', split_axis=0, concat_axis=0, tiled=True)]
    ppermute x3, waiting for transfers between devices: 5.04 us -> 2.49 us  [shards(): queries[s] = lax.ppermute(queries[s - 1], 'seq', down)]
    unnamed x46 -> x14, local copies, waits for them, and re-layouts: 5.71 us -> 4.93 us
  transfers between devices with their start and end apart: 30 -> 31, of which waited for: 14 -> 14; matrix products, arithmetic and copies ran while one was open for 0% -> 0% of each run, Pallas kernels for 3% -> 3%
where the time goes in v2:
time: 121 us; the launch traced here: 120 us
  waiting for transfers between devices  47.3 us (39%)
  starting transfers between devices  34.2 us (28%)
  Pallas kernels  18.6 us (15%)
  blocking collectives  14.9 us (12%)
  local copies, waits for them, and re-layouts  4.93 us (4%)
    ppermute x4, waiting for transfers between devices, shards(): queries[-s] = lax.ppermute(queries[1 - s], 'seq', up)  22.4 us
    pallas_call x12, Pallas kernels, call(): pl.pallas_call(kernel, out_shape=out_shape, compiler_params=pltpu.Compile...  18.6 us
    ppermute x4, waiting for transfers between devices, shards(): from_up = [lax.ppermute(sent, 'seq', down)]  17 us
    all_to_all x1, blocking collectives, shards(): got = lax.all_to_all(values, 'pre', split_axis=0, concat_axis=0, tiled=True)  14.9 us
    ppermute x3, starting transfers between devices, shards(): queries[s] = lax.ppermute(queries[s - 1], 'seq', down)  10.4 us
    ppermute x4, starting transfers between devices, shards(): from_up = [lax.ppermute(sent, 'seq', down)]  8.75 us
    all_to_all x1, starting transfers between devices, shards(): lax.all_to_all(decode_q, 'pre', split_axis=0, concat_axis=0, tiled=True)  7.48 us
    unnamed x14, local copies, waits for them, and re-layouts  4.93 us
  transfers between devices with their start and end apart: 31, of which 14 were waited for; matrix products, arithmetic and copies ran while one was open for 0% of the time, Pallas kernels for 3%

profile of v2, /device:TPU:2, one launch (start us, length us, event | category | flops | bytes accessed | tf_op | source)
XLA Modules:
  0.0 120.1 jit_solution(8120075527506313450)
XLA Ops:
  0.0 7.5 %all-to-all-start = ((bf16[16,16,576]{2,1,0:T(8,128)(2,1)}), bf16[16,16,576]{2,1,0:T(8,128)(2,1)S(1)}, u32[]{:S(2)}, u32[]{:S(2)}) async-start(bf16[16,16,576]{2,1,0:T(8,128)(2,1)} %bitcast.7), calls=%async_computation | async-start | bytes 655360 | tf_op jit(solution)/shard_map/all_to_all | solution.py:314
  7.5 1.2 %copy-done = bf16[8,512,128]{2,1,0:T(8,128)(2,1)S(1)} copy-done((bf16[8,512,128]{2,1,0:T(8,128)(2,1)S(1)}, bf16[8,512,128]{2,1,0:T(8,128)(2,1)}, u32[]{:S(2)}) %copy-start) | copy-done | bytes 1048600
  8.7 1.0 copy-done.2
  9.7 0.8 copy-done.3
  10.5 0.9 shard_map.74.new_ref
  11.4 0.0 copy-start.4
  11.4 0.6 copy-done.4
  12.1 0.7 copy-done.5
  12.7 0.7 copy-done.6
  13.4 1.7 %shard_map.73.plan_ref = s32[16,11]{1,0:T(8,128)S(1)} custom-call(s32[1,16]{1,0:T(1,128)S(1)} %copy-done.4, s32[1,16]{1,0:T(1,128)S(1)} %copy-done.5, s32[1,1,1,128]{3,2,1,0:T(1,128)S(1)} %copy-done.6, s32[1]{0:T(128)} %bitcast.1.split_ref), custom_call_target="tpu_custom_call" | custom-call | tf_op jit(solution)/shard_map/pallas_call | solution.py:268
  15.1 0.4 all-to-all-done.refs_4_
  15.5 1.9 %collective-permute-start = (bf16[16,16,576]{2,1,0:T(8,128)(2,1)S(1)}, bf16[16,16,576]{2,1,0:T(8,128)(2,1)S(1)}, u32[]{:S(2)}, u32[]{:S(2)}) collective-permute-start(bf16[16,16,576]{2,1,0:T(8,128)(2,1)S(1)} %all-to-all-done.refs_4_), channel_id=1, source_target_pairs={{0,2},{2,4},{4,6},{6,8},{8,10},{10,12},{12,14},{14,0},{1,3},{3,5},... | collective-permute-start | bytes 884744 | tf_op jit(solution)/shard_map/ppermute | solution.py:343
  17.4 3.9 %collective-permute-start.4 = (bf16[16,16,576]{2,1,0:T(8,128)(2,1)S(1)}, bf16[16,16,576]{2,1,0:T(8,128)(2,1)S(1)}, u32[]{:S(2)}, u32[]{:S(2)}) collective-permute-start(bf16[16,16,576]{2,1,0:T(8,128)(2,1)S(1)} %all-to-all-done.refs_4_), channel_id=1, source_target_pairs={{0,14},{2,0},{4,2},{6,4},{8,6},{10,8},{12,10},{14,12},{1,15},{3,1}... | collective-permute-start | bytes 884744 | tf_op jit(solution)/shard_map/ppermute | solution.py:345
  21.4 6.8 %collective-permute-done.refs_3_ = bf16[16,16,576]{2,1,0:T(8,128)(2,1)S(1)} collective-permute-done((bf16[16,16,576]{2,1,0:T(8,128)(2,1)S(1)}, bf16[16,16,576]{2,1,0:T(8,128)(2,1)S(1)}, u32[]{:S(2)}, u32[]{:S(2)}) %collective-permute-start) | collective-permute-done | bytes 294944 | tf_op jit(solution)/shard_map/ppermute | solution.py:343
  28.2 0.0 collective-permute-start.1
  28.2 0.0 collective-permute-done.4.refs_5_
  28.2 3.2 %collective-permute-start.5 = (bf16[16,16,576]{2,1,0:T(8,128)(2,1)S(1)}, bf16[16,16,576]{2,1,0:T(8,128)(2,1)S(1)}, u32[]{:S(2)}, u32[]{:S(2)}) collective-permute-start(bf16[16,16,576]{2,1,0:T(8,128)(2,1)S(1)} %collective-permute-done.4.refs_5_), channel_id=1, source_target_pairs={{0,14},{2,0},{4,2},{6,4},{8,6},{10,8},{12,10},{14,12},{1,15},{3,1}... | collective-permute-start | bytes 884744 | tf_op jit(solution)/shard_map/ppermute | solution.py:345
  31.4 5.9 %collective-permute-done.1.refs_2_ = bf16[16,16,576]{2,1,0:T(8,128)(2,1)S(1)} collective-permute-done((bf16[16,16,576]{2,1,0:T(8,128)(2,1)S(1)}, bf16[16,16,576]{2,1,0:T(8,128)(2,1)S(1)}, u32[]{:S(2)}, u32[]{:S(2)}) %collective-permute-start.1) | collective-permute-done | bytes 294944 | tf_op jit(solution)/shard_map/ppermute | solution.py:343
  37.3 0.5 collective-permute-start.12
  37.8 0.0 collective-permute-start.10
  37.8 3.2 %collective-permute-start.6 = (bf16[16,16,576]{2,1,0:T(8,128)(2,1)S(1)}, bf16[16,16,576]{2,1,0:T(8,128)(2,1)S(1)}, u32[]{:S(2)}, u32[]{:S(2)}) collective-permute-start(bf16[16,16,576]{2,1,0:T(8,128)(2,1)S(1)} %collective-permute-done.5.refs_6_), channel_id=1, source_target_pairs={{0,14},{2,0},{4,2},{6,4},{8,6},{10,8},{12,10},{14,12},{1,15},{3,1}... | collective-permute-start | bytes 884744 | tf_op jit(solution)/shard_map/ppermute | solution.py:345
  41.0 4.5 %collective-permute-done.2.refs_1_ = bf16[16,16,576]{2,1,0:T(8,128)(2,1)S(1)} collective-permute-done((bf16[16,16,576]{2,1,0:T(8,128)(2,1)S(1)}, bf16[16,16,576]{2,1,0:T(8,128)(2,1)S(1)}, u32[]{:S(2)}, u32[]{:S(2)}) %collective-permute-start.2) | collective-permute-done | bytes 294944 | tf_op jit(solution)/shard_map/ppermute | solution.py:343
  45.6 0.0 collective-permute-start.3
  45.6 0.0 collective-permute-done.11.refs_12_
  45.6 0.0 collective-permute-start.13
  45.6 0.5 collective-permute-start.9
  46.1 0.1 collective-permute-start.8
  46.2 2.5 %collective-permute-done.6.refs_7_ = bf16[16,16,576]{2,1,0:T(8,128)(2,1)S(1)} collective-permute-done((bf16[16,16,576]{2,1,0:T(8,128)(2,1)S(1)}, bf16[16,16,576]{2,1,0:T(8,128)(2,1)S(1)}, u32[]{:S(2)}, u32[]{:S(2)}) %collective-permute-start.6) | collective-permute-done | bytes 294944 | tf_op jit(solution)/shard_map/ppermute | solution.py:345
  48.7 0.0 collective-permute-start.14
  48.7 5.2 %collective-permute-done.3.refs_0_ = bf16[16,16,576]{2,1,0:T(8,128)(2,1)S(1)} collective-permute-done((bf16[16,16,576]{2,1,0:T(8,128)(2,1)S(1)}, bf16[16,16,576]{2,1,0:T(8,128)(2,1)S(1)}, u32[]{:S(2)}, u32[]{:S(2)}) %collective-permute-start.3) | collective-permute-done | bytes 294944 | tf_op jit(solution)/shard_map/ppermute | solution.py:343
  53.9 0.0 collective-permute-start.7
  53.9 1.6 %collective-permute-done.7.refs_8_ = bf16[16,16,576]{2,1,0:T(8,128)(2,1)S(1)} collective-permute-done((bf16[16,16,576]{2,1,0:T(8,128)(2,1)S(1)}, bf16[16,16,576]{2,1,0:T(8,128)(2,1)S(1)}, u32[]{:S(2)}, u32[]{:S(2)}) %collective-permute-start.7) | collective-permute-done | bytes 294944 | tf_op jit(solution)/shard_map/ppermute | solution.py:311
  55.5 12.5 %shard_map.75 = (bf16[17,16,512]{2,1,0:T(8,128)(2,1)S(1)}, bf16[17,16,512]{2,1,0:T(8,128)(2,1)S(1)}, bf16[17,16,512]{2,1,0:T(8,128)(2,1)S(1)}, bf16[17,16,512]{2...) custom-call(s32[16,11]{1,0:T(8,128)S(1)} %shard_map.73.plan_ref, ...), custom_call_target="tpu_custom_call" | custom-call | tf_op jit(solution)/shard_map/pallas_call | solution.py:268
  68.0 0.2 collective-permute-start.19
  68.3 0.4 collective-permute-start.26
  68.6 0.1 collective-permute-start.18
  68.8 0.9 collective-permute-done.19.refs_1_
  69.7 0.2 shard_map.76
  69.9 0.1 collective-permute-start.20
  70.0 0.2 collective-permute-start.17
  70.2 0.4 collective-permute-start.25
  70.5 0.0 collective-permute-done.26.refs_1_
  70.6 0.2 shard_map.80
  70.7 2.0 %collective-permute-start.27 = (bf16[17,16,512]{2,1,0:T(8,128)(2,1)S(1)}, bf16[17,16,512]{2,1,0:T(8,128)(2,1)S(1)}, u32[]{:S(2)}, u32[]{:S(2)}) collective-permute-start(bf16[17,16,512]{2,1,0:T(8,128)(2,1)S(1)} %shard_map.80), channel_id=1, source_target_pairs={{0,2},{2,4},{4,6},{6,8},{8,10},{10,12},{12,14},{14,0},{1,3},{3,5},... | collective-permute-start | bytes 835592 | tf_op jit(solution)/shard_map/ppermute | solution.py:374
  72.7 5.9 %collective-permute-done.20.refs_2_ = bf16[17,16,512]{2,1,0:T(8,128)(2,1)S(1)} collective-permute-done((bf16[17,16,512]{2,1,0:T(8,128)(2,1)S(1)}, bf16[17,16,512]{2,1,0:T(8,128)(2,1)S(1)}, u32[]{:S(2)}, u32[]{:S(2)}) %collective-permute-start.20) | collective-permute-done | bytes 278560 | tf_op jit(solution)/shard_map/ppermute | solution.py:371
  78.6 0.2 shard_map.77
  78.9 1.6 %collective-permute-start.21 = (bf16[17,16,512]{2,1,0:T(8,128)(2,1)S(1)}, bf16[17,16,512]{2,1,0:T(8,128)(2,1)S(1)}, u32[]{:S(2)}, u32[]{:S(2)}) collective-permute-start(bf16[17,16,512]{2,1,0:T(8,128)(2,1)S(1)} %shard_map.77), channel_id=1, source_target_pairs={{0,14},{2,0},{4,2},{6,4},{8,6},{10,8},{12,10},{14,12},{1,15},{3,1}... | collective-permute-start | bytes 835592 | tf_op jit(solution)/shard_map/ppermute | solution.py:371
  80.5 0.5 collective-permute-start.24
  81.0 0.2 shard_map.81
  81.2 0.6 collective-permute-start.28
  81.8 5.0 %collective-permute-done.21.refs_2_ = bf16[17,16,512]{2,1,0:T(8,128)(2,1)S(1)} collective-permute-done((bf16[17,16,512]{2,1,0:T(8,128)(2,1)S(1)}, bf16[17,16,512]{2,1,0:T(8,128)(2,1)S(1)}, u32[]{:S(2)}, u32[]{:S(2)}) %collective-permute-start.21) | collective-permute-done | bytes 278560 | tf_op jit(solution)/shard_map/ppermute | solution.py:371
  86.8 0.2 shard_map.78
  87.1 3.3 %collective-permute-start.22 = (bf16[17,16,512]{2,1,0:T(8,128)(2,1)S(1)}, bf16[17,16,512]{2,1,0:T(8,128)(2,1)S(1)}, u32[]{:S(2)}, u32[]{:S(2)}) collective-permute-start(bf16[17,16,512]{2,1,0:T(8,128)(2,1)S(1)} %shard_map.78), channel_id=1, source_target_pairs={{0,14},{2,0},{4,2},{6,4},{8,6},{10,8},{12,10},{14,12},{1,15},{3,1}... | collective-permute-start | bytes 835592 | tf_op jit(solution)/shard_map/ppermute | solution.py:371
  90.4 0.7 collective-permute-done.28.refs_2_
  91.1 0.2 shard_map.82
  91.3 0.1 collective-permute-start.29
  91.4 3.8 %collective-permute-done.22.refs_2_ = bf16[17,16,512]{2,1,0:T(8,128)(2,1)S(1)} collective-permute-done((bf16[17,16,512]{2,1,0:T(8,128)(2,1)S(1)}, bf16[17,16,512]{2,1,0:T(8,128)(2,1)S(1)}, u32[]{:S(2)}, u32[]{:S(2)}) %collective-permute-start.22) | collective-permute-done | bytes 278560 | tf_op jit(solution)/shard_map/ppermute | solution.py:371
  95.2 0.2 shard_map.79
  95.4 3.8 %collective-permute-start.23 = (bf16[17,16,512]{2,1,0:T(8,128)(2,1)S(1)}, bf16[17,16,512]{2,1,0:T(8,128)(2,1)S(1)}, u32[]{:S(2)}, u32[]{:S(2)}) collective-permute-start(bf16[17,16,512]{2,1,0:T(8,128)(2,1)S(1)} %shard_map.79), channel_id=1, source_target_pairs={{0,14},{2,0},{4,2},{6,4},{8,6},{10,8},{12,10},{14,12},{1,15},{3,1}... | collective-permute-start | bytes 835592 | tf_op jit(solution)/shard_map/ppermute | solution.py:371
  99.2 1.8 %collective-permute-done.29.refs_3_ = bf16[17,16,512]{2,1,0:T(8,128)(2,1)S(1)} collective-permute-done((bf16[17,16,512]{2,1,0:T(8,128)(2,1)S(1)}, bf16[17,16,512]{2,1,0:T(8,128)(2,1)S(1)}, u32[]{:S(2)}, u32[]{:S(2)}) %collective-permute-start.29) | collective-permute-done | bytes 278560 | tf_op jit(solution)/shard_map/ppermute | solution.py:374
  101.0 2.3 %collective-permute-done.23.refs_2_ = bf16[17,16,512]{2,1,0:T(8,128)(2,1)S(1)} collective-permute-done((bf16[17,16,512]{2,1,0:T(8,128)(2,1)S(1)}, bf16[17,16,512]{2,1,0:T(8,128)(2,1)S(1)}, u32[]{:S(2)}, u32[]{:S(2)}) %collective-permute-start.23) | collective-permute-done | bytes 278560 | tf_op jit(solution)/shard_map/ppermute | solution.py:371
  103.3 0.9 shard_map.83
  104.2 14.9 %all_to_all.10.cache_ref = f32[16,2,1152]{2,1,0:T(2,128)S(1)} all-to-all(f32[16,2,1152]{2,1,0:T(2,128)S(1)} %shard_map.83), channel_id=1, replica_groups=mesh['pre'=16,'seq'=8,'dec'=2] {'pre'}, dimensions={0} | all-to-all | bytes 294912 | tf_op jit(solution)/shard_map/all_to_all | solution.py:384
  119.1 1.0 shard_map.84
  (25 shorter events, 0.1 us)
Async XLA Ops:
  0.0 15.5 %all-to-all-start = ((bf16[16,16,576]{2,1,0:T(8,128)(2,1)}), bf16[16,16,576]{2,1,0:T(8,128)(2,1)S(1)}, u32[]{:S(2)}, u32[]{:S(2)}) async-start(bf16[16,16,576]{2,1,0:T(8,128)(2,1)} %bitcast.7), calls=%async_computation | async-start | bytes 655360 | tf_op jit(solution)/shard_map/all_to_all | solution.py:314
  7.5 1.2 %copy-start = (bf16[8,512,128]{2,1,0:T(8,128)(2,1)S(1)}, bf16[8,512,128]{2,1,0:T(8,128)(2,1)}, u32[]{:S(2)}) copy-start(bf16[8,512,128]{2,1,0:T(8,128)(2,1)} %refs_4_.1) | copy-start | bytes 3145732
  8.7 1.0 copy-start.2
  9.7 0.8 copy-start.3
  11.4 0.7 copy-start.4
  12.1 0.7 copy-start.5
  12.7 0.7 copy-start.6
  15.5 12.7 %collective-permute-start = (bf16[16,16,576]{2,1,0:T(8,128)(2,1)S(1)}, bf16[16,16,576]{2,1,0:T(8,128)(2,1)S(1)}, u32[]{:S(2)}, u32[]{:S(2)}) collective-permute-start(bf16[16,16,576]{2,1,0:T(8,128)(2,1)S(1)} %all-to-all-done.refs_4_), channel_id=1, source_target_pairs={{0,2},{2,4},{4,6},{6,8},{8,10},{10,12},{12,14},{14,0},{1,3},{3,5},... | collective-permute-start | bytes 884744 | tf_op jit(solution)/shard_map/ppermute | solution.py:343
  17.4 10.8 %collective-permute-start.4 = (bf16[16,16,576]{2,1,0:T(8,128)(2,1)S(1)}, bf16[16,16,576]{2,1,0:T(8,128)(2,1)S(1)}, u32[]{:S(2)}, u32[]{:S(2)}) collective-permute-start(bf16[16,16,576]{2,1,0:T(8,128)(2,1)S(1)} %all-to-all-done.refs_4_), channel_id=1, source_target_pairs={{0,14},{2,0},{4,2},{6,4},{8,6},{10,8},{12,10},{14,12},{1,15},{3,1}... | collective-permute-start | bytes 884744 | tf_op jit(solution)/shard_map/ppermute | solution.py:345
  28.2 9.1 %collective-permute-start.1 = (bf16[16,16,576]{2,1,0:T(8,128)(2,1)S(1)}, bf16[16,16,576]{2,1,0:T(8,128)(2,1)S(1)}, u32[]{:S(2)}, u32[]{:S(2)}) collective-permute-start(bf16[16,16,576]{2,1,0:T(8,128)(2,1)S(1)} %collective-permute-done.refs_3_), channel_id=1, source_target_pairs={{0,2},{2,4},{4,6},{6,8},{8,10},{10,12},{12,14},{14,0},{1,3},{3,5},... | collective-permute-start | bytes 884744 | tf_op jit(solution)/shard_map/ppermute | solution.py:343
  28.2 9.6 %collective-permute-start.5 = (bf16[16,16,576]{2,1,0:T(8,128)(2,1)S(1)}, bf16[16,16,576]{2,1,0:T(8,128)(2,1)S(1)}, u32[]{:S(2)}, u32[]{:S(2)}) collective-permute-start(bf16[16,16,576]{2,1,0:T(8,128)(2,1)S(1)} %collective-permute-done.4.refs_5_), channel_id=1, source_target_pairs={{0,14},{2,0},{4,2},{6,4},{8,6},{10,8},{12,10},{14,12},{1,15},{3,1}... | collective-permute-start | bytes 884744 | tf_op jit(solution)/shard_map/ppermute | solution.py:345
  37.3 8.3 %collective-permute-start.2 = (bf16[16,16,576]{2,1,0:T(8,128)(2,1)S(1)}, bf16[16,16,576]{2,1,0:T(8,128)(2,1)S(1)}, u32[]{:S(2)}, u32[]{:S(2)}) collective-permute-start(bf16[16,16,576]{2,1,0:T(8,128)(2,1)S(1)} %collective-permute-done.1.refs_2_), channel_id=1, source_target_pairs={{0,2},{2,4},{4,6},{6,8},{8,10},{10,12},{12,14},{14,0},{1,3},{3,5},... | collective-permute-start | bytes 884744 | tf_op jit(solution)/shard_map/ppermute | solution.py:343
  37.3 8.3 %collective-permute-start.11 = (bf16[16,16,576]{2,1,0:T(8,128)(2,1)S(1)}, bf16[16,16,576]{2,1,0:T(8,128)(2,1)S(1)}, u32[]{:S(2)}, u32[]{:S(2)}) collective-permute-start(bf16[16,16,576]{2,1,0:T(8,128)(2,1)S(1)} %all-to-all-done.refs_4_), channel_id=1, source_target_pairs={{0,1},{1,0},{2,3},{3,2},{4,5},{5,4},{6,7},{7,6},{8,9},{9,8},{10,11... | collective-permute-start | bytes 884744 | tf_op jit(solution)/shard_map/ppermute | solution.py:311
  37.3 8.3 %collective-permute-start.12 = (bf16[16,16,576]{2,1,0:T(8,128)(2,1)S(1)}, bf16[16,16,576]{2,1,0:T(8,128)(2,1)S(1)}, u32[]{:S(2)}, u32[]{:S(2)}) collective-permute-start(bf16[16,16,576]{2,1,0:T(8,128)(2,1)S(1)} %collective-permute-done.4.refs_5_), channel_id=1, source_target_pairs={{0,1},{1,0},{2,3},{3,2},{4,5},{5,4},{6,7},{7,6},{8,9},{9,8},{10,11... | collective-permute-start | bytes 884744 | tf_op jit(solution)/shard_map/ppermute | solution.py:311
  37.8 8.3 %collective-permute-start.10 = (bf16[16,16,576]{2,1,0:T(8,128)(2,1)S(1)}, bf16[16,16,576]{2,1,0:T(8,128)(2,1)S(1)}, u32[]{:S(2)}, u32[]{:S(2)}) collective-permute-start(bf16[16,16,576]{2,1,0:T(8,128)(2,1)S(1)} %collective-permute-done.refs_3_), channel_id=1, source_target_pairs={{0,1},{1,0},{2,3},{3,2},{4,5},{5,4},{6,7},{7,6},{8,9},{9,8},{10,11... | collective-permute-start | bytes 884744 | tf_op jit(solution)/shard_map/ppermute | solution.py:311
  37.8 10.9 %collective-permute-start.6 = (bf16[16,16,576]{2,1,0:T(8,128)(2,1)S(1)}, bf16[16,16,576]{2,1,0:T(8,128)(2,1)S(1)}, u32[]{:S(2)}, u32[]{:S(2)}) collective-permute-start(bf16[16,16,576]{2,1,0:T(8,128)(2,1)S(1)} %collective-permute-done.5.refs_6_), channel_id=1, source_target_pairs={{0,14},{2,0},{4,2},{6,4},{8,6},{10,8},{12,10},{14,12},{1,15},{3,1}... | collective-permute-start | bytes 884744 | tf_op jit(solution)/shard_map/ppermute | solution.py:345
  45.6 8.3 %collective-permute-start.3 = (bf16[16,16,576]{2,1,0:T(8,128)(2,1)S(1)}, bf16[16,16,576]{2,1,0:T(8,128)(2,1)S(1)}, u32[]{:S(2)}, u32[]{:S(2)}) collective-permute-start(bf16[16,16,576]{2,1,0:T(8,128)(2,1)S(1)} %collective-permute-done.2.refs_1_), channel_id=1, source_target_pairs={{0,2},{2,4},{4,6},{6,8},{8,10},{10,12},{12,14},{14,0},{1,3},{3,5},... | collective-permute-start | bytes 884744 | tf_op jit(solution)/shard_map/ppermute | solution.py:343
  45.6 8.3 %collective-permute-start.13 = (bf16[16,16,576]{2,1,0:T(8,128)(2,1)S(1)}, bf16[16,16,576]{2,1,0:T(8,128)(2,1)S(1)}, u32[]{:S(2)}, u32[]{:S(2)}) collective-permute-start(bf16[16,16,576]{2,1,0:T(8,128)(2,1)S(1)} %collective-permute-done.5.refs_6_), channel_id=1, source_target_pairs={{0,1},{1,0},{2,3},{3,2},{4,5},{5,4},{6,7},{7,6},{8,9},{9,8},{10,11... | collective-permute-start | bytes 884744 | tf_op jit(solution)/shard_map/ppermute | solution.py:311
  45.6 8.3 %collective-permute-start.9 = (bf16[16,16,576]{2,1,0:T(8,128)(2,1)S(1)}, bf16[16,16,576]{2,1,0:T(8,128)(2,1)S(1)}, u32[]{:S(2)}, u32[]{:S(2)}) collective-permute-start(bf16[16,16,576]{2,1,0:T(8,128)(2,1)S(1)} %collective-permute-done.1.refs_2_), channel_id=1, source_target_pairs={{0,1},{1,0},{2,3},{3,2},{4,5},{5,4},{6,7},{7,6},{8,9},{9,8},{10,11... | collective-permute-start | bytes 884744 | tf_op jit(solution)/shard_map/ppermute | solution.py:311
  46.1 7.8 %collective-permute-start.8 = (bf16[16,16,576]{2,1,0:T(8,128)(2,1)S(1)}, bf16[16,16,576]{2,1,0:T(8,128)(2,1)S(1)}, u32[]{:S(2)}, u32[]{:S(2)}) collective-permute-start(bf16[16,16,576]{2,1,0:T(8,128)(2,1)S(1)} %collective-permute-done.2.refs_1_), channel_id=1, source_target_pairs={{0,1},{1,0},{2,3},{3,2},{4,5},{5,4},{6,7},{7,6},{8,9},{9,8},{10,11... | collective-permute-start | bytes 884744 | tf_op jit(solution)/shard_map/ppermute | solution.py:311
  48.7 5.2 %collective-permute-start.14 = (bf16[16,16,576]{2,1,0:T(8,128)(2,1)S(1)}, bf16[16,16,576]{2,1,0:T(8,128)(2,1)S(1)}, u32[]{:S(2)}, u32[]{:S(2)}) collective-permute-start(bf16[16,16,576]{2,1,0:T(8,128)(2,1)S(1)} %collective-permute-done.6.refs_7_), channel_id=1, source_target_pairs={{0,1},{1,0},{2,3},{3,2},{4,5},{5,4},{6,7},{7,6},{8,9},{9,8},{10,11... | collective-permute-start | bytes 884744 | tf_op jit(solution)/shard_map/ppermute | solution.py:311
  53.9 1.6 %collective-permute-start.7 = (bf16[16,16,576]{2,1,0:T(8,128)(2,1)S(1)}, bf16[16,16,576]{2,1,0:T(8,128)(2,1)S(1)}, u32[]{:S(2)}, u32[]{:S(2)}) collective-permute-start(bf16[16,16,576]{2,1,0:T(8,128)(2,1)S(1)} %collective-permute-done.3.refs_0_), channel_id=1, source_target_pairs={{0,1},{1,0},{2,3},{3,2},{4,5},{5,4},{6,7},{7,6},{8,9},{9,8},{10,11... | collective-permute-start | bytes 884744 | tf_op jit(solution)/shard_map/ppermute | solution.py:311
  55.5 47.8 %copy-start.1 = (bf16[8,512,128]{2,1,0:T(8,128)(2,1)S(1)}, bf16[8,512,128]{2,1,0:T(8,128)(2,1)}, u32[]{:S(2)}) copy-start(bf16[8,512,128]{2,1,0:T(8,128)(2,1)} %refs_4_.1) | copy-start | bytes 3145732
  68.0 1.6 %collective-permute-start.19 = (bf16[17,16,512]{2,1,0:T(8,128)(2,1)S(1)}, bf16[17,16,512]{2,1,0:T(8,128)(2,1)S(1)}, u32[]{:S(2)}, u32[]{:S(2)}) collective-permute-start(bf16[17,16,512]{2,1,0:T(8,128)(2,1)S(1)} %get-tuple-element.35), channel_id=1, source_target_pairs={{0,1},{1,0},{2,3},{3,2},{4,5},{5,4},{6,7},{7,6},{8,9},{9,8},{10,11... | collective-permute-start | bytes 835592 | tf_op jit(solution)/shard_map/ppermute | solution.py:311
  68.3 2.3 %collective-permute-start.26 = (bf16[17,16,512]{2,1,0:T(8,128)(2,1)S(1)}, bf16[17,16,512]{2,1,0:T(8,128)(2,1)S(1)}, u32[]{:S(2)}, u32[]{:S(2)}) collective-permute-start(bf16[17,16,512]{2,1,0:T(8,128)(2,1)S(1)} %get-tuple-element.41), channel_id=1, source_target_pairs={{0,1},{1,0},{2,3},{3,2},{4,5},{5,4},{6,7},{7,6},{8,9},{9,8},{10,11... | collective-permute-start | bytes 835592 | tf_op jit(solution)/shard_map/ppermute | solution.py:311
  68.6 4.1 %collective-permute-start.18 = (bf16[17,16,512]{2,1,0:T(8,128)(2,1)S(1)}, bf16[17,16,512]{2,1,0:T(8,128)(2,1)S(1)}, u32[]{:S(2)}, u32[]{:S(2)}) collective-permute-start(bf16[17,16,512]{2,1,0:T(8,128)(2,1)S(1)} %get-tuple-element.33), channel_id=1, source_target_pairs={{0,1},{1,0},{2,3},{3,2},{4,5},{5,4},{6,7},{7,6},{8,9},{9,8},{10,11... | collective-permute-start | bytes 835592 | tf_op jit(solution)/shard_map/ppermute | solution.py:311
  69.9 8.8 %collective-permute-start.20 = (bf16[17,16,512]{2,1,0:T(8,128)(2,1)S(1)}, bf16[17,16,512]{2,1,0:T(8,128)(2,1)S(1)}, u32[]{:S(2)}, u32[]{:S(2)}) collective-permute-start(bf16[17,16,512]{2,1,0:T(8,128)(2,1)S(1)} %shard_map.76), channel_id=1, source_target_pairs={{0,14},{2,0},{4,2},{6,4},{8,6},{10,8},{12,10},{14,12},{1,15},{3,1}... | collective-permute-start | bytes 835592 | tf_op jit(solution)/shard_map/ppermute | solution.py:371
  70.0 11.9 %collective-permute-start.17 = (bf16[17,16,512]{2,1,0:T(8,128)(2,1)S(1)}, bf16[17,16,512]{2,1,0:T(8,128)(2,1)S(1)}, u32[]{:S(2)}, u32[]{:S(2)}) collective-permute-start(bf16[17,16,512]{2,1,0:T(8,128)(2,1)S(1)} %get-tuple-element.31), channel_id=1, source_target_pairs={{0,1},{1,0},{2,3},{3,2},{4,5},{5,4},{6,7},{7,6},{8,9},{9,8},{10,11... | collective-permute-start | bytes 835592 | tf_op jit(solution)/shard_map/ppermute | solution.py:311
  70.2 10.3 %collective-permute-start.25 = (bf16[17,16,512]{2,1,0:T(8,128)(2,1)S(1)}, bf16[17,16,512]{2,1,0:T(8,128)(2,1)S(1)}, u32[]{:S(2)}, u32[]{:S(2)}) collective-permute-start(bf16[17,16,512]{2,1,0:T(8,128)(2,1)S(1)} %get-tuple-element.39), channel_id=1, source_target_pairs={{0,1},{1,0},{2,3},{3,2},{4,5},{5,4},{6,7},{7,6},{8,9},{9,8},{10,11... | collective-permute-start | bytes 835592 | tf_op jit(solution)/shard_map/ppermute | solution.py:311
  70.7 10.2 %collective-permute-start.27 = (bf16[17,16,512]{2,1,0:T(8,128)(2,1)S(1)}, bf16[17,16,512]{2,1,0:T(8,128)(2,1)S(1)}, u32[]{:S(2)}, u32[]{:S(2)}) collective-permute-start(bf16[17,16,512]{2,1,0:T(8,128)(2,1)S(1)} %shard_map.80), channel_id=1, source_target_pairs={{0,2},{2,4},{4,6},{6,8},{8,10},{10,12},{12,14},{14,0},{1,3},{3,5},... | collective-permute-start | bytes 835592 | tf_op jit(solution)/shard_map/ppermute | solution.py:374
  78.9 7.9 %collective-permute-start.21 = (bf16[17,16,512]{2,1,0:T(8,128)(2,1)S(1)}, bf16[17,16,512]{2,1,0:T(8,128)(2,1)S(1)}, u32[]{:S(2)}, u32[]{:S(2)}) collective-permute-start(bf16[17,16,512]{2,1,0:T(8,128)(2,1)S(1)} %shard_map.77), channel_id=1, source_target_pairs={{0,14},{2,0},{4,2},{6,4},{8,6},{10,8},{12,10},{14,12},{1,15},{3,1}... | collective-permute-start | bytes 835592 | tf_op jit(solution)/shard_map/ppermute | solution.py:371
  80.5 11.0 %collective-permute-start.16 = (bf16[17,16,512]{2,1,0:T(8,128)(2,1)S(1)}, bf16[17,16,512]{2,1,0:T(8,128)(2,1)S(1)}, u32[]{:S(2)}, u32[]{:S(2)}) collective-permute-start(bf16[17,16,512]{2,1,0:T(8,128)(2,1)S(1)} %get-tuple-element.29), channel_id=1, source_target_pairs={{0,1},{1,0},{2,3},{3,2},{4,5},{5,4},{6,7},{7,6},{8,9},{9,8},{10,11... | collective-permute-start | bytes 835592 | tf_op jit(solution)/shard_map/ppermute | solution.py:311
  80.5 9.9 %collective-permute-start.24 = (bf16[17,16,512]{2,1,0:T(8,128)(2,1)S(1)}, bf16[17,16,512]{2,1,0:T(8,128)(2,1)S(1)}, u32[]{:S(2)}, u32[]{:S(2)}) collective-permute-start(bf16[17,16,512]{2,1,0:T(8,128)(2,1)S(1)} %get-tuple-element.37), channel_id=1, source_target_pairs={{0,1},{1,0},{2,3},{3,2},{4,5},{5,4},{6,7},{7,6},{8,9},{9,8},{10,11... | collective-permute-start | bytes 835592 | tf_op jit(solution)/shard_map/ppermute | solution.py:311
  81.2 9.9 %collective-permute-start.28 = (bf16[17,16,512]{2,1,0:T(8,128)(2,1)S(1)}, bf16[17,16,512]{2,1,0:T(8,128)(2,1)S(1)}, u32[]{:S(2)}, u32[]{:S(2)}) collective-permute-start(bf16[17,16,512]{2,1,0:T(8,128)(2,1)S(1)} %shard_map.81), channel_id=1, source_target_pairs={{0,2},{2,4},{4,6},{6,8},{8,10},{10,12},{12,14},{14,0},{1,3},{3,5},... | collective-permute-start | bytes 835592 | tf_op jit(solution)/shard_map/ppermute | solution.py:374
  87.1 8.1 %collective-permute-start.22 = (bf16[17,16,512]{2,1,0:T(8,128)(2,1)S(1)}, bf16[17,16,512]{2,1,0:T(8,128)(2,1)S(1)}, u32[]{:S(2)}, u32[]{:S(2)}) collective-permute-start(bf16[17,16,512]{2,1,0:T(8,128)(2,1)S(1)} %shard_map.78), channel_id=1, source_target_pairs={{0,14},{2,0},{4,2},{6,4},{8,6},{10,8},{12,10},{14,12},{1,15},{3,1}... | collective-permute-start | bytes 835592 | tf_op jit(solution)/shard_map/ppermute | solution.py:371
  90.4 8.8 %collective-permute-start.15 = (bf16[17,16,512]{2,1,0:T(8,128)(2,1)S(1)}, bf16[17,16,512]{2,1,0:T(8,128)(2,1)S(1)}, u32[]{:S(2)}, u32[]{:S(2)}) collective-permute-start(bf16[17,16,512]{2,1,0:T(8,128)(2,1)S(1)} %get-tuple-element.27), channel_id=1, source_target_pairs={{0,1},{1,0},{2,3},{3,2},{4,5},{5,4},{6,7},{7,6},{8,9},{9,8},{10,11... | collective-permute-start | bytes 835592 | tf_op jit(solution)/shard_map/ppermute | solution.py:311
  91.3 9.7 %collective-permute-start.29 = (bf16[17,16,512]{2,1,0:T(8,128)(2,1)S(1)}, bf16[17,16,512]{2,1,0:T(8,128)(2,1)S(1)}, u32[]{:S(2)}, u32[]{:S(2)}) collective-permute-start(bf16[17,16,512]{2,1,0:T(8,128)(2,1)S(1)} %shard_map.82), channel_id=1, source_target_pairs={{0,2},{2,4},{4,6},{6,8},{8,10},{10,12},{12,14},{14,0},{1,3},{3,5},... | collective-permute-start | bytes 835592 | tf_op jit(solution)/shard_map/ppermute | solution.py:374
  95.4 7.8 %collective-permute-start.23 = (bf16[17,16,512]{2,1,0:T(8,128)(2,1)S(1)}, bf16[17,16,512]{2,1,0:T(8,128)(2,1)S(1)}, u32[]{:S(2)}, u32[]{:S(2)}) collective-permute-start(bf16[17,16,512]{2,1,0:T(8,128)(2,1)S(1)} %shard_map.79), channel_id=1, source_target_pairs={{0,14},{2,0},{4,2},{6,4},{8,6},{10,8},{12,10},{14,12},{1,15},{3,1}... | collective-permute-start | bytes 835592 | tf_op jit(solution)/shard_map/ppermute | solution.py:371

commit v3 on v2

--- a/solution.py
+++ b/solution.py
@@ -62,15 +62,50 @@
             out_ref[at, 3 + j] = table_ref[0, 0, 0, i * slots + j]
 
 
+def as_pieces(refs):
+    per_core = len(refs) // 2
+    pieces = []
+    for core in (refs[:per_core], refs[per_core:]):
+        pieces += [core[:2]] + [(ref,) for ref in core[2:]]
+    return pieces
+
+
+def load(piece, who):
+    if len(piece) == 1:
+        return piece[0][who]
+    first, second = piece
+    half = first.shape[0]
+    low = first[jnp.minimum(who, half - 1)]
+    high = second[jnp.maximum(who - half, 0)]
+    return jnp.where(who < half, low, high)
+
+
+def store(piece, who, value):
+    if len(piece) == 1:
+        piece[0][who] = value
+        return
+    first, second = piece
+    half = first.shape[0] - 1
+
+    @pl.when(who < half)
+    def _():
+        first[who] = value
+
+    @pl.when(who >= half)
+    def _():
+        second[who - half] = value
+
+
 def attention_kernel(n_pieces, plan_ref, *refs):
-    q_refs = refs[:n_pieces]
-    pool_ref = refs[n_pieces]
-    o_refs = refs[n_pieces + 1 : 2 * n_pieces + 1]
-    kbuf, stat_ref, sems = refs[2 * n_pieces + 1 :]
-    requests, rows, _ = q_refs[0].shape
+    n_refs = n_pieces + 2
+    q_pieces = as_pieces(refs[:n_refs])
+    pool_ref = refs[n_refs]
+    o_pieces = as_pieces(refs[n_refs + 1 : 2 * n_refs + 1])
+    kbuf, stat_ref, sems = refs[2 * n_refs + 1 :]
+    requests, rows, _ = q_pieces[1][0].shape
     slots = plan_ref.shape[1] - 3
     block = pool_ref.shape[2]
-    latent = o_refs[0].shape[2]
+    latent = o_pieces[0][0].shape[2]
     groups = requests // GROUP
 
     def each(g, act):
@@ -101,7 +136,7 @@
         keys, scores, tops = [], [], []
         for m, who in enumerate(whos):
             used = plan_ref[g * GROUP + m, 2]
-            q = jnp.concatenate([ref[who] for ref in q_refs], axis=0)
+            q = jnp.concatenate([load(piece, who) for piece in q_pieces], axis=0)
             keys.append(
                 [
                     jnp.concatenate([kbuf[half, m, 2 * c], kbuf[half, m, 2 * c + 1]], axis=1)
@@ -131,8 +166,8 @@
             total = jnp.sum(total, axis=1, keepdims=True)
             some = total > 0
             out = (out * jnp.where(some, 1.0 / total, 0.0)).astype(BF16)
-            for n, ref in enumerate(o_refs):
-                ref[who] = out[n * rows : (n + 1) * rows]
+            for n, piece in enumerate(o_pieces):
+                store(piece, who, out[n * rows : (n + 1) * rows])
             stat = jnp.where(some, tops[m] + jnp.log2(total), EMPTY)
             stat_ref[...] = jnp.where(lane == who, stat, stat_ref[...])
 
@@ -153,19 +188,24 @@
         def _():
             for m in range(GROUP):
                 who = plan_ref[g * GROUP + m, 0]
-                for ref in o_refs:
-                    ref[who] = jnp.zeros((rows, latent), BF16)
+                for piece in o_pieces:
+                    store(piece, who, jnp.zeros((rows, latent), BF16))
                 stat_ref[...] = jnp.where(lane == who, EMPTY, stat_ref[...])
 
         return carry
 
     lax.fori_loop(0, groups, step, 0)
-    for n, ref in enumerate(o_refs):
-        write_stat(ref, stat_ref[n * rows : (n + 1) * rows, :])
-
-
-def weights_of(refs):
-    stats = [read_stat(ref) for ref in refs]
+    for n, piece in enumerate(o_pieces):
+        for ref in piece:
+            write_stat(ref, stat_ref[n * rows : (n + 1) * rows, :])
+
+
+def weights_of(refs, spans):
+    stats = []
+    for ref, (first, last) in zip(refs, spans):
+        stat = read_stat(ref)
+        lane = lax.broadcasted_iota(jnp.int32, stat.shape, 1)
+        stats.append(jnp.where((lane >= first) & (lane < last), stat, EMPTY))
     top = functools.reduce(jnp.maximum, stats)
     parts = [jnp.exp2(stat - top) for stat in stats]
     total = functools.reduce(jnp.add, parts)
@@ -173,20 +213,22 @@
     return [part * share for part in parts], top + jnp.log2(total)
 
 
-def combined(refs, weights, who):
+def combined(refs, spans, weights, who):
     out = None
-    for ref, weight in zip(refs, weights):
-        part = ref[who].astype(F32) * weight[:, who : who + 1]
-        out = part if out is None else out + part
+    for ref, (first, last), weight in zip(refs, spans, weights):
+        if first <= who < last:
+            part = ref[who - first].astype(F32) * weight[:, who : who + 1]
+            out = part if out is None else out + part
     return out
 
 
-def combine_kernel(*refs):
+def combine_kernel(spans, *refs):
     *pieces, out_ref = refs
-    weights, stat = weights_of(pieces)
+    weights, stat = weights_of(pieces, spans)
     write_stat(out_ref, stat)
-    for who in range(out_ref.shape[0] - 1):
-        out_ref[who] = combined(pieces, weights, who).astype(BF16)
+    first, last = spans[0]
+    for who in range(first, last):
+        out_ref[who - first] = combined(pieces, spans, weights, who).astype(BF16)
 
 
 def project(latents, stats, proj_ref, out_ref):
@@ -240,8 +282,11 @@
 def finish_kernel(*refs):
     *pieces, proj_ref, out_ref = refs
     requests = out_ref.shape[0]
-    weights, stat = weights_of(pieces)
-    latents = [combined(pieces, weights, who).astype(BF16) for who in range(requests)]
+    spans = [(0, requests)] * len(pieces)
+    weights, stat = weights_of(pieces, spans)
+    latents = [
+        combined(pieces, spans, weights, who).astype(BF16) for who in range(requests)
+    ]
     stats = [stat[:, who : who + 1] for who in range(requests)]
     project(latents, stats, proj_ref, out_ref)
 
@@ -282,13 +327,16 @@
 
 
 def combine(pieces):
-    return call(
-        combine_kernel,
-        jax.ShapeDtypeStruct(pieces[0].shape, BF16),
-        *pieces,
+    arrays = [array for array, _ in pieces]
+    spans = tuple(span for _, span in pieces)
+    out = call(
+        functools.partial(combine_kernel, spans),
+        jax.ShapeDtypeStruct(arrays[0].shape, BF16),
+        *arrays,
         in_specs=vmem(len(pieces)),
         out_specs=vmem(1)[0],
     )
+    return out, spans[0]
 
 
 def shards(block_pool, block_table, lengths, destination, query_latent, new_latent, value_proj):
@@ -301,7 +349,7 @@
     latent, value_width = value_proj.shape[1:]
     block = block_pool.shape[4]
     slots = block_table.shape[3] // requests
-    far, near = ring // 2, (ring - 1) // 2
+    far = ring // 2
     pool = jnp.swapaxes(block_pool[0, 0, 0], 1, 2)
 
     up = [(i, (i + 1) % ring) for i in range(ring)]
@@ -338,23 +386,36 @@
 
     own_q, plan, new_values = lax.optimization_barrier((own_q, plan, new_values))
 
+    half = requests // 2
     queries = {0: own_q}
-    for s in range(1, far + 1):
+    for s in range(1, far):
         queries[-s] = lax.ppermute(queries[1 - s], "seq", up)
-        if s <= near:
-            queries[s] = lax.ppermute(queries[s - 1], "seq", down)
+        queries[s] = lax.ppermute(queries[s - 1], "seq", down)
+    halves = [
+        lax.ppermute(queries[1 - far][:half], "seq", up),
+        lax.ppermute(queries[far - 1][half:], "seq", down),
+    ]
     order = sorted(queries)
-    q_list = [queries[r] for r in order] + [swap(queries[r]) for r in order]
-    n_pieces = len(q_list)
+    early = [r for r in order if abs(r) < far - 2]
+    late = [r for r in order if abs(r) >= far - 2]
+    waited = early + [2 - far, far - 2]
+    tied = dict(zip(waited, lax.optimization_barrier([queries[r] for r in waited])))
+    tied.update(zip(late, lax.optimization_barrier([queries[r] for r in late])))
+    near_by = [tied[r] for r in order]
+    q_list = halves + near_by + [swap(x) for x in near_by + halves]
+    q_list = q_list[: len(order) + 2] + q_list[-2:] + q_list[len(order) + 2 : -2]
+    n_pieces = 2 * (len(order) + 1)
+    half_piece = jax.ShapeDtypeStruct((half + 1, rows, latent), BF16)
     piece = jax.ShapeDtypeStruct((requests + 1, rows, latent), BF16)
+    shapes = ([half_piece] * 2 + [piece] * len(order)) * 2
     outs = call(
         functools.partial(attention_kernel, n_pieces),
-        [piece] * n_pieces,
+        shapes,
         plan,
         *q_list,
         pool,
-        in_specs=smem(1) + vmem(n_pieces) + [pl.BlockSpec(memory_space=pltpu.HBM)],
-        out_specs=vmem(n_pieces),
+        in_specs=smem(1) + vmem(len(q_list)) + [pl.BlockSpec(memory_space=pltpu.HBM)],
+        out_specs=vmem(len(q_list)),
         scratch_shapes=[
             pltpu.VMEM((2, GROUP, slots, width, block), BF16),
             pltpu.VMEM((n_pieces * rows, 128), F32),
@@ -362,17 +423,25 @@
         ],
         mib=44,
     )
-    mine = dict(zip(order, outs[: len(order)]))
-    others = {r: swap(x) for r, x in zip(order, outs[len(order) :])}
-
-    from_up, from_down = [], []
-    for s in range(far, 0, -1):
-        sent = combine([mine[-s], others[-s]] + from_up)
-        from_up = [lax.ppermute(sent, "seq", down)]
-        if s <= near:
-            sent = combine([mine[s], others[s]] + from_down)
-            from_down = [lax.ppermute(sent, "seq", up)]
-    pieces = [mine[0], others[0]] + from_up + from_down
+    per_core = len(outs) // 2
+    everything, low, high = (0, requests), (0, half), (half, requests)
+    names = ["low", "high"] + order
+    span_of = {"low": low, "high": high}
+    both = {}
+    for name, own, other in zip(names, outs[:per_core], outs[per_core:]):
+        span = span_of.get(name, everything)
+        both[name] = [(own, span), (swap(other), span)]
+
+    def passed(name, arrived, way):
+        sent, span = combine(both[name] + arrived)
+        return [(lax.ppermute(sent, "seq", way), span)]
+
+    from_up = passed("low", [], down)
+    from_down = passed("high", [], up)
+    for s in range(far - 1, 0, -1):
+        from_up = passed(-s, from_up, down)
+        from_down = passed(s, from_down, up)
+    pieces = [array for array, _ in both[0] + from_up + from_down]
     values = call(
         finish_kernel,
         values_shape,

time: 121 us -> 124 us (1.025)
  starting transfers between devices: 34.2 us -> 40.7 us
  waiting for transfers between devices: 47.3 us -> 42.9 us
  Pallas kernels: 18.6 us -> 21 us
  blocking collectives: 14.9 us -> 13.6 us
    ppermute x4 -> x3, waiting for transfers between devices: 22.4 us -> 0.1 us  [shards(): queries[-s] = lax.ppermute(queries[1 - s], 'seq', up)]
    ppermute x3, waiting for transfers between devices: 2.49 us -> 15.2 us  [shards(): queries[s] = lax.ppermute(queries[s - 1], 'seq', down)]
    ppermute x7 -> x10, waiting for transfers between devices: 19.4 us -> 25.4 us  [the longest x8 20 us: passed(): return [(lax.ppermute(sent, 'seq', way), span)]]
    ppermute x7 -> x10, starting transfers between devices: 11.4 us -> 15.5 us  [the longest x8 11.6 us: passed(): return [(lax.ppermute(sent, 'seq', way), span)]]
    ppermute x3, starting transfers between devices: 10.4 us -> 13.2 us  [shards(): queries[s] = lax.ppermute(queries[s - 1], 'seq', down)]
    pallas_call x12 -> x13, Pallas kernels: 18.6 us -> 21 us  [call(): pl.pallas_call(kernel, out_shape=out_shape, compiler_params=pltpu.Compile...]
    ppermute x4 -> x3, starting transfers between devices: 1.93 us -> 0.01 us  [shards(): queries[-s] = lax.ppermute(queries[1 - s], 'seq', up)]
    ppermute x16 -> x18, starting transfers between devices: 2.96 us -> 4.42 us  [swap(): return lax.ppermute(x, 'dec', [(0, 1), (1, 0)])]
  transfers between devices with their start and end apart: 31 -> 35, of which waited for: 14 -> 14; matrix products, arithmetic and copies ran while one was open for 0% -> 0% of each run, Pallas kernels for 3% -> 3%
where the time goes in v3:
time: 124 us; the launch traced here: 123 us
  waiting for transfers between devices  42.9 us (35%)
  starting transfers between devices  40.7 us (33%)
  Pallas kernels  21 us (17%)
  blocking collectives  13.6 us (11%)
  local copies, waits for them, and re-layouts  4.96 us (4%)
    pallas_call x13, Pallas kernels, call(): pl.pallas_call(kernel, out_shape=out_shape, compiler_params=pltpu.Compile...  21 us
    ppermute x8, waiting for transfers between devices, passed(): return [(lax.ppermute(sent, 'seq', way), span)]  20 us
    ppermute x3, waiting for transfers between devices, shards(): queries[s] = lax.ppermute(queries[s - 1], 'seq', down)  15.2 us
    all_to_all x1, blocking collectives, shards(): got = lax.all_to_all(values, 'pre', split_axis=0, concat_axis=0, tiled=True)  13.6 us
    ppermute x3, starting transfers between devices, shards(): queries[s] = lax.ppermute(queries[s - 1], 'seq', down)  13.2 us
    ppermute x8, starting transfers between devices, passed(): return [(lax.ppermute(sent, 'seq', way), span)]  11.6 us
    all_to_all x1, starting transfers between devices, shards(): lax.all_to_all(decode_q, 'pre', split_axis=0, concat_axis=0, tiled=True)  7.48 us
    unnamed x14, local copies, waits for them, and re-layouts  4.94 us
  transfers between devices with their start and end apart: 35, of which 14 were waited for; matrix products, arithmetic and copies ran while one was open for 0% of the time, Pallas kernels for 3%

profile of v3, /device:TPU:2, one launch (start us, length us, event | category | flops | bytes accessed | tf_op | source)
XLA Modules:
  0.0 123.3 jit_solution(10478580071324095725)
XLA Ops:
  0.0 7.5 %all-to-all-start = ((bf16[16,16,576]{2,1,0:T(8,128)(2,1)}), bf16[16,16,576]{2,1,0:T(8,128)(2,1)S(1)}, u32[]{:S(2)}, u32[]{:S(2)}) async-start(bf16[16,16,576]{2,1,0:T(8,128)(2,1)} %bitcast.7), calls=%async_computation | async-start | bytes 655360 | tf_op jit(solution)/shard_map/all_to_all | solution.py:362
  7.5 1.2 copy-done
  8.7 1.0 copy-done.2
  9.7 0.8 copy-done.3
  10.5 0.9 shard_map.74.new_ref
  11.4 0.0 copy-start.4
  11.4 0.6 copy-done.4
  12.1 0.7 copy-done.5
  12.7 0.7 copy-done.6
  13.4 1.7 %shard_map.73.plan_ref = s32[16,11]{1,0:T(8,128)S(1)} custom-call(s32[1,16]{1,0:T(1,128)S(1)} %copy-done.4, s32[1,16]{1,0:T(1,128)S(1)} %copy-done.5, s32[1,1,1,128]{3,2,1,0:T(1,128)S(1)} %copy-done.6, s32[1]{0:T(128)} %bitcast.1.split_ref), custom_call_target="tpu_custom_call" | custom-call | tf_op jit(solution)/shard_map/pallas_call | solution.py:313
  15.1 0.4 all-to-all-done.refs_5_
  15.5 5.9 %collective-permute-start.4 = (bf16[16,16,576]{2,1,0:T(8,128)(2,1)S(1)}, bf16[16,16,576]{2,1,0:T(8,128)(2,1)S(1)}, u32[]{:S(2)}, u32[]{:S(2)}) collective-permute-start(bf16[16,16,576]{2,1,0:T(8,128)(2,1)S(1)} %all-to-all-done.refs_5_), channel_id=1, source_target_pairs={{0,14},{2,0},{4,2},{6,4},{8,6},{10,8},{12,10},{14,12},{1,15},{3,1}... | collective-permute-start | bytes 884744 | tf_op jit(solution)/shard_map/ppermute | solution.py:393
  21.4 6.1 %collective-permute-done.4.refs_6_ = bf16[16,16,576]{2,1,0:T(8,128)(2,1)S(1)} collective-permute-done((bf16[16,16,576]{2,1,0:T(8,128)(2,1)S(1)}, bf16[16,16,576]{2,1,0:T(8,128)(2,1)S(1)}, u32[]{:S(2)}, u32[]{:S(2)}) %collective-permute-start.4) | collective-permute-done | bytes 294944 | tf_op jit(solution)/shard_map/ppermute | solution.py:393
  27.4 3.7 %collective-permute-start.5 = (bf16[16,16,576]{2,1,0:T(8,128)(2,1)S(1)}, bf16[16,16,576]{2,1,0:T(8,128)(2,1)S(1)}, u32[]{:S(2)}, u32[]{:S(2)}) collective-permute-start(bf16[16,16,576]{2,1,0:T(8,128)(2,1)S(1)} %collective-permute-done.4.refs_6_), channel_id=1, source_target_pairs={{0,14},{2,0},{4,2},{6,4},{8,6},{10,8},{12,10},{14,12},{1,15},{3,1}... | collective-permute-start | bytes 884744 | tf_op jit(solution)/shard_map/ppermute | solution.py:393
  31.1 5.1 %collective-permute-done.5.refs_7_ = bf16[16,16,576]{2,1,0:T(8,128)(2,1)S(1)} collective-permute-done((bf16[16,16,576]{2,1,0:T(8,128)(2,1)S(1)}, bf16[16,16,576]{2,1,0:T(8,128)(2,1)S(1)}, u32[]{:S(2)}, u32[]{:S(2)}) %collective-permute-start.5) | collective-permute-done | bytes 294944 | tf_op jit(solution)/shard_map/ppermute | solution.py:393
  36.3 3.7 %collective-permute-start.6 = (bf16[16,16,576]{2,1,0:T(8,128)(2,1)S(1)}, bf16[16,16,576]{2,1,0:T(8,128)(2,1)S(1)}, u32[]{:S(2)}, u32[]{:S(2)}) collective-permute-start(bf16[16,16,576]{2,1,0:T(8,128)(2,1)S(1)} %collective-permute-done.5.refs_7_), channel_id=1, source_target_pairs={{0,14},{2,0},{4,2},{6,4},{8,6},{10,8},{12,10},{14,12},{1,15},{3,1}... | collective-permute-start | bytes 884744 | tf_op jit(solution)/shard_map/ppermute | solution.py:393
  40.0 0.5 collective-permute-start.13
  40.5 0.1 collective-permute-start.14
  40.6 4.0 %collective-permute-done.6.refs_8_ = bf16[16,16,576]{2,1,0:T(8,128)(2,1)S(1)} collective-permute-done((bf16[16,16,576]{2,1,0:T(8,128)(2,1)S(1)}, bf16[16,16,576]{2,1,0:T(8,128)(2,1)S(1)}, u32[]{:S(2)}, u32[]{:S(2)}) %collective-permute-start.6) | collective-permute-done | bytes 294944 | tf_op jit(solution)/shard_map/ppermute | solution.py:393
  44.6 3.8 %collective-permute-start.7 = (bf16[8,16,576]{2,1,0:T(8,128)(2,1)S(1)}, bf16[8,16,576]{2,1,0:T(8,128)(2,1)S(1)}, u32[]{:S(2)}, u32[]{:S(2)}) collective-permute-start(bf16[8,16,576]{2,1,0:T(8,128)(2,1)S(1)} %slice.9), channel_id=1, source_target_pairs={{0,14},{2,0},{4,2},{6,4},{8,6},{10,8},{12,10},{14,12},{1,15},{3,1}... | collective-permute-start | bytes 442376 | tf_op jit(solution)/shard_map/ppermute | solution.py:396
  48.4 0.1 collective-permute-done.2.refs_2_
  48.5 0.1 collective-permute-start.3
  48.6 0.1 collective-permute-start.10
  48.7 0.5 collective-permute-start.11
  49.2 2.0 %collective-permute-done.7.refs_1_ = bf16[8,16,576]{2,1,0:T(8,128)(2,1)S(1)} collective-permute-done((bf16[8,16,576]{2,1,0:T(8,128)(2,1)S(1)}, bf16[8,16,576]{2,1,0:T(8,128)(2,1)S(1)}, u32[]{:S(2)}, u32[]{:S(2)}) %collective-permute-start.7) | collective-permute-done | bytes 147488 | tf_op jit(solution)/shard_map/ppermute | solution.py:396
  51.2 0.5 collective-permute-start.15
  51.7 3.4 %collective-permute-done.3.refs_0_ = bf16[8,16,576]{2,1,0:T(8,128)(2,1)S(1)} collective-permute-done((bf16[8,16,576]{2,1,0:T(8,128)(2,1)S(1)}, bf16[8,16,576]{2,1,0:T(8,128)(2,1)S(1)}, u32[]{:S(2)}, u32[]{:S(2)}) %collective-permute-start.3) | collective-permute-done | bytes 147488 | tf_op jit(solution)/shard_map/ppermute | solution.py:395
  55.1 0.0 collective-permute-start.16
  55.1 0.5 collective-permute-start.8
  55.6 1.3 %collective-permute-done.8.refs_9_ = bf16[8,16,576]{2,1,0:T(8,128)(2,1)S(1)} collective-permute-done((bf16[8,16,576]{2,1,0:T(8,128)(2,1)S(1)}, bf16[8,16,576]{2,1,0:T(8,128)(2,1)S(1)}, u32[]{:S(2)}, u32[]{:S(2)}) %collective-permute-start.8) | collective-permute-done | bytes 147488 | tf_op jit(solution)/shard_map/ppermute | solution.py:359
  57.0 0.0 copy-start.1
  57.0 14.7 %shard_map.75 = (bf16[9,16,512]{2,1,0:T(8,128)(2,1)S(1)}, bf16[9,16,512]{2,1,0:T(8,128)(2,1)S(1)}, bf16[17,16,512]{2,1,0:T(8,128)(2,1)S(1)}, bf16[17,16,512]{2,1...) custom-call(s32[16,11]{1,0:T(8,128)S(1)} %shard_map.73.plan_ref, ...), custom_call_target="tpu_custom_call" | custom-call | tf_op jit(solution)/shard_map/pallas_call | solution.py:313
  71.8 0.2 collective-permute-start.21
  72.0 0.4 collective-permute-start.29
  72.4 0.1 collective-permute-start.20
  72.5 0.4 collective-permute-start.28
  72.9 0.3 collective-permute-done.21.refs_1_
  73.2 0.1 shard_map.76
  73.4 0.1 collective-permute-start.22
  73.5 0.1 shard_map.80
  73.6 2.1 %collective-permute-start.30 = (bf16[9,16,512]{2,1,0:T(8,128)(2,1)S(1)}, bf16[9,16,512]{2,1,0:T(8,128)(2,1)S(1)}, u32[]{:S(2)}, u32[]{:S(2)}) collective-permute-start(bf16[9,16,512]{2,1,0:T(8,128)(2,1)S(1)} %shard_map.80), channel_id=1, source_target_pairs={{0,2},{2,4},{4,6},{6,8},{8,10},{10,12},{12,14},{14,0},{1,3},{3,5},... | collective-permute-start | bytes 442376 | tf_op jit(solution)/shard_map/ppermute | solution.py:437
  75.7 0.5 collective-permute-start.27
  76.2 3.1 %collective-permute-done.22.refs_2_ = bf16[9,16,512]{2,1,0:T(8,128)(2,1)S(1)} collective-permute-done((bf16[9,16,512]{2,1,0:T(8,128)(2,1)S(1)}, bf16[9,16,512]{2,1,0:T(8,128)(2,1)S(1)}, u32[]{:S(2)}, u32[]{:S(2)}) %collective-permute-start.22) | collective-permute-done | bytes 147488 | tf_op jit(solution)/shard_map/ppermute | solution.py:437
  79.3 0.2 shard_map.77
  79.6 1.6 %collective-permute-start.23 = (bf16[17,16,512]{2,1,0:T(8,128)(2,1)S(1)}, bf16[17,16,512]{2,1,0:T(8,128)(2,1)S(1)}, u32[]{:S(2)}, u32[]{:S(2)}) collective-permute-start(bf16[17,16,512]{2,1,0:T(8,128)(2,1)S(1)} %shard_map.77), channel_id=1, source_target_pairs={{0,14},{2,0},{4,2},{6,4},{8,6},{10,8},{12,10},{14,12},{1,15},{3,1}... | collective-permute-start | bytes 835592 | tf_op jit(solution)/shard_map/ppermute | solution.py:437
  81.1 0.2 shard_map.81
  81.4 0.8 collective-permute-start.31
  82.2 0.5 collective-permute-start.26
  82.7 4.8 %collective-permute-done.23.refs_2_ = bf16[17,16,512]{2,1,0:T(8,128)(2,1)S(1)} collective-permute-done((bf16[17,16,512]{2,1,0:T(8,128)(2,1)S(1)}, bf16[17,16,512]{2,1,0:T(8,128)(2,1)S(1)}, u32[]{:S(2)}, u32[]{:S(2)}) %collective-permute-start.23) | collective-permute-done | bytes 278560 | tf_op jit(solution)/shard_map/ppermute | solution.py:437
  87.5 0.2 shard_map.78
  87.8 3.1 %collective-permute-start.24 = (bf16[17,16,512]{2,1,0:T(8,128)(2,1)S(1)}, bf16[17,16,512]{2,1,0:T(8,128)(2,1)S(1)}, u32[]{:S(2)}, u32[]{:S(2)}) collective-permute-start(bf16[17,16,512]{2,1,0:T(8,128)(2,1)S(1)} %shard_map.78), channel_id=1, source_target_pairs={{0,14},{2,0},{4,2},{6,4},{8,6},{10,8},{12,10},{14,12},{1,15},{3,1}... | collective-permute-start | bytes 835592 | tf_op jit(solution)/shard_map/ppermute | solution.py:437
  90.9 0.2 shard_map.82
  91.1 0.1 collective-permute-start.32
  91.2 0.1 collective-permute-start.17
  91.3 4.4 %collective-permute-done.24.refs_2_ = bf16[17,16,512]{2,1,0:T(8,128)(2,1)S(1)} collective-permute-done((bf16[17,16,512]{2,1,0:T(8,128)(2,1)S(1)}, bf16[17,16,512]{2,1,0:T(8,128)(2,1)S(1)}, u32[]{:S(2)}, u32[]{:S(2)}) %collective-permute-start.24) | collective-permute-done | bytes 278560 | tf_op jit(solution)/shard_map/ppermute | solution.py:437
  95.7 0.2 shard_map.79
  95.9 3.8 %collective-permute-start.25 = (bf16[17,16,512]{2,1,0:T(8,128)(2,1)S(1)}, bf16[17,16,512]{2,1,0:T(8,128)(2,1)S(1)}, u32[]{:S(2)}, u32[]{:S(2)}) collective-permute-start(bf16[17,16,512]{2,1,0:T(8,128)(2,1)S(1)} %shard_map.79), channel_id=1, source_target_pairs={{0,14},{2,0},{4,2},{6,4},{8,6},{10,8},{12,10},{14,12},{1,15},{3,1}... | collective-permute-start | bytes 835592 | tf_op jit(solution)/shard_map/ppermute | solution.py:437
  99.7 0.2 shard_map.83
  99.9 0.1 collective-permute-start.33
  100.0 3.7 %collective-permute-done.25.refs_2_ = bf16[17,16,512]{2,1,0:T(8,128)(2,1)S(1)} collective-permute-done((bf16[17,16,512]{2,1,0:T(8,128)(2,1)S(1)}, bf16[17,16,512]{2,1,0:T(8,128)(2,1)S(1)}, u32[]{:S(2)}, u32[]{:S(2)}) %collective-permute-start.25) | collective-permute-done | bytes 278560 | tf_op jit(solution)/shard_map/ppermute | solution.py:437
  103.8 4.0 %collective-permute-done.33.refs_3_ = bf16[17,16,512]{2,1,0:T(8,128)(2,1)S(1)} collective-permute-done((bf16[17,16,512]{2,1,0:T(8,128)(2,1)S(1)}, bf16[17,16,512]{2,1,0:T(8,128)(2,1)S(1)}, u32[]{:S(2)}, u32[]{:S(2)}) %collective-permute-start.33) | collective-permute-done | bytes 278560 | tf_op jit(solution)/shard_map/ppermute | solution.py:437
  107.8 0.9 shard_map.84
  108.7 13.6 %all_to_all.10.cache_ref = f32[16,2,1152]{2,1,0:T(2,128)S(1)} all-to-all(f32[16,2,1152]{2,1,0:T(2,128)S(1)} %shard_map.84), channel_id=1, replica_groups=mesh['pre'=16,'seq'=8,'dec'=2] {'pre'}, dimensions={0} | all-to-all | bytes 294912 | tf_op jit(solution)/shard_map/all_to_all | solution.py:453
  122.3 1.0 shard_map.85
  (36 shorter events, 0.1 us)
Async XLA Ops:
  0.0 15.5 %all-to-all-start = ((bf16[16,16,576]{2,1,0:T(8,128)(2,1)}), bf16[16,16,576]{2,1,0:T(8,128)(2,1)S(1)}, u32[]{:S(2)}, u32[]{:S(2)}) async-start(bf16[16,16,576]{2,1,0:T(8,128)(2,1)} %bitcast.7), calls=%async_computation | async-start | bytes 655360 | tf_op jit(solution)/shard_map/all_to_all | solution.py:362
  7.5 1.2 copy-start
  8.7 1.0 copy-start.2
  9.7 0.8 copy-start.3
  11.4 0.7 copy-start.4
  12.1 0.7 copy-start.5
  12.7 0.7 copy-start.6
  15.5 11.9 %collective-permute-start.4 = (bf16[16,16,576]{2,1,0:T(8,128)(2,1)S(1)}, bf16[16,16,576]{2,1,0:T(8,128)(2,1)S(1)}, u32[]{:S(2)}, u32[]{:S(2)}) collective-permute-start(bf16[16,16,576]{2,1,0:T(8,128)(2,1)S(1)} %all-to-all-done.refs_5_), channel_id=1, source_target_pairs={{0,14},{2,0},{4,2},{6,4},{8,6},{10,8},{12,10},{14,12},{1,15},{3,1}... | collective-permute-start | bytes 884744 | tf_op jit(solution)/shard_map/ppermute | solution.py:393
  21.4 9.8 %collective-permute-start = (bf16[16,16,576]{2,1,0:T(8,128)(2,1)S(1)}, bf16[16,16,576]{2,1,0:T(8,128)(2,1)S(1)}, u32[]{:S(2)}, u32[]{:S(2)}) collective-permute-start(bf16[16,16,576]{2,1,0:T(8,128)(2,1)S(1)} %all-to-all-done.refs_5_), channel_id=1, source_target_pairs={{0,2},{2,4},{4,6},{6,8},{8,10},{10,12},{12,14},{14,0},{1,3},{3,5},... | collective-permute-start | bytes 884744 | tf_op jit(solution)/shard_map/ppermute | solution.py:392
  27.4 8.8 %collective-permute-start.5 = (bf16[16,16,576]{2,1,0:T(8,128)(2,1)S(1)}, bf16[16,16,576]{2,1,0:T(8,128)(2,1)S(1)}, u32[]{:S(2)}, u32[]{:S(2)}) collective-permute-start(bf16[16,16,576]{2,1,0:T(8,128)(2,1)S(1)} %collective-permute-done.4.refs_6_), channel_id=1, source_target_pairs={{0,14},{2,0},{4,2},{6,4},{8,6},{10,8},{12,10},{14,12},{1,15},{3,1}... | collective-permute-start | bytes 884744 | tf_op jit(solution)/shard_map/ppermute | solution.py:393
  31.1 8.8 %collective-permute-start.1 = (bf16[16,16,576]{2,1,0:T(8,128)(2,1)S(1)}, bf16[16,16,576]{2,1,0:T(8,128)(2,1)S(1)}, u32[]{:S(2)}, u32[]{:S(2)}) collective-permute-start(bf16[16,16,576]{2,1,0:T(8,128)(2,1)S(1)} %collective-permute-done.refs_4_), channel_id=1, source_target_pairs={{0,2},{2,4},{4,6},{6,8},{8,10},{10,12},{12,14},{14,0},{1,3},{3,5},... | collective-permute-start | bytes 884744 | tf_op jit(solution)/shard_map/ppermute | solution.py:392
  36.3 8.3 %collective-permute-start.6 = (bf16[16,16,576]{2,1,0:T(8,128)(2,1)S(1)}, bf16[16,16,576]{2,1,0:T(8,128)(2,1)S(1)}, u32[]{:S(2)}, u32[]{:S(2)}) collective-permute-start(bf16[16,16,576]{2,1,0:T(8,128)(2,1)S(1)} %collective-permute-done.5.refs_7_), channel_id=1, source_target_pairs={{0,14},{2,0},{4,2},{6,4},{8,6},{10,8},{12,10},{14,12},{1,15},{3,1}... | collective-permute-start | bytes 884744 | tf_op jit(solution)/shard_map/ppermute | solution.py:393
  40.0 8.5 %collective-permute-start.2 = (bf16[16,16,576]{2,1,0:T(8,128)(2,1)S(1)}, bf16[16,16,576]{2,1,0:T(8,128)(2,1)S(1)}, u32[]{:S(2)}, u32[]{:S(2)}) collective-permute-start(bf16[16,16,576]{2,1,0:T(8,128)(2,1)S(1)} %collective-permute-done.1.refs_3_), channel_id=1, source_target_pairs={{0,2},{2,4},{4,6},{6,8},{8,10},{10,12},{12,14},{14,0},{1,3},{3,5},... | collective-permute-start | bytes 884744 | tf_op jit(solution)/shard_map/ppermute | solution.py:392
  40.0 8.6 %collective-permute-start.12 = (bf16[16,16,576]{2,1,0:T(8,128)(2,1)S(1)}, bf16[16,16,576]{2,1,0:T(8,128)(2,1)S(1)}, u32[]{:S(2)}, u32[]{:S(2)}) collective-permute-start(bf16[16,16,576]{2,1,0:T(8,128)(2,1)S(1)} %collective-permute-done.refs_4_), channel_id=1, source_target_pairs={{0,1},{1,0},{2,3},{3,2},{4,5},{5,4},{6,7},{7,6},{8,9},{9,8},{10,11... | collective-permute-start | bytes 884744 | tf_op jit(solution)/shard_map/ppermute | solution.py:359
  40.0 8.7 %collective-permute-start.13 = (bf16[16,16,576]{2,1,0:T(8,128)(2,1)S(1)}, bf16[16,16,576]{2,1,0:T(8,128)(2,1)S(1)}, u32[]{:S(2)}, u32[]{:S(2)}) collective-permute-start(bf16[16,16,576]{2,1,0:T(8,128)(2,1)S(1)} %all-to-all-done.refs_5_), channel_id=1, source_target_pairs={{0,1},{1,0},{2,3},{3,2},{4,5},{5,4},{6,7},{7,6},{8,9},{9,8},{10,11... | collective-permute-start | bytes 884744 | tf_op jit(solution)/shard_map/ppermute | solution.py:359
  40.5 10.8 %collective-permute-start.14 = (bf16[16,16,576]{2,1,0:T(8,128)(2,1)S(1)}, bf16[16,16,576]{2,1,0:T(8,128)(2,1)S(1)}, u32[]{:S(2)}, u32[]{:S(2)}) collective-permute-start(bf16[16,16,576]{2,1,0:T(8,128)(2,1)S(1)} %collective-permute-done.4.refs_6_), channel_id=1, source_target_pairs={{0,1},{1,0},{2,3},{3,2},{4,5},{5,4},{6,7},{7,6},{8,9},{9,8},{10,11... | collective-permute-start | bytes 884744 | tf_op jit(solution)/shard_map/ppermute | solution.py:359
  44.6 6.7 %collective-permute-start.7 = (bf16[8,16,576]{2,1,0:T(8,128)(2,1)S(1)}, bf16[8,16,576]{2,1,0:T(8,128)(2,1)S(1)}, u32[]{:S(2)}, u32[]{:S(2)}) collective-permute-start(bf16[8,16,576]{2,1,0:T(8,128)(2,1)S(1)} %slice.9), channel_id=1, source_target_pairs={{0,14},{2,0},{4,2},{6,4},{8,6},{10,8},{12,10},{14,12},{1,15},{3,1}... | collective-permute-start | bytes 442376 | tf_op jit(solution)/shard_map/ppermute | solution.py:396
  48.5 6.6 %collective-permute-start.3 = (bf16[8,16,576]{2,1,0:T(8,128)(2,1)S(1)}, bf16[8,16,576]{2,1,0:T(8,128)(2,1)S(1)}, u32[]{:S(2)}, u32[]{:S(2)}) collective-permute-start(bf16[8,16,576]{2,1,0:T(8,128)(2,1)S(1)} %slice.8), channel_id=1, source_target_pairs={{0,2},{2,4},{4,6},{6,8},{8,10},{10,12},{12,14},{14,0},{1,3},{3,5},... | collective-permute-start | bytes 442376 | tf_op jit(solution)/shard_map/ppermute | solution.py:395
  48.6 8.4 %collective-permute-start.10 = (bf16[16,16,576]{2,1,0:T(8,128)(2,1)S(1)}, bf16[16,16,576]{2,1,0:T(8,128)(2,1)S(1)}, u32[]{:S(2)}, u32[]{:S(2)}) collective-permute-start(bf16[16,16,576]{2,1,0:T(8,128)(2,1)S(1)} %collective-permute-done.2.refs_2_), channel_id=1, source_target_pairs={{0,1},{1,0},{2,3},{3,2},{4,5},{5,4},{6,7},{7,6},{8,9},{9,8},{10,11... | collective-permute-start | bytes 884744 | tf_op jit(solution)/shard_map/ppermute | solution.py:359
  48.7 8.3 %collective-permute-start.11 = (bf16[16,16,576]{2,1,0:T(8,128)(2,1)S(1)}, bf16[16,16,576]{2,1,0:T(8,128)(2,1)S(1)}, u32[]{:S(2)}, u32[]{:S(2)}) collective-permute-start(bf16[16,16,576]{2,1,0:T(8,128)(2,1)S(1)} %collective-permute-done.1.refs_3_), channel_id=1, source_target_pairs={{0,1},{1,0},{2,3},{3,2},{4,5},{5,4},{6,7},{7,6},{8,9},{9,8},{10,11... | collective-permute-start | bytes 884744 | tf_op jit(solution)/shard_map/ppermute | solution.py:359
  51.2 3.9 %collective-permute-start.9 = (bf16[8,16,576]{2,1,0:T(8,128)(2,1)S(1)}, bf16[8,16,576]{2,1,0:T(8,128)(2,1)S(1)}, u32[]{:S(2)}, u32[]{:S(2)}) collective-permute-start(bf16[8,16,576]{2,1,0:T(8,128)(2,1)S(1)} %collective-permute-done.7.refs_1_), channel_id=1, source_target_pairs={{0,1},{1,0},{2,3},{3,2},{4,5},{5,4},{6,7},{7,6},{8,9},{9,8},{10,11... | collective-permute-start | bytes 442376 | tf_op jit(solution)/shard_map/ppermute | solution.py:359
  51.2 5.8 %collective-permute-start.15 = (bf16[16,16,576]{2,1,0:T(8,128)(2,1)S(1)}, bf16[16,16,576]{2,1,0:T(8,128)(2,1)S(1)}, u32[]{:S(2)}, u32[]{:S(2)}) collective-permute-start(bf16[16,16,576]{2,1,0:T(8,128)(2,1)S(1)} %collective-permute-done.5.refs_7_), channel_id=1, source_target_pairs={{0,1},{1,0},{2,3},{3,2},{4,5},{5,4},{6,7},{7,6},{8,9},{9,8},{10,11... | collective-permute-start | bytes 884744 | tf_op jit(solution)/shard_map/ppermute | solution.py:359
  55.1 1.9 %collective-permute-start.16 = (bf16[16,16,576]{2,1,0:T(8,128)(2,1)S(1)}, bf16[16,16,576]{2,1,0:T(8,128)(2,1)S(1)}, u32[]{:S(2)}, u32[]{:S(2)}) collective-permute-start(bf16[16,16,576]{2,1,0:T(8,128)(2,1)S(1)} %collective-permute-done.6.refs_8_), channel_id=1, source_target_pairs={{0,1},{1,0},{2,3},{3,2},{4,5},{5,4},{6,7},{7,6},{8,9},{9,8},{10,11... | collective-permute-start | bytes 884744 | tf_op jit(solution)/shard_map/ppermute | solution.py:359
  55.1 1.9 %collective-permute-start.8 = (bf16[8,16,576]{2,1,0:T(8,128)(2,1)S(1)}, bf16[8,16,576]{2,1,0:T(8,128)(2,1)S(1)}, u32[]{:S(2)}, u32[]{:S(2)}) collective-permute-start(bf16[8,16,576]{2,1,0:T(8,128)(2,1)S(1)} %collective-permute-done.3.refs_0_), channel_id=1, source_target_pairs={{0,1},{1,0},{2,3},{3,2},{4,5},{5,4},{6,7},{7,6},{8,9},{9,8},{10,11... | collective-permute-start | bytes 442376 | tf_op jit(solution)/shard_map/ppermute | solution.py:359
  57.0 50.8 %copy-start.1 = (bf16[8,512,128]{2,1,0:T(8,128)(2,1)S(1)}, bf16[8,512,128]{2,1,0:T(8,128)(2,1)}, u32[]{:S(2)}) copy-start(bf16[8,512,128]{2,1,0:T(8,128)(2,1)} %refs_4_.1) | copy-start | bytes 3145732
  71.8 1.5 %collective-permute-start.21 = (bf16[9,16,512]{2,1,0:T(8,128)(2,1)S(1)}, bf16[9,16,512]{2,1,0:T(8,128)(2,1)S(1)}, u32[]{:S(2)}, u32[]{:S(2)}) collective-permute-start(bf16[9,16,512]{2,1,0:T(8,128)(2,1)S(1)} %get-tuple-element.51), channel_id=1, source_target_pairs={{0,1},{1,0},{2,3},{3,2},{4,5},{5,4},{6,7},{7,6},{8,9},{9,8},{10,11... | collective-permute-start | bytes 442376 | tf_op jit(solution)/shard_map/ppermute | solution.py:359
  72.0 1.5 %collective-permute-start.29 = (bf16[9,16,512]{2,1,0:T(8,128)(2,1)S(1)}, bf16[9,16,512]{2,1,0:T(8,128)(2,1)S(1)}, u32[]{:S(2)}, u32[]{:S(2)}) collective-permute-start(bf16[9,16,512]{2,1,0:T(8,128)(2,1)S(1)} %get-tuple-element.59), channel_id=1, source_target_pairs={{0,1},{1,0},{2,3},{3,2},{4,5},{5,4},{6,7},{7,6},{8,9},{9,8},{10,11... | collective-permute-start | bytes 442376 | tf_op jit(solution)/shard_map/ppermute | solution.py:359
  72.4 3.3 %collective-permute-start.20 = (bf16[17,16,512]{2,1,0:T(8,128)(2,1)S(1)}, bf16[17,16,512]{2,1,0:T(8,128)(2,1)S(1)}, u32[]{:S(2)}, u32[]{:S(2)}) collective-permute-start(bf16[17,16,512]{2,1,0:T(8,128)(2,1)S(1)} %get-tuple-element.49), channel_id=1, source_target_pairs={{0,1},{1,0},{2,3},{3,2},{4,5},{5,4},{6,7},{7,6},{8,9},{9,8},{10,11... | collective-permute-start | bytes 835592 | tf_op jit(solution)/shard_map/ppermute | solution.py:359
  72.5 8.6 %collective-permute-start.28 = (bf16[17,16,512]{2,1,0:T(8,128)(2,1)S(1)}, bf16[17,16,512]{2,1,0:T(8,128)(2,1)S(1)}, u32[]{:S(2)}, u32[]{:S(2)}) collective-permute-start(bf16[17,16,512]{2,1,0:T(8,128)(2,1)S(1)} %get-tuple-element.57), channel_id=1, source_target_pairs={{0,1},{1,0},{2,3},{3,2},{4,5},{5,4},{6,7},{7,6},{8,9},{9,8},{10,11... | collective-permute-start | bytes 835592 | tf_op jit(solution)/shard_map/ppermute | solution.py:359
  73.4 6.0 %collective-permute-start.22 = (bf16[9,16,512]{2,1,0:T(8,128)(2,1)S(1)}, bf16[9,16,512]{2,1,0:T(8,128)(2,1)S(1)}, u32[]{:S(2)}, u32[]{:S(2)}) collective-permute-start(bf16[9,16,512]{2,1,0:T(8,128)(2,1)S(1)} %shard_map.76), channel_id=1, source_target_pairs={{0,14},{2,0},{4,2},{6,4},{8,6},{10,8},{12,10},{14,12},{1,15},{3,1}... | collective-permute-start | bytes 442376 | tf_op jit(solution)/shard_map/ppermute | solution.py:437
  73.6 7.5 %collective-permute-start.30 = (bf16[9,16,512]{2,1,0:T(8,128)(2,1)S(1)}, bf16[9,16,512]{2,1,0:T(8,128)(2,1)S(1)}, u32[]{:S(2)}, u32[]{:S(2)}) collective-permute-start(bf16[9,16,512]{2,1,0:T(8,128)(2,1)S(1)} %shard_map.80), channel_id=1, source_target_pairs={{0,2},{2,4},{4,6},{6,8},{8,10},{10,12},{12,14},{14,0},{1,3},{3,5},... | collective-permute-start | bytes 442376 | tf_op jit(solution)/shard_map/ppermute | solution.py:437
  75.7 6.5 %collective-permute-start.19 = (bf16[17,16,512]{2,1,0:T(8,128)(2,1)S(1)}, bf16[17,16,512]{2,1,0:T(8,128)(2,1)S(1)}, u32[]{:S(2)}, u32[]{:S(2)}) collective-permute-start(bf16[17,16,512]{2,1,0:T(8,128)(2,1)S(1)} %get-tuple-element.47), channel_id=1, source_target_pairs={{0,1},{1,0},{2,3},{3,2},{4,5},{5,4},{6,7},{7,6},{8,9},{9,8},{10,11... | collective-permute-start | bytes 835592 | tf_op jit(solution)/shard_map/ppermute | solution.py:359
  75.7 15.2 %collective-permute-start.27 = (bf16[17,16,512]{2,1,0:T(8,128)(2,1)S(1)}, bf16[17,16,512]{2,1,0:T(8,128)(2,1)S(1)}, u32[]{:S(2)}, u32[]{:S(2)}) collective-permute-start(bf16[17,16,512]{2,1,0:T(8,128)(2,1)S(1)} %get-tuple-element.55), channel_id=1, source_target_pairs={{0,1},{1,0},{2,3},{3,2},{4,5},{5,4},{6,7},{7,6},{8,9},{9,8},{10,11... | collective-permute-start | bytes 835592 | tf_op jit(solution)/shard_map/ppermute | solution.py:359
  79.6 8.0 %collective-permute-start.23 = (bf16[17,16,512]{2,1,0:T(8,128)(2,1)S(1)}, bf16[17,16,512]{2,1,0:T(8,128)(2,1)S(1)}, u32[]{:S(2)}, u32[]{:S(2)}) collective-permute-start(bf16[17,16,512]{2,1,0:T(8,128)(2,1)S(1)} %shard_map.77), channel_id=1, source_target_pairs={{0,14},{2,0},{4,2},{6,4},{8,6},{10,8},{12,10},{14,12},{1,15},{3,1}... | collective-permute-start | bytes 835592 | tf_op jit(solution)/shard_map/ppermute | solution.py:437
  81.4 9.5 %collective-permute-start.31 = (bf16[17,16,512]{2,1,0:T(8,128)(2,1)S(1)}, bf16[17,16,512]{2,1,0:T(8,128)(2,1)S(1)}, u32[]{:S(2)}, u32[]{:S(2)}) collective-permute-start(bf16[17,16,512]{2,1,0:T(8,128)(2,1)S(1)} %shard_map.81), channel_id=1, source_target_pairs={{0,2},{2,4},{4,6},{6,8},{8,10},{10,12},{12,14},{14,0},{1,3},{3,5},... | collective-permute-start | bytes 835592 | tf_op jit(solution)/shard_map/ppermute | solution.py:437
  82.2 9.1 %collective-permute-start.18 = (bf16[17,16,512]{2,1,0:T(8,128)(2,1)S(1)}, bf16[17,16,512]{2,1,0:T(8,128)(2,1)S(1)}, u32[]{:S(2)}, u32[]{:S(2)}) collective-permute-start(bf16[17,16,512]{2,1,0:T(8,128)(2,1)S(1)} %get-tuple-element.45), channel_id=1, source_target_pairs={{0,1},{1,0},{2,3},{3,2},{4,5},{5,4},{6,7},{7,6},{8,9},{9,8},{10,11... | collective-permute-start | bytes 835592 | tf_op jit(solution)/shard_map/ppermute | solution.py:359
  82.2 17.5 %collective-permute-start.26 = (bf16[17,16,512]{2,1,0:T(8,128)(2,1)S(1)}, bf16[17,16,512]{2,1,0:T(8,128)(2,1)S(1)}, u32[]{:S(2)}, u32[]{:S(2)}) collective-permute-start(bf16[17,16,512]{2,1,0:T(8,128)(2,1)S(1)} %get-tuple-element.53), channel_id=1, source_target_pairs={{0,1},{1,0},{2,3},{3,2},{4,5},{5,4},{6,7},{7,6},{8,9},{9,8},{10,11... | collective-permute-start | bytes 835592 | tf_op jit(solution)/shard_map/ppermute | solution.py:359
  87.8 7.9 %collective-permute-start.24 = (bf16[17,16,512]{2,1,0:T(8,128)(2,1)S(1)}, bf16[17,16,512]{2,1,0:T(8,128)(2,1)S(1)}, u32[]{:S(2)}, u32[]{:S(2)}) collective-permute-start(bf16[17,16,512]{2,1,0:T(8,128)(2,1)S(1)} %shard_map.78), channel_id=1, source_target_pairs={{0,14},{2,0},{4,2},{6,4},{8,6},{10,8},{12,10},{14,12},{1,15},{3,1}... | collective-permute-start | bytes 835592 | tf_op jit(solution)/shard_map/ppermute | solution.py:437
  91.1 8.6 %collective-permute-start.32 = (bf16[17,16,512]{2,1,0:T(8,128)(2,1)S(1)}, bf16[17,16,512]{2,1,0:T(8,128)(2,1)S(1)}, u32[]{:S(2)}, u32[]{:S(2)}) collective-permute-start(bf16[17,16,512]{2,1,0:T(8,128)(2,1)S(1)} %shard_map.82), channel_id=1, source_target_pairs={{0,2},{2,4},{4,6},{6,8},{8,10},{10,12},{12,14},{14,0},{1,3},{3,5},... | collective-permute-start | bytes 835592 | tf_op jit(solution)/shard_map/ppermute | solution.py:437
  91.2 8.8 %collective-permute-start.17 = (bf16[17,16,512]{2,1,0:T(8,128)(2,1)S(1)}, bf16[17,16,512]{2,1,0:T(8,128)(2,1)S(1)}, u32[]{:S(2)}, u32[]{:S(2)}) collective-permute-start(bf16[17,16,512]{2,1,0:T(8,128)(2,1)S(1)} %get-tuple-element.43), channel_id=1, source_target_pairs={{0,1},{1,0},{2,3},{3,2},{4,5},{5,4},{6,7},{7,6},{8,9},{9,8},{10,11... | collective-permute-start | bytes 835592 | tf_op jit(solution)/shard_map/ppermute | solution.py:359
  95.9 7.8 %collective-permute-start.25 = (bf16[17,16,512]{2,1,0:T(8,128)(2,1)S(1)}, bf16[17,16,512]{2,1,0:T(8,128)(2,1)S(1)}, u32[]{:S(2)}, u32[]{:S(2)}) collective-permute-start(bf16[17,16,512]{2,1,0:T(8,128)(2,1)S(1)} %shard_map.79), channel_id=1, source_target_pairs={{0,14},{2,0},{4,2},{6,4},{8,6},{10,8},{12,10},{14,12},{1,15},{3,1}... | collective-permute-start | bytes 835592 | tf_op jit(solution)/shard_map/ppermute | solution.py:437
  99.9 7.8 %collective-permute-start.33 = (bf16[17,16,512]{2,1,0:T(8,128)(2,1)S(1)}, bf16[17,16,512]{2,1,0:T(8,128)(2,1)S(1)}, u32[]{:S(2)}, u32[]{:S(2)}) collective-permute-start(bf16[17,16,512]{2,1,0:T(8,128)(2,1)S(1)} %shard_map.83), channel_id=1, source_target_pairs={{0,2},{2,4},{4,6},{6,8},{8,10},{10,12},{12,14},{14,0},{1,3},{3,5},... | collective-permute-start | bytes 835592 | tf_op jit(solution)/shard_map/ppermute | solution.py:437

commit v4 on v2

--- a/solution.py
+++ b/solution.py
@@ -164,8 +164,12 @@
         write_stat(ref, stat_ref[n * rows : (n + 1) * rows, :])
 
 
-def weights_of(refs):
-    stats = [read_stat(ref) for ref in refs]
+def weights_of(refs, spans):
+    stats = []
+    for ref, (first, last) in zip(refs, spans):
+        stat = read_stat(ref)
+        lane = lax.broadcasted_iota(jnp.int32, stat.shape, 1)
+        stats.append(jnp.where((lane >= first) & (lane < last), stat, EMPTY))
     top = functools.reduce(jnp.maximum, stats)
     parts = [jnp.exp2(stat - top) for stat in stats]
     total = functools.reduce(jnp.add, parts)
@@ -173,20 +177,22 @@
     return [part * share for part in parts], top + jnp.log2(total)
 
 
-def combined(refs, weights, who):
+def combined(refs, spans, weights, who):
     out = None
-    for ref, weight in zip(refs, weights):
-        part = ref[who].astype(F32) * weight[:, who : who + 1]
-        out = part if out is None else out + part
+    for ref, (first, last), weight in zip(refs, spans, weights):
+        if first <= who < last:
+            part = ref[who - first].astype(F32) * weight[:, who : who + 1]
+            out = part if out is None else out + part
     return out
 
 
-def combine_kernel(*refs):
-    *pieces, out_ref = refs
-    weights, stat = weights_of(pieces)
-    write_stat(out_ref, stat)
-    for who in range(out_ref.shape[0] - 1):
-        out_ref[who] = combined(pieces, weights, who).astype(BF16)
+def combine_kernel(spans, out_spans, *refs):
+    pieces, out_refs = refs[: len(spans)], refs[len(spans) :]
+    weights, stat = weights_of(pieces, spans)
+    for out_ref, (first, last) in zip(out_refs, out_spans):
+        write_stat(out_ref, stat)
+        for who in range(first, last):
+            out_ref[who - first] = combined(pieces, spans, weights, who).astype(BF16)
 
 
 def project(latents, stats, proj_ref, out_ref):
@@ -240,8 +246,11 @@
 def finish_kernel(*refs):
     *pieces, proj_ref, out_ref = refs
     requests = out_ref.shape[0]
-    weights, stat = weights_of(pieces)
-    latents = [combined(pieces, weights, who).astype(BF16) for who in range(requests)]
+    spans = [(0, requests)] * len(pieces)
+    weights, stat = weights_of(pieces, spans)
+    latents = [
+        combined(pieces, spans, weights, who).astype(BF16) for who in range(requests)
+    ]
     stats = [stat[:, who : who + 1] for who in range(requests)]
     project(latents, stats, proj_ref, out_ref)
 
@@ -281,14 +290,21 @@
     return [pl.BlockSpec(memory_space=pltpu.SMEM)] * count
 
 
-def combine(pieces):
-    return call(
-        combine_kernel,
-        jax.ShapeDtypeStruct(pieces[0].shape, BF16),
-        *pieces,
-        in_specs=vmem(len(pieces)),
-        out_specs=vmem(1)[0],
-    )
+def combine(pieces, out_spans):
+    arrays = [array for array, _ in pieces]
+    spans = tuple(span for _, span in pieces)
+    shapes = [
+        jax.ShapeDtypeStruct((last - first + 1,) + arrays[0].shape[1:], BF16)
+        for first, last in out_spans
+    ]
+    outs = call(
+        functools.partial(combine_kernel, spans, tuple(out_spans)),
+        shapes,
+        *arrays,
+        in_specs=vmem(len(arrays)),
+        out_specs=vmem(len(shapes)),
+    )
+    return list(zip(outs, out_spans))
 
 
 def shards(block_pool, block_table, lengths, destination, query_latent, new_latent, value_proj):
@@ -336,13 +352,15 @@
         out_specs=vmem(1)[0],
     )
 
-    own_q, plan, new_values = lax.optimization_barrier((own_q, plan, new_values))
-
     queries = {0: own_q}
     for s in range(1, far + 1):
         queries[-s] = lax.ppermute(queries[1 - s], "seq", up)
         if s <= near:
             queries[s] = lax.ppermute(queries[s - 1], "seq", down)
+        if s == 1:
+            queries[-s], plan = lax.optimization_barrier((queries[-s], plan))
+        if s == 2:
+            queries[-s], new_values = lax.optimization_barrier((queries[-s], new_values))
     order = sorted(queries)
     q_list = [queries[r] for r in order] + [swap(queries[r]) for r in order]
     n_pieces = len(q_list)
@@ -362,17 +380,23 @@
         ],
         mib=44,
     )
-    mine = dict(zip(order, outs[: len(order)]))
-    others = {r: swap(x) for r, x in zip(order, outs[len(order) :])}
-
-    from_up, from_down = [], []
-    for s in range(far, 0, -1):
-        sent = combine([mine[-s], others[-s]] + from_up)
-        from_up = [lax.ppermute(sent, "seq", down)]
-        if s <= near:
-            sent = combine([mine[s], others[s]] + from_down)
-            from_down = [lax.ppermute(sent, "seq", up)]
-    pieces = [mine[0], others[0]] + from_up + from_down
+    everything = (0, requests)
+    both = {
+        r: [(own, everything), (swap(other), everything)]
+        for r, own, other in zip(order, outs[: len(order)], outs[len(order) :])
+    }
+
+    def sent(piece, way):
+        array, span = piece
+        return [(lax.ppermute(array, "seq", way), span)]
+
+    halves = [(0, requests // 2), (requests // 2, requests)]
+    low, high = combine(both[-far], halves)
+    from_up, from_down = sent(low, down), sent(high, up)
+    for s in range(far - 1, 0, -1):
+        from_up = sent(combine(both[-s] + from_up, [everything])[0], down)
+        from_down = sent(combine(both[s] + from_down, [everything])[0], up)
+    pieces = [array for array, _ in both[0] + from_up + from_down]
     values = call(
         finish_kernel,
         values_shape,

time: 121 us -> 118 us (0.975)
  blocking collectives: 14.9 us -> 26.4 us
  waiting for transfers between devices: 47.3 us -> 39.3 us
  starting transfers between devices: 34.2 us -> 27.4 us
    all_to_all x0 -> x1, blocking collectives: none -> 15.5 us  [shards(): lax.all_to_all(decode_q, 'pre', split_axis=0, concat_axis=0, tiled=True)]
    ppermute x4, waiting for transfers between devices: 22.4 us -> 11.1 us  [shards(): queries[-s] = lax.ppermute(queries[1 - s], 'seq', up)]
    all_to_all x1 -> x0, starting transfers between devices: 7.48 us -> none  [shards(): lax.all_to_all(decode_q, 'pre', split_axis=0, concat_axis=0, tiled=True)]
    all_to_all x1, blocking collectives: 14.9 us -> 10.9 us  [shards(): got = lax.all_to_all(values, 'pre', split_axis=0, concat_axis=0, tiled=True)]
    ppermute x3, waiting for transfers between devices: 2.49 us -> 5.22 us  [shards(): queries[s] = lax.ppermute(queries[s - 1], 'seq', down)]
    ppermute x7 -> x8, waiting for transfers between devices: 19.4 us -> 20.5 us  [sent(): return [(lax.ppermute(array, 'seq', way), span)]]
    ppermute x7 -> x8, starting transfers between devices: 11.4 us -> 11.5 us  [sent(): return [(lax.ppermute(array, 'seq', way), span)]]
  transfers between devices with their start and end apart: 31 -> 31, of which waited for: 14 -> 13; matrix products, arithmetic and copies ran while one was open for 0% -> 0% of each run, Pallas kernels for 3% -> 4%
where the time goes in v4:
time: 118 us; the launch traced here: 117 us
  waiting for transfers between devices  39.3 us (33%)
  starting transfers between devices  27.4 us (23%)
  blocking collectives  26.4 us (22%)
  Pallas kernels  19 us (16%)
  local copies, waits for them, and re-layouts  4.94 us (4%)
    ppermute x8, waiting for transfers between devices, sent(): return [(lax.ppermute(array, 'seq', way), span)]  20.5 us
    pallas_call x12, Pallas kernels, call(): pl.pallas_call(kernel, out_shape=out_shape, compiler_params=pltpu.Compile...  19 us
    all_to_all x1, blocking collectives, shards(): lax.all_to_all(decode_q, 'pre', split_axis=0, concat_axis=0, tiled=True)  15.5 us
    ppermute x8, starting transfers between devices, sent(): return [(lax.ppermute(array, 'seq', way), span)]  11.5 us
    ppermute x4, waiting for transfers between devices, shards(): queries[-s] = lax.ppermute(queries[1 - s], 'seq', up)  11.1 us
    ppermute x3, starting transfers between devices, shards(): queries[s] = lax.ppermute(queries[s - 1], 'seq', down)  11 us
    all_to_all x1, blocking collectives, shards(): got = lax.all_to_all(values, 'pre', split_axis=0, concat_axis=0, tiled=True)  10.9 us
    ppermute x3, waiting for transfers between devices, shards(): queries[s] = lax.ppermute(queries[s - 1], 'seq', down)  5.22 us
  transfers between devices with their start and end apart: 31, of which 13 were waited for; matrix products, arithmetic and copies ran while one was open for 0% of the time, Pallas kernels for 4%

profile of v4, /device:TPU:2, one launch (start us, length us, event | category | flops | bytes accessed | tf_op | source)
XLA Modules:
  0.0 117.3 jit_solution(6368315010431528392)
XLA Ops:
  0.0 15.5 %all_to_all.10.refs_4_ = bf16[16,16,576]{2,1,0:T(8,128)(2,1)S(1)} all-to-all(bf16[16,16,576]{2,1,0:T(8,128)(2,1)} %bitcast.7), channel_id=1, replica_groups=mesh['pre'=16,'seq'=8,'dec'=2] {'pre'}, dimensions={0} | all-to-all | bytes 589824 | tf_op jit(solution)/shard_map/all_to_all | solution.py:330
  15.5 1.9 %collective-permute-start = (bf16[16,16,576]{2,1,0:T(8,128)(2,1)S(1)}, bf16[16,16,576]{2,1,0:T(8,128)(2,1)S(1)}, u32[]{:S(2)}, u32[]{:S(2)}) collective-permute-start(bf16[16,16,576]{2,1,0:T(8,128)(2,1)S(1)} %all_to_all.10.refs_4_), channel_id=1, source_target_pairs={{0,2},{2,4},{4,6},{6,8},{8,10},{10,12},{12,14},{14,0},{1,3},{3,5},... | collective-permute-start | bytes 884744 | tf_op jit(solution)/shard_map/ppermute | solution.py:357
  17.4 0.7 copy-done.4
  18.1 0.7 copy-done.5
  18.7 0.7 copy-done.6
  19.4 1.7 %shard_map.73.plan_ref = s32[16,11]{1,0:T(8,128)S(1)} custom-call(s32[1,16]{1,0:T(1,128)S(1)} %copy-done.4, s32[1,16]{1,0:T(1,128)S(1)} %copy-done.5, s32[1,1,1,128]{3,2,1,0:T(1,128)S(1)} %copy-done.6, s32[1]{0:T(128)} %bitcast.1.split_ref), custom_call_target="tpu_custom_call" | custom-call | tf_op jit(solution)/shard_map/pallas_call | solution.py:277
  21.1 4.0 %collective-permute-start.4 = (bf16[16,16,576]{2,1,0:T(8,128)(2,1)S(1)}, bf16[16,16,576]{2,1,0:T(8,128)(2,1)S(1)}, u32[]{:S(2)}, u32[]{:S(2)}) collective-permute-start(bf16[16,16,576]{2,1,0:T(8,128)(2,1)S(1)} %all_to_all.10.refs_4_), channel_id=1, source_target_pairs={{0,14},{2,0},{4,2},{6,4},{8,6},{10,8},{12,10},{14,12},{1,15},{3,1}... | collective-permute-start | bytes 884744 | tf_op jit(solution)/shard_map/ppermute | solution.py:359
  25.1 2.8 %collective-permute-done.refs_3_ = bf16[16,16,576]{2,1,0:T(8,128)(2,1)S(1)} collective-permute-done((bf16[16,16,576]{2,1,0:T(8,128)(2,1)S(1)}, bf16[16,16,576]{2,1,0:T(8,128)(2,1)S(1)}, u32[]{:S(2)}, u32[]{:S(2)}) %collective-permute-start) | collective-permute-done | bytes 294944 | tf_op jit(solution)/shard_map/ppermute | solution.py:357
  27.9 1.2 %copy-done = bf16[8,512,128]{2,1,0:T(8,128)(2,1)S(1)} copy-done((bf16[8,512,128]{2,1,0:T(8,128)(2,1)S(1)}, bf16[8,512,128]{2,1,0:T(8,128)(2,1)}, u32[]{:S(2)}) %copy-start) | copy-done | bytes 1048600
  29.1 1.0 copy-done.2
  30.1 0.8 copy-done.3
  30.9 0.9 shard_map.74.new_ref
  31.8 0.0 collective-permute-done.4.refs_5_
  31.8 3.3 %collective-permute-start.5 = (bf16[16,16,576]{2,1,0:T(8,128)(2,1)S(1)}, bf16[16,16,576]{2,1,0:T(8,128)(2,1)S(1)}, u32[]{:S(2)}, u32[]{:S(2)}) collective-permute-start(bf16[16,16,576]{2,1,0:T(8,128)(2,1)S(1)} %collective-permute-done.4.refs_5_), channel_id=1, source_target_pairs={{0,14},{2,0},{4,2},{6,4},{8,6},{10,8},{12,10},{14,12},{1,15},{3,1}... | collective-permute-start | bytes 884744 | tf_op jit(solution)/shard_map/ppermute | solution.py:359
  35.1 1.6 %collective-permute-done.1.refs_2_ = bf16[16,16,576]{2,1,0:T(8,128)(2,1)S(1)} collective-permute-done((bf16[16,16,576]{2,1,0:T(8,128)(2,1)S(1)}, bf16[16,16,576]{2,1,0:T(8,128)(2,1)S(1)}, u32[]{:S(2)}, u32[]{:S(2)}) %collective-permute-start.1) | collective-permute-done | bytes 294944 | tf_op jit(solution)/shard_map/ppermute | solution.py:357
  36.7 0.0 collective-permute-start.2
  36.7 0.0 collective-permute-start.11
  36.7 0.5 collective-permute-start.12
  37.2 0.0 collective-permute-start.10
  37.2 2.8 %collective-permute-done.5.refs_6_ = bf16[16,16,576]{2,1,0:T(8,128)(2,1)S(1)} collective-permute-done((bf16[16,16,576]{2,1,0:T(8,128)(2,1)S(1)}, bf16[16,16,576]{2,1,0:T(8,128)(2,1)S(1)}, u32[]{:S(2)}, u32[]{:S(2)}) %collective-permute-start.5) | collective-permute-done | bytes 294944 | tf_op jit(solution)/shard_map/ppermute | solution.py:359
  40.0 3.7 %collective-permute-start.6 = (bf16[16,16,576]{2,1,0:T(8,128)(2,1)S(1)}, bf16[16,16,576]{2,1,0:T(8,128)(2,1)S(1)}, u32[]{:S(2)}, u32[]{:S(2)}) collective-permute-start(bf16[16,16,576]{2,1,0:T(8,128)(2,1)S(1)} %collective-permute-done.5.refs_6_), channel_id=1, source_target_pairs={{0,14},{2,0},{4,2},{6,4},{8,6},{10,8},{12,10},{14,12},{1,15},{3,1}... | collective-permute-start | bytes 884744 | tf_op jit(solution)/shard_map/ppermute | solution.py:359
  43.7 1.5 %collective-permute-done.2.refs_1_ = bf16[16,16,576]{2,1,0:T(8,128)(2,1)S(1)} collective-permute-done((bf16[16,16,576]{2,1,0:T(8,128)(2,1)S(1)}, bf16[16,16,576]{2,1,0:T(8,128)(2,1)S(1)}, u32[]{:S(2)}, u32[]{:S(2)}) %collective-permute-start.2) | collective-permute-done | bytes 294944 | tf_op jit(solution)/shard_map/ppermute | solution.py:357
  45.2 0.0 collective-permute-start.3
  45.2 0.0 collective-permute-done.11.refs_12_
  45.2 0.0 collective-permute-start.9
  45.2 0.5 collective-permute-start.13
  45.7 0.1 collective-permute-start.8
  45.8 2.5 %collective-permute-done.6.refs_7_ = bf16[16,16,576]{2,1,0:T(8,128)(2,1)S(1)} collective-permute-done((bf16[16,16,576]{2,1,0:T(8,128)(2,1)S(1)}, bf16[16,16,576]{2,1,0:T(8,128)(2,1)S(1)}, u32[]{:S(2)}, u32[]{:S(2)}) %collective-permute-start.6) | collective-permute-done | bytes 294944 | tf_op jit(solution)/shard_map/ppermute | solution.py:359
  48.3 5.2 %collective-permute-done.3.refs_0_ = bf16[16,16,576]{2,1,0:T(8,128)(2,1)S(1)} collective-permute-done((bf16[16,16,576]{2,1,0:T(8,128)(2,1)S(1)}, bf16[16,16,576]{2,1,0:T(8,128)(2,1)S(1)}, u32[]{:S(2)}, u32[]{:S(2)}) %collective-permute-start.3) | collective-permute-done | bytes 294944 | tf_op jit(solution)/shard_map/ppermute | solution.py:357
  53.5 0.0 collective-permute-start.7
  53.5 0.0 collective-permute-done.13.refs_14_
  53.5 0.0 collective-permute-done.8.refs_9_
  53.5 1.6 %collective-permute-done.7.refs_8_ = bf16[16,16,576]{2,1,0:T(8,128)(2,1)S(1)} collective-permute-done((bf16[16,16,576]{2,1,0:T(8,128)(2,1)S(1)}, bf16[16,16,576]{2,1,0:T(8,128)(2,1)S(1)}, u32[]{:S(2)}, u32[]{:S(2)}) %collective-permute-start.7) | collective-permute-done | bytes 294944 | tf_op jit(solution)/shard_map/ppermute | solution.py:327
  55.1 12.8 %shard_map.75 = (bf16[17,16,512]{2,1,0:T(8,128)(2,1)S(1)}, bf16[17,16,512]{2,1,0:T(8,128)(2,1)S(1)}, bf16[17,16,512]{2,1,0:T(8,128)(2,1)S(1)}, bf16[17,16,512]{2...) custom-call(s32[16,11]{1,0:T(8,128)S(1)} %shard_map.73.plan_ref, ...), custom_call_target="tpu_custom_call" | custom-call | tf_op jit(solution)/shard_map/pallas_call | solution.py:277
  67.9 0.2 collective-permute-start.19
  68.2 0.4 collective-permute-start.18
  68.5 0.1 collective-permute-start.26
  68.7 0.9 collective-permute-done.19.refs_1_
  69.6 0.2 shard_map.76
  69.8 0.1 collective-permute-start.20
  69.9 2.0 %collective-permute-start.27 = (bf16[9,16,512]{2,1,0:T(8,128)(2,1)S(1)}, bf16[9,16,512]{2,1,0:T(8,128)(2,1)S(1)}, u32[]{:S(2)}, u32[]{:S(2)}) collective-permute-start(bf16[9,16,512]{2,1,0:T(8,128)(2,1)S(1)} %get-tuple-element.47), channel_id=1, source_target_pairs={{0,2},{2,4},{4,6},{6,8},{8,10},{10,12},{12,14},{14,0},{1,3},{3,5},... | collective-permute-start | bytes 442376 | tf_op jit(solution)/shard_map/ppermute | solution.py:391
  71.9 0.5 collective-permute-start.25
  72.4 3.3 %collective-permute-done.20.refs_2_ = bf16[9,16,512]{2,1,0:T(8,128)(2,1)S(1)} collective-permute-done((bf16[9,16,512]{2,1,0:T(8,128)(2,1)S(1)}, bf16[9,16,512]{2,1,0:T(8,128)(2,1)S(1)}, u32[]{:S(2)}, u32[]{:S(2)}) %collective-permute-start.20) | collective-permute-done | bytes 147488 | tf_op jit(solution)/shard_map/ppermute | solution.py:391
  75.7 0.2 shard_map.77
  76.0 1.6 %collective-permute-start.21 = (bf16[17,16,512]{2,1,0:T(8,128)(2,1)S(1)}, bf16[17,16,512]{2,1,0:T(8,128)(2,1)S(1)}, u32[]{:S(2)}, u32[]{:S(2)}) collective-permute-start(bf16[17,16,512]{2,1,0:T(8,128)(2,1)S(1)} %shard_map.77), channel_id=1, source_target_pairs={{0,14},{2,0},{4,2},{6,4},{8,6},{10,8},{12,10},{14,12},{1,15},{3,1}... | collective-permute-start | bytes 835592 | tf_op jit(solution)/shard_map/ppermute | solution.py:391
  77.5 0.2 shard_map.80
  77.8 0.6 collective-permute-start.28
  78.4 0.5 collective-permute-start.24
  78.9 5.0 %collective-permute-done.21.refs_2_ = bf16[17,16,512]{2,1,0:T(8,128)(2,1)S(1)} collective-permute-done((bf16[17,16,512]{2,1,0:T(8,128)(2,1)S(1)}, bf16[17,16,512]{2,1,0:T(8,128)(2,1)S(1)}, u32[]{:S(2)}, u32[]{:S(2)}) %collective-permute-start.21) | collective-permute-done | bytes 278560 | tf_op jit(solution)/shard_map/ppermute | solution.py:391
  83.9 0.2 shard_map.78
  84.2 3.3 %collective-permute-start.22 = (bf16[17,16,512]{2,1,0:T(8,128)(2,1)S(1)}, bf16[17,16,512]{2,1,0:T(8,128)(2,1)S(1)}, u32[]{:S(2)}, u32[]{:S(2)}) collective-permute-start(bf16[17,16,512]{2,1,0:T(8,128)(2,1)S(1)} %shard_map.78), channel_id=1, source_target_pairs={{0,14},{2,0},{4,2},{6,4},{8,6},{10,8},{12,10},{14,12},{1,15},{3,1}... | collective-permute-start | bytes 835592 | tf_op jit(solution)/shard_map/ppermute | solution.py:391
  87.5 0.2 shard_map.81
  87.7 0.1 collective-permute-start.29
  87.8 0.1 collective-permute-start.15
  87.9 4.3 %collective-permute-done.22.refs_2_ = bf16[17,16,512]{2,1,0:T(8,128)(2,1)S(1)} collective-permute-done((bf16[17,16,512]{2,1,0:T(8,128)(2,1)S(1)}, bf16[17,16,512]{2,1,0:T(8,128)(2,1)S(1)}, u32[]{:S(2)}, u32[]{:S(2)}) %collective-permute-start.22) | collective-permute-done | bytes 278560 | tf_op jit(solution)/shard_map/ppermute | solution.py:391
  92.3 0.2 shard_map.79
  92.5 3.8 %collective-permute-start.23 = (bf16[17,16,512]{2,1,0:T(8,128)(2,1)S(1)}, bf16[17,16,512]{2,1,0:T(8,128)(2,1)S(1)}, u32[]{:S(2)}, u32[]{:S(2)}) collective-permute-start(bf16[17,16,512]{2,1,0:T(8,128)(2,1)S(1)} %shard_map.79), channel_id=1, source_target_pairs={{0,14},{2,0},{4,2},{6,4},{8,6},{10,8},{12,10},{14,12},{1,15},{3,1}... | collective-permute-start | bytes 835592 | tf_op jit(solution)/shard_map/ppermute | solution.py:391
  96.3 0.2 shard_map.82
  96.6 0.1 collective-permute-start.30
  96.7 3.7 %collective-permute-done.23.refs_2_ = bf16[17,16,512]{2,1,0:T(8,128)(2,1)S(1)} collective-permute-done((bf16[17,16,512]{2,1,0:T(8,128)(2,1)S(1)}, bf16[17,16,512]{2,1,0:T(8,128)(2,1)S(1)}, u32[]{:S(2)}, u32[]{:S(2)}) %collective-permute-start.23) | collective-permute-done | bytes 278560 | tf_op jit(solution)/shard_map/ppermute | solution.py:391
  100.4 4.0 %collective-permute-done.30.refs_3_ = bf16[17,16,512]{2,1,0:T(8,128)(2,1)S(1)} collective-permute-done((bf16[17,16,512]{2,1,0:T(8,128)(2,1)S(1)}, bf16[17,16,512]{2,1,0:T(8,128)(2,1)S(1)}, u32[]{:S(2)}, u32[]{:S(2)}) %collective-permute-start.30) | collective-permute-done | bytes 278560 | tf_op jit(solution)/shard_map/ppermute | solution.py:391
  104.4 0.9 shard_map.83
  105.4 10.9 %all_to_all.11.cache_ref = f32[16,2,1152]{2,1,0:T(2,128)S(1)} all-to-all(f32[16,2,1152]{2,1,0:T(2,128)S(1)} %shard_map.83), channel_id=1, replica_groups=mesh['pre'=16,'seq'=8,'dec'=2] {'pre'}, dimensions={0} | all-to-all | bytes 294912 | tf_op jit(solution)/shard_map/all_to_all | solution.py:408
  116.3 1.0 shard_map.84
  (26 shorter events, 0.1 us)
Async XLA Ops:
  15.5 12.4 %collective-permute-start = (bf16[16,16,576]{2,1,0:T(8,128)(2,1)S(1)}, bf16[16,16,576]{2,1,0:T(8,128)(2,1)S(1)}, u32[]{:S(2)}, u32[]{:S(2)}) collective-permute-start(bf16[16,16,576]{2,1,0:T(8,128)(2,1)S(1)} %all_to_all.10.refs_4_), channel_id=1, source_target_pairs={{0,2},{2,4},{4,6},{6,8},{8,10},{10,12},{12,14},{14,0},{1,3},{3,5},... | collective-permute-start | bytes 884744 | tf_op jit(solution)/shard_map/ppermute | solution.py:357
  17.4 0.7 copy-start.4
  18.1 0.7 copy-start.5
  18.7 0.7 copy-start.6
  21.1 10.7 %collective-permute-start.4 = (bf16[16,16,576]{2,1,0:T(8,128)(2,1)S(1)}, bf16[16,16,576]{2,1,0:T(8,128)(2,1)S(1)}, u32[]{:S(2)}, u32[]{:S(2)}) collective-permute-start(bf16[16,16,576]{2,1,0:T(8,128)(2,1)S(1)} %all_to_all.10.refs_4_), channel_id=1, source_target_pairs={{0,14},{2,0},{4,2},{6,4},{8,6},{10,8},{12,10},{14,12},{1,15},{3,1}... | collective-permute-start | bytes 884744 | tf_op jit(solution)/shard_map/ppermute | solution.py:359
  27.9 8.8 %collective-permute-start.1 = (bf16[16,16,576]{2,1,0:T(8,128)(2,1)S(1)}, bf16[16,16,576]{2,1,0:T(8,128)(2,1)S(1)}, u32[]{:S(2)}, u32[]{:S(2)}) collective-permute-start(bf16[16,16,576]{2,1,0:T(8,128)(2,1)S(1)} %collective-permute-done.refs_3_), channel_id=1, source_target_pairs={{0,2},{2,4},{4,6},{6,8},{8,10},{10,12},{12,14},{14,0},{1,3},{3,5},... | collective-permute-start | bytes 884744 | tf_op jit(solution)/shard_map/ppermute | solution.py:357
  27.9 1.2 %copy-start = (bf16[8,512,128]{2,1,0:T(8,128)(2,1)S(1)}, bf16[8,512,128]{2,1,0:T(8,128)(2,1)}, u32[]{:S(2)}) copy-start(bf16[8,512,128]{2,1,0:T(8,128)(2,1)} %refs_4_.1) | copy-start | bytes 3145732
  29.1 1.0 copy-start.2
  30.1 0.8 copy-start.3
  31.8 8.2 %collective-permute-start.5 = (bf16[16,16,576]{2,1,0:T(8,128)(2,1)S(1)}, bf16[16,16,576]{2,1,0:T(8,128)(2,1)S(1)}, u32[]{:S(2)}, u32[]{:S(2)}) collective-permute-start(bf16[16,16,576]{2,1,0:T(8,128)(2,1)S(1)} %collective-permute-done.4.refs_5_), channel_id=1, source_target_pairs={{0,14},{2,0},{4,2},{6,4},{8,6},{10,8},{12,10},{14,12},{1,15},{3,1}... | collective-permute-start | bytes 884744 | tf_op jit(solution)/shard_map/ppermute | solution.py:359
  36.7 8.5 %collective-permute-start.2 = (bf16[16,16,576]{2,1,0:T(8,128)(2,1)S(1)}, bf16[16,16,576]{2,1,0:T(8,128)(2,1)S(1)}, u32[]{:S(2)}, u32[]{:S(2)}) collective-permute-start(bf16[16,16,576]{2,1,0:T(8,128)(2,1)S(1)} %collective-permute-done.1.refs_2_), channel_id=1, source_target_pairs={{0,2},{2,4},{4,6},{6,8},{8,10},{10,12},{12,14},{14,0},{1,3},{3,5},... | collective-permute-start | bytes 884744 | tf_op jit(solution)/shard_map/ppermute | solution.py:357
  36.7 8.5 %collective-permute-start.11 = (bf16[16,16,576]{2,1,0:T(8,128)(2,1)S(1)}, bf16[16,16,576]{2,1,0:T(8,128)(2,1)S(1)}, u32[]{:S(2)}, u32[]{:S(2)}) collective-permute-start(bf16[16,16,576]{2,1,0:T(8,128)(2,1)S(1)} %all_to_all.10.refs_4_), channel_id=1, source_target_pairs={{0,1},{1,0},{2,3},{3,2},{4,5},{5,4},{6,7},{7,6},{8,9},{9,8},{10,11... | collective-permute-start | bytes 884744 | tf_op jit(solution)/shard_map/ppermute | solution.py:327
  36.7 8.5 %collective-permute-start.12 = (bf16[16,16,576]{2,1,0:T(8,128)(2,1)S(1)}, bf16[16,16,576]{2,1,0:T(8,128)(2,1)S(1)}, u32[]{:S(2)}, u32[]{:S(2)}) collective-permute-start(bf16[16,16,576]{2,1,0:T(8,128)(2,1)S(1)} %collective-permute-done.4.refs_5_), channel_id=1, source_target_pairs={{0,1},{1,0},{2,3},{3,2},{4,5},{5,4},{6,7},{7,6},{8,9},{9,8},{10,11... | collective-permute-start | bytes 884744 | tf_op jit(solution)/shard_map/ppermute | solution.py:327
  37.2 8.5 %collective-permute-start.10 = (bf16[16,16,576]{2,1,0:T(8,128)(2,1)S(1)}, bf16[16,16,576]{2,1,0:T(8,128)(2,1)S(1)}, u32[]{:S(2)}, u32[]{:S(2)}) collective-permute-start(bf16[16,16,576]{2,1,0:T(8,128)(2,1)S(1)} %collective-permute-done.refs_3_), channel_id=1, source_target_pairs={{0,1},{1,0},{2,3},{3,2},{4,5},{5,4},{6,7},{7,6},{8,9},{9,8},{10,11... | collective-permute-start | bytes 884744 | tf_op jit(solution)/shard_map/ppermute | solution.py:327
  40.0 8.3 %collective-permute-start.6 = (bf16[16,16,576]{2,1,0:T(8,128)(2,1)S(1)}, bf16[16,16,576]{2,1,0:T(8,128)(2,1)S(1)}, u32[]{:S(2)}, u32[]{:S(2)}) collective-permute-start(bf16[16,16,576]{2,1,0:T(8,128)(2,1)S(1)} %collective-permute-done.5.refs_6_), channel_id=1, source_target_pairs={{0,14},{2,0},{4,2},{6,4},{8,6},{10,8},{12,10},{14,12},{1,15},{3,1}... | collective-permute-start | bytes 884744 | tf_op jit(solution)/shard_map/ppermute | solution.py:359
  45.2 8.3 %collective-permute-start.3 = (bf16[16,16,576]{2,1,0:T(8,128)(2,1)S(1)}, bf16[16,16,576]{2,1,0:T(8,128)(2,1)S(1)}, u32[]{:S(2)}, u32[]{:S(2)}) collective-permute-start(bf16[16,16,576]{2,1,0:T(8,128)(2,1)S(1)} %collective-permute-done.2.refs_1_), channel_id=1, source_target_pairs={{0,2},{2,4},{4,6},{6,8},{8,10},{10,12},{12,14},{14,0},{1,3},{3,5},... | collective-permute-start | bytes 884744 | tf_op jit(solution)/shard_map/ppermute | solution.py:357
  45.2 8.3 %collective-permute-start.9 = (bf16[16,16,576]{2,1,0:T(8,128)(2,1)S(1)}, bf16[16,16,576]{2,1,0:T(8,128)(2,1)S(1)}, u32[]{:S(2)}, u32[]{:S(2)}) collective-permute-start(bf16[16,16,576]{2,1,0:T(8,128)(2,1)S(1)} %collective-permute-done.1.refs_2_), channel_id=1, source_target_pairs={{0,1},{1,0},{2,3},{3,2},{4,5},{5,4},{6,7},{7,6},{8,9},{9,8},{10,11... | collective-permute-start | bytes 884744 | tf_op jit(solution)/shard_map/ppermute | solution.py:327
  45.2 8.3 %collective-permute-start.13 = (bf16[16,16,576]{2,1,0:T(8,128)(2,1)S(1)}, bf16[16,16,576]{2,1,0:T(8,128)(2,1)S(1)}, u32[]{:S(2)}, u32[]{:S(2)}) collective-permute-start(bf16[16,16,576]{2,1,0:T(8,128)(2,1)S(1)} %collective-permute-done.5.refs_6_), channel_id=1, source_target_pairs={{0,1},{1,0},{2,3},{3,2},{4,5},{5,4},{6,7},{7,6},{8,9},{9,8},{10,11... | collective-permute-start | bytes 884744 | tf_op jit(solution)/shard_map/ppermute | solution.py:327
  45.7 7.8 %collective-permute-start.8 = (bf16[16,16,576]{2,1,0:T(8,128)(2,1)S(1)}, bf16[16,16,576]{2,1,0:T(8,128)(2,1)S(1)}, u32[]{:S(2)}, u32[]{:S(2)}) collective-permute-start(bf16[16,16,576]{2,1,0:T(8,128)(2,1)S(1)} %collective-permute-done.2.refs_1_), channel_id=1, source_target_pairs={{0,1},{1,0},{2,3},{3,2},{4,5},{5,4},{6,7},{7,6},{8,9},{9,8},{10,11... | collective-permute-start | bytes 884744 | tf_op jit(solution)/shard_map/ppermute | solution.py:327
  48.3 5.2 %collective-permute-start.14 = (bf16[16,16,576]{2,1,0:T(8,128)(2,1)S(1)}, bf16[16,16,576]{2,1,0:T(8,128)(2,1)S(1)}, u32[]{:S(2)}, u32[]{:S(2)}) collective-permute-start(bf16[16,16,576]{2,1,0:T(8,128)(2,1)S(1)} %collective-permute-done.6.refs_7_), channel_id=1, source_target_pairs={{0,1},{1,0},{2,3},{3,2},{4,5},{5,4},{6,7},{7,6},{8,9},{9,8},{10,11... | collective-permute-start | bytes 884744 | tf_op jit(solution)/shard_map/ppermute | solution.py:327
  53.5 1.6 %collective-permute-start.7 = (bf16[16,16,576]{2,1,0:T(8,128)(2,1)S(1)}, bf16[16,16,576]{2,1,0:T(8,128)(2,1)S(1)}, u32[]{:S(2)}, u32[]{:S(2)}) collective-permute-start(bf16[16,16,576]{2,1,0:T(8,128)(2,1)S(1)} %collective-permute-done.3.refs_0_), channel_id=1, source_target_pairs={{0,1},{1,0},{2,3},{3,2},{4,5},{5,4},{6,7},{7,6},{8,9},{9,8},{10,11... | collective-permute-start | bytes 884744 | tf_op jit(solution)/shard_map/ppermute | solution.py:327
  55.1 49.3 %copy-start.1 = (bf16[8,512,128]{2,1,0:T(8,128)(2,1)S(1)}, bf16[8,512,128]{2,1,0:T(8,128)(2,1)}, u32[]{:S(2)}) copy-start(bf16[8,512,128]{2,1,0:T(8,128)(2,1)} %refs_4_.1) | copy-start | bytes 3145732
  67.9 1.6 %collective-permute-start.19 = (bf16[17,16,512]{2,1,0:T(8,128)(2,1)S(1)}, bf16[17,16,512]{2,1,0:T(8,128)(2,1)S(1)}, u32[]{:S(2)}, u32[]{:S(2)}) collective-permute-start(bf16[17,16,512]{2,1,0:T(8,128)(2,1)S(1)} %get-tuple-element.39), channel_id=1, source_target_pairs={{0,1},{1,0},{2,3},{3,2},{4,5},{5,4},{6,7},{7,6},{8,9},{9,8},{10,11... | collective-permute-start | bytes 835592 | tf_op jit(solution)/shard_map/ppermute | solution.py:327
  68.2 3.7 %collective-permute-start.18 = (bf16[17,16,512]{2,1,0:T(8,128)(2,1)S(1)}, bf16[17,16,512]{2,1,0:T(8,128)(2,1)S(1)}, u32[]{:S(2)}, u32[]{:S(2)}) collective-permute-start(bf16[17,16,512]{2,1,0:T(8,128)(2,1)S(1)} %get-tuple-element.37), channel_id=1, source_target_pairs={{0,1},{1,0},{2,3},{3,2},{4,5},{5,4},{6,7},{7,6},{8,9},{9,8},{10,11... | collective-permute-start | bytes 835592 | tf_op jit(solution)/shard_map/ppermute | solution.py:327
  68.5 9.0 %collective-permute-start.26 = (bf16[17,16,512]{2,1,0:T(8,128)(2,1)S(1)}, bf16[17,16,512]{2,1,0:T(8,128)(2,1)S(1)}, u32[]{:S(2)}, u32[]{:S(2)}) collective-permute-start(bf16[17,16,512]{2,1,0:T(8,128)(2,1)S(1)} %get-tuple-element.46), channel_id=1, source_target_pairs={{0,1},{1,0},{2,3},{3,2},{4,5},{5,4},{6,7},{7,6},{8,9},{9,8},{10,11... | collective-permute-start | bytes 835592 | tf_op jit(solution)/shard_map/ppermute | solution.py:327
  69.8 6.0 %collective-permute-start.20 = (bf16[9,16,512]{2,1,0:T(8,128)(2,1)S(1)}, bf16[9,16,512]{2,1,0:T(8,128)(2,1)S(1)}, u32[]{:S(2)}, u32[]{:S(2)}) collective-permute-start(bf16[9,16,512]{2,1,0:T(8,128)(2,1)S(1)} %get-tuple-element.40), channel_id=1, source_target_pairs={{0,14},{2,0},{4,2},{6,4},{8,6},{10,8},{12,10},{14,12},{1,15},{3,1}... | collective-permute-start | bytes 442376 | tf_op jit(solution)/shard_map/ppermute | solution.py:391
  69.9 7.7 %collective-permute-start.27 = (bf16[9,16,512]{2,1,0:T(8,128)(2,1)S(1)}, bf16[9,16,512]{2,1,0:T(8,128)(2,1)S(1)}, u32[]{:S(2)}, u32[]{:S(2)}) collective-permute-start(bf16[9,16,512]{2,1,0:T(8,128)(2,1)S(1)} %get-tuple-element.47), channel_id=1, source_target_pairs={{0,2},{2,4},{4,6},{6,8},{8,10},{10,12},{12,14},{14,0},{1,3},{3,5},... | collective-permute-start | bytes 442376 | tf_op jit(solution)/shard_map/ppermute | solution.py:391
  71.9 6.5 %collective-permute-start.17 = (bf16[17,16,512]{2,1,0:T(8,128)(2,1)S(1)}, bf16[17,16,512]{2,1,0:T(8,128)(2,1)S(1)}, u32[]{:S(2)}, u32[]{:S(2)}) collective-permute-start(bf16[17,16,512]{2,1,0:T(8,128)(2,1)S(1)} %get-tuple-element.35), channel_id=1, source_target_pairs={{0,1},{1,0},{2,3},{3,2},{4,5},{5,4},{6,7},{7,6},{8,9},{9,8},{10,11... | collective-permute-start | bytes 835592 | tf_op jit(solution)/shard_map/ppermute | solution.py:327
  71.9 15.6 %collective-permute-start.25 = (bf16[17,16,512]{2,1,0:T(8,128)(2,1)S(1)}, bf16[17,16,512]{2,1,0:T(8,128)(2,1)S(1)}, u32[]{:S(2)}, u32[]{:S(2)}) collective-permute-start(bf16[17,16,512]{2,1,0:T(8,128)(2,1)S(1)} %get-tuple-element.44), channel_id=1, source_target_pairs={{0,1},{1,0},{2,3},{3,2},{4,5},{5,4},{6,7},{7,6},{8,9},{9,8},{10,11... | collective-permute-start | bytes 835592 | tf_op jit(solution)/shard_map/ppermute | solution.py:327
  76.0 7.9 %collective-permute-start.21 = (bf16[17,16,512]{2,1,0:T(8,128)(2,1)S(1)}, bf16[17,16,512]{2,1,0:T(8,128)(2,1)S(1)}, u32[]{:S(2)}, u32[]{:S(2)}) collective-permute-start(bf16[17,16,512]{2,1,0:T(8,128)(2,1)S(1)} %shard_map.77), channel_id=1, source_target_pairs={{0,14},{2,0},{4,2},{6,4},{8,6},{10,8},{12,10},{14,12},{1,15},{3,1}... | collective-permute-start | bytes 835592 | tf_op jit(solution)/shard_map/ppermute | solution.py:391
  77.8 9.7 %collective-permute-start.28 = (bf16[17,16,512]{2,1,0:T(8,128)(2,1)S(1)}, bf16[17,16,512]{2,1,0:T(8,128)(2,1)S(1)}, u32[]{:S(2)}, u32[]{:S(2)}) collective-permute-start(bf16[17,16,512]{2,1,0:T(8,128)(2,1)S(1)} %shard_map.80), channel_id=1, source_target_pairs={{0,2},{2,4},{4,6},{6,8},{8,10},{10,12},{12,14},{14,0},{1,3},{3,5},... | collective-permute-start | bytes 835592 | tf_op jit(solution)/shard_map/ppermute | solution.py:391
  78.4 9.6 %collective-permute-start.16 = (bf16[17,16,512]{2,1,0:T(8,128)(2,1)S(1)}, bf16[17,16,512]{2,1,0:T(8,128)(2,1)S(1)}, u32[]{:S(2)}, u32[]{:S(2)}) collective-permute-start(bf16[17,16,512]{2,1,0:T(8,128)(2,1)S(1)} %get-tuple-element.33), channel_id=1, source_target_pairs={{0,1},{1,0},{2,3},{3,2},{4,5},{5,4},{6,7},{7,6},{8,9},{9,8},{10,11... | collective-permute-start | bytes 835592 | tf_op jit(solution)/shard_map/ppermute | solution.py:327
  78.4 17.9 %collective-permute-start.24 = (bf16[17,16,512]{2,1,0:T(8,128)(2,1)S(1)}, bf16[17,16,512]{2,1,0:T(8,128)(2,1)S(1)}, u32[]{:S(2)}, u32[]{:S(2)}) collective-permute-start(bf16[17,16,512]{2,1,0:T(8,128)(2,1)S(1)} %get-tuple-element.42), channel_id=1, source_target_pairs={{0,1},{1,0},{2,3},{3,2},{4,5},{5,4},{6,7},{7,6},{8,9},{9,8},{10,11... | collective-permute-start | bytes 835592 | tf_op jit(solution)/shard_map/ppermute | solution.py:327
  84.2 8.1 %collective-permute-start.22 = (bf16[17,16,512]{2,1,0:T(8,128)(2,1)S(1)}, bf16[17,16,512]{2,1,0:T(8,128)(2,1)S(1)}, u32[]{:S(2)}, u32[]{:S(2)}) collective-permute-start(bf16[17,16,512]{2,1,0:T(8,128)(2,1)S(1)} %shard_map.78), channel_id=1, source_target_pairs={{0,14},{2,0},{4,2},{6,4},{8,6},{10,8},{12,10},{14,12},{1,15},{3,1}... | collective-permute-start | bytes 835592 | tf_op jit(solution)/shard_map/ppermute | solution.py:391
  87.7 8.6 %collective-permute-start.29 = (bf16[17,16,512]{2,1,0:T(8,128)(2,1)S(1)}, bf16[17,16,512]{2,1,0:T(8,128)(2,1)S(1)}, u32[]{:S(2)}, u32[]{:S(2)}) collective-permute-start(bf16[17,16,512]{2,1,0:T(8,128)(2,1)S(1)} %shard_map.81), channel_id=1, source_target_pairs={{0,2},{2,4},{4,6},{6,8},{8,10},{10,12},{12,14},{14,0},{1,3},{3,5},... | collective-permute-start | bytes 835592 | tf_op jit(solution)/shard_map/ppermute | solution.py:391
  87.8 8.8 %collective-permute-start.15 = (bf16[17,16,512]{2,1,0:T(8,128)(2,1)S(1)}, bf16[17,16,512]{2,1,0:T(8,128)(2,1)S(1)}, u32[]{:S(2)}, u32[]{:S(2)}) collective-permute-start(bf16[17,16,512]{2,1,0:T(8,128)(2,1)S(1)} %get-tuple-element.31), channel_id=1, source_target_pairs={{0,1},{1,0},{2,3},{3,2},{4,5},{5,4},{6,7},{7,6},{8,9},{9,8},{10,11... | collective-permute-start | bytes 835592 | tf_op jit(solution)/shard_map/ppermute | solution.py:327
  92.5 7.8 %collective-permute-start.23 = (bf16[17,16,512]{2,1,0:T(8,128)(2,1)S(1)}, bf16[17,16,512]{2,1,0:T(8,128)(2,1)S(1)}, u32[]{:S(2)}, u32[]{:S(2)}) collective-permute-start(bf16[17,16,512]{2,1,0:T(8,128)(2,1)S(1)} %shard_map.79), channel_id=1, source_target_pairs={{0,14},{2,0},{4,2},{6,4},{8,6},{10,8},{12,10},{14,12},{1,15},{3,1}... | collective-permute-start | bytes 835592 | tf_op jit(solution)/shard_map/ppermute | solution.py:391
  96.6 7.8 %collective-permute-start.30 = (bf16[17,16,512]{2,1,0:T(8,128)(2,1)S(1)}, bf16[17,16,512]{2,1,0:T(8,128)(2,1)S(1)}, u32[]{:S(2)}, u32[]{:S(2)}) collective-permute-start(bf16[17,16,512]{2,1,0:T(8,128)(2,1)S(1)} %shard_map.82), channel_id=1, source_target_pairs={{0,2},{2,4},{4,6},{6,8},{8,10},{10,12},{12,14},{14,0},{1,3},{3,5},... | collective-permute-start | bytes 835592 | tf_op jit(solution)/shard_map/ppermute | solution.py:391

commit v5 on v4

--- a/solution.py
+++ b/solution.py
@@ -13,6 +13,7 @@
 BF16 = jnp.bfloat16
 MIB = 1024 * 1024
 GROUP = 2
+AHEAD = 3
 
 
 def pack_stat(stat):
@@ -73,30 +74,35 @@
     latent = o_refs[0].shape[2]
     groups = requests // GROUP
 
-    def each(g, act):
+    def fetch(g):
         pairs = plan_ref[g * GROUP + GROUP - 1, 1]
-        half = lax.rem(g, 2)
-        for m in range(GROUP):
-            for j in range(slots):
-
-                @pl.when(j // 2 < pairs)
-                def _():
-                    act(
+        part = lax.rem(g, AHEAD + 1)
+        for c in range(slots // 2):
+
+            @pl.when(c < pairs)
+            def _():
+                for m in range(GROUP):
+                    for j in (2 * c, 2 * c + 1):
                         pltpu.make_async_copy(
                             pool_ref.at[plan_ref[g * GROUP + m, 3 + j]],
-                            kbuf.at[half, m, j],
-                            sems.at[half, m, j],
-                        )
-                    )
-
-    each(0, lambda c: c.start())
+                            kbuf.at[part, m, j],
+                            sems.at[part],
+                        ).start()
+
+    def arrived(part, pairs):
+        blocks = kbuf.at[part, :, pl.ds(0, 2 * pairs)]
+        pltpu.make_async_copy(blocks, blocks, sems.at[part]).wait()
+
+    for g in range(AHEAD):
+        fetch(g)
     stat_ref[...] = jnp.zeros_like(stat_ref)
     lane = lax.broadcasted_iota(jnp.int32, stat_ref.shape, 1)
     pair = 2 * block
     column = lax.broadcasted_iota(jnp.int32, (1, pair), 1)
 
     def compute(g, pairs):
-        half = lax.rem(g, 2)
+        part = lax.rem(g, AHEAD + 1)
+        arrived(part, pairs)
         whos = [plan_ref[g * GROUP + m, 0] for m in range(GROUP)]
         keys, scores, tops = [], [], []
         for m, who in enumerate(whos):
@@ -104,7 +110,7 @@
             q = jnp.concatenate([ref[who] for ref in q_refs], axis=0)
             keys.append(
                 [
-                    jnp.concatenate([kbuf[half, m, 2 * c], kbuf[half, m, 2 * c + 1]], axis=1)
+                    jnp.concatenate([kbuf[part, m, 2 * c], kbuf[part, m, 2 * c + 1]], axis=1)
                     for c in range(pairs)
                 ]
             )
@@ -121,13 +127,13 @@
             for c in range(pairs):
                 e = jnp.exp2(scores[m][c] - tops[m])
                 total = e if total is None else total + e
-                part = lax.dot_general(
+                product = lax.dot_general(
                     e.astype(BF16),
                     keys[m][c][:latent],
                     (((1,), (1,)), ((), ())),
                     preferred_element_type=F32,
                 )
-                out = part if out is None else out + part
+                out = product if out is None else out + product
             total = jnp.sum(total, axis=1, keepdims=True)
             some = total > 0
             out = (out * jnp.where(some, 1.0 / total, 0.0)).astype(BF16)
@@ -137,11 +143,10 @@
             stat_ref[...] = jnp.where(lane == who, stat, stat_ref[...])
 
     def step(g, carry):
-        @pl.when(g + 1 < groups)
+        @pl.when(g + AHEAD < groups)
         def _():
-            each(g + 1, lambda c: c.start())
-
-        each(g, lambda c: c.wait())
+            fetch(g + AHEAD)
+
         pairs_here = plan_ref[g * GROUP + GROUP - 1, 1]
         for pairs in range(1, slots // 2 + 1):
 
@@ -374,9 +379,9 @@
         in_specs=smem(1) + vmem(n_pieces) + [pl.BlockSpec(memory_space=pltpu.HBM)],
         out_specs=vmem(n_pieces),
         scratch_shapes=[
-            pltpu.VMEM((2, GROUP, slots, width, block), BF16),
+            pltpu.VMEM((AHEAD + 1, GROUP, slots, width, block), BF16),
             pltpu.VMEM((n_pieces * rows, 128), F32),
-            pltpu.SemaphoreType.DMA((2, GROUP, slots)),
+            pltpu.SemaphoreType.DMA((AHEAD + 1,)),
         ],
         mib=44,
     )

time: 118 us -> 116 us (0.983)
  Pallas kernels: 19 us -> 17.7 us
    pallas_call x12, Pallas kernels: 19 us -> 17.7 us  [call(): pl.pallas_call(kernel, out_shape=out_shape, compiler_params=pltpu.Compile...]
where the time goes in v5:
time: 116 us
  waiting for transfers between devices  39.3 us (34%)
  starting transfers between devices  27.4 us (24%)
  blocking collectives  26.4 us (23%)
  Pallas kernels  17.7 us (15%)
  local copies, waits for them, and re-layouts  4.94 us (4%)
    ppermute x8, waiting for transfers between devices, sent(): return [(lax.ppermute(array, 'seq', way), span)]  20.5 us
    pallas_call x12, Pallas kernels, call(): pl.pallas_call(kernel, out_shape=out_shape, compiler_params=pltpu.Compile...  17.7 us
    all_to_all x1, blocking collectives, shards(): lax.all_to_all(decode_q, 'pre', split_axis=0, concat_axis=0, tiled=True)  15.5 us
    ppermute x8, starting transfers between devices, sent(): return [(lax.ppermute(array, 'seq', way), span)]  11.5 us
    ppermute x4, waiting for transfers between devices, shards(): queries[-s] = lax.ppermute(queries[1 - s], 'seq', up)  11.1 us
    ppermute x3, starting transfers between devices, shards(): queries[s] = lax.ppermute(queries[s - 1], 'seq', down)  11 us
    all_to_all x1, blocking collectives, shards(): got = lax.all_to_all(values, 'pre', split_axis=0, concat_axis=0, tiled=True)  10.9 us
    ppermute x3, waiting for transfers between devices, shards(): queries[s] = lax.ppermute(queries[s - 1], 'seq', down)  5.22 us
  transfers between devices with their start and end apart: 31, of which 13 were waited for; matrix products, arithmetic and copies ran while one was open for 0% of the time, Pallas kernels for 4%

profile of v5, /device:TPU:2, one launch (start us, length us, event | category | flops | bytes accessed | tf_op | source)
XLA Modules:
  0.0 115.9 jit_solution(9697985260961160614)
XLA Ops:
  0.0 15.5 %all_to_all.10.refs_4_ = bf16[16,16,576]{2,1,0:T(8,128)(2,1)S(1)} all-to-all(bf16[16,16,576]{2,1,0:T(8,128)(2,1)} %bitcast.7), channel_id=1, replica_groups=mesh['pre'=16,'seq'=8,'dec'=2] {'pre'}, dimensions={0} | all-to-all | bytes 589824 | tf_op jit(solution)/shard_map/all_to_all | solution.py:335
  15.5 1.9 %collective-permute-start = (bf16[16,16,576]{2,1,0:T(8,128)(2,1)S(1)}, bf16[16,16,576]{2,1,0:T(8,128)(2,1)S(1)}, u32[]{:S(2)}, u32[]{:S(2)}) collective-permute-start(bf16[16,16,576]{2,1,0:T(8,128)(2,1)S(1)} %all_to_all.10.refs_4_), channel_id=1, source_target_pairs={{0,2},{2,4},{4,6},{6,8},{8,10},{10,12},{12,14},{14,0},{1,3},{3,5},... | collective-permute-start | bytes 884744 | tf_op jit(solution)/shard_map/ppermute | solution.py:362
  17.4 0.7 copy-done.4
  18.1 0.7 copy-done.5
  18.7 0.7 copy-done.6
  19.4 1.7 %shard_map.73.plan_ref = s32[16,11]{1,0:T(8,128)S(1)} custom-call(s32[1,16]{1,0:T(1,128)S(1)} %copy-done.4, s32[1,16]{1,0:T(1,128)S(1)} %copy-done.5, s32[1,1,1,128]{3,2,1,0:T(1,128)S(1)} %copy-done.6, s32[1]{0:T(128)} %bitcast.1.split_ref), custom_call_target="tpu_custom_call" | custom-call | tf_op jit(solution)/shard_map/pallas_call | solution.py:282
  21.1 4.0 %collective-permute-start.4 = (bf16[16,16,576]{2,1,0:T(8,128)(2,1)S(1)}, bf16[16,16,576]{2,1,0:T(8,128)(2,1)S(1)}, u32[]{:S(2)}, u32[]{:S(2)}) collective-permute-start(bf16[16,16,576]{2,1,0:T(8,128)(2,1)S(1)} %all_to_all.10.refs_4_), channel_id=1, source_target_pairs={{0,14},{2,0},{4,2},{6,4},{8,6},{10,8},{12,10},{14,12},{1,15},{3,1}... | collective-permute-start | bytes 884744 | tf_op jit(solution)/shard_map/ppermute | solution.py:364
  25.1 2.8 %collective-permute-done.refs_3_ = bf16[16,16,576]{2,1,0:T(8,128)(2,1)S(1)} collective-permute-done((bf16[16,16,576]{2,1,0:T(8,128)(2,1)S(1)}, bf16[16,16,576]{2,1,0:T(8,128)(2,1)S(1)}, u32[]{:S(2)}, u32[]{:S(2)}) %collective-permute-start) | collective-permute-done | bytes 294944 | tf_op jit(solution)/shard_map/ppermute | solution.py:362
  27.9 1.2 %copy-done = bf16[8,512,128]{2,1,0:T(8,128)(2,1)S(1)} copy-done((bf16[8,512,128]{2,1,0:T(8,128)(2,1)S(1)}, bf16[8,512,128]{2,1,0:T(8,128)(2,1)}, u32[]{:S(2)}) %copy-start) | copy-done | bytes 1048600
  29.1 1.0 copy-done.2
  30.1 0.8 copy-done.3
  30.9 0.9 shard_map.74.new_ref
  31.8 0.0 collective-permute-done.4.refs_5_
  31.8 3.3 %collective-permute-start.5 = (bf16[16,16,576]{2,1,0:T(8,128)(2,1)S(1)}, bf16[16,16,576]{2,1,0:T(8,128)(2,1)S(1)}, u32[]{:S(2)}, u32[]{:S(2)}) collective-permute-start(bf16[16,16,576]{2,1,0:T(8,128)(2,1)S(1)} %collective-permute-done.4.refs_5_), channel_id=1, source_target_pairs={{0,14},{2,0},{4,2},{6,4},{8,6},{10,8},{12,10},{14,12},{1,15},{3,1}... | collective-permute-start | bytes 884744 | tf_op jit(solution)/shard_map/ppermute | solution.py:364
  35.1 1.6 %collective-permute-done.1.refs_2_ = bf16[16,16,576]{2,1,0:T(8,128)(2,1)S(1)} collective-permute-done((bf16[16,16,576]{2,1,0:T(8,128)(2,1)S(1)}, bf16[16,16,576]{2,1,0:T(8,128)(2,1)S(1)}, u32[]{:S(2)}, u32[]{:S(2)}) %collective-permute-start.1) | collective-permute-done | bytes 294944 | tf_op jit(solution)/shard_map/ppermute | solution.py:362
  36.7 0.0 collective-permute-start.2
  36.7 0.0 collective-permute-start.11
  36.7 0.5 collective-permute-start.12
  37.2 0.0 collective-permute-start.10
  37.2 2.8 %collective-permute-done.5.refs_6_ = bf16[16,16,576]{2,1,0:T(8,128)(2,1)S(1)} collective-permute-done((bf16[16,16,576]{2,1,0:T(8,128)(2,1)S(1)}, bf16[16,16,576]{2,1,0:T(8,128)(2,1)S(1)}, u32[]{:S(2)}, u32[]{:S(2)}) %collective-permute-start.5) | collective-permute-done | bytes 294944 | tf_op jit(solution)/shard_map/ppermute | solution.py:364
  40.0 3.7 %collective-permute-start.6 = (bf16[16,16,576]{2,1,0:T(8,128)(2,1)S(1)}, bf16[16,16,576]{2,1,0:T(8,128)(2,1)S(1)}, u32[]{:S(2)}, u32[]{:S(2)}) collective-permute-start(bf16[16,16,576]{2,1,0:T(8,128)(2,1)S(1)} %collective-permute-done.5.refs_6_), channel_id=1, source_target_pairs={{0,14},{2,0},{4,2},{6,4},{8,6},{10,8},{12,10},{14,12},{1,15},{3,1}... | collective-permute-start | bytes 884744 | tf_op jit(solution)/shard_map/ppermute | solution.py:364
  43.7 1.5 %collective-permute-done.2.refs_1_ = bf16[16,16,576]{2,1,0:T(8,128)(2,1)S(1)} collective-permute-done((bf16[16,16,576]{2,1,0:T(8,128)(2,1)S(1)}, bf16[16,16,576]{2,1,0:T(8,128)(2,1)S(1)}, u32[]{:S(2)}, u32[]{:S(2)}) %collective-permute-start.2) | collective-permute-done | bytes 294944 | tf_op jit(solution)/shard_map/ppermute | solution.py:362
  45.2 0.0 collective-permute-start.3
  45.2 0.0 collective-permute-done.11.refs_12_
  45.2 0.0 collective-permute-start.9
  45.2 0.5 collective-permute-start.13
  45.7 0.1 collective-permute-start.8
  45.8 2.5 %collective-permute-done.6.refs_7_ = bf16[16,16,576]{2,1,0:T(8,128)(2,1)S(1)} collective-permute-done((bf16[16,16,576]{2,1,0:T(8,128)(2,1)S(1)}, bf16[16,16,576]{2,1,0:T(8,128)(2,1)S(1)}, u32[]{:S(2)}, u32[]{:S(2)}) %collective-permute-start.6) | collective-permute-done | bytes 294944 | tf_op jit(solution)/shard_map/ppermute | solution.py:364
  48.3 0.0 collective-permute-start.14
  48.3 5.2 %collective-permute-done.3.refs_0_ = bf16[16,16,576]{2,1,0:T(8,128)(2,1)S(1)} collective-permute-done((bf16[16,16,576]{2,1,0:T(8,128)(2,1)S(1)}, bf16[16,16,576]{2,1,0:T(8,128)(2,1)S(1)}, u32[]{:S(2)}, u32[]{:S(2)}) %collective-permute-start.3) | collective-permute-done | bytes 294944 | tf_op jit(solution)/shard_map/ppermute | solution.py:362
  53.5 0.0 collective-permute-start.7
  53.5 1.6 %collective-permute-done.7.refs_8_ = bf16[16,16,576]{2,1,0:T(8,128)(2,1)S(1)} collective-permute-done((bf16[16,16,576]{2,1,0:T(8,128)(2,1)S(1)}, bf16[16,16,576]{2,1,0:T(8,128)(2,1)S(1)}, u32[]{:S(2)}, u32[]{:S(2)}) %collective-permute-start.7) | collective-permute-done | bytes 294944 | tf_op jit(solution)/shard_map/ppermute | solution.py:332
  55.1 11.5 %shard_map.75 = (bf16[17,16,512]{2,1,0:T(8,128)(2,1)S(1)}, bf16[17,16,512]{2,1,0:T(8,128)(2,1)S(1)}, bf16[17,16,512]{2,1,0:T(8,128)(2,1)S(1)}, bf16[17,16,512]{2...) custom-call(s32[16,11]{1,0:T(8,128)S(1)} %shard_map.73.plan_ref, ...), custom_call_target="tpu_custom_call" | custom-call | tf_op jit(solution)/shard_map/pallas_call | solution.py:282
  66.6 0.2 collective-permute-start.19
  66.9 0.4 collective-permute-start.18
  67.2 0.1 collective-permute-start.26
  67.4 0.9 collective-permute-done.19.refs_1_
  68.3 0.2 shard_map.76
  68.5 0.1 collective-permute-start.20
  68.6 2.0 %collective-permute-start.27 = (bf16[9,16,512]{2,1,0:T(8,128)(2,1)S(1)}, bf16[9,16,512]{2,1,0:T(8,128)(2,1)S(1)}, u32[]{:S(2)}, u32[]{:S(2)}) collective-permute-start(bf16[9,16,512]{2,1,0:T(8,128)(2,1)S(1)} %get-tuple-element.47), channel_id=1, source_target_pairs={{0,2},{2,4},{4,6},{6,8},{8,10},{10,12},{12,14},{14,0},{1,3},{3,5},... | collective-permute-start | bytes 442376 | tf_op jit(solution)/shard_map/ppermute | solution.py:396
  70.6 0.0 collective-permute-start.17
  70.6 0.5 collective-permute-start.25
  71.1 3.3 %collective-permute-done.20.refs_2_ = bf16[9,16,512]{2,1,0:T(8,128)(2,1)S(1)} collective-permute-done((bf16[9,16,512]{2,1,0:T(8,128)(2,1)S(1)}, bf16[9,16,512]{2,1,0:T(8,128)(2,1)S(1)}, u32[]{:S(2)}, u32[]{:S(2)}) %collective-permute-start.20) | collective-permute-done | bytes 147488 | tf_op jit(solution)/shard_map/ppermute | solution.py:396
  74.4 0.2 shard_map.77
  74.7 1.6 %collective-permute-start.21 = (bf16[17,16,512]{2,1,0:T(8,128)(2,1)S(1)}, bf16[17,16,512]{2,1,0:T(8,128)(2,1)S(1)}, u32[]{:S(2)}, u32[]{:S(2)}) collective-permute-start(bf16[17,16,512]{2,1,0:T(8,128)(2,1)S(1)} %shard_map.77), channel_id=1, source_target_pairs={{0,14},{2,0},{4,2},{6,4},{8,6},{10,8},{12,10},{14,12},{1,15},{3,1}... | collective-permute-start | bytes 835592 | tf_op jit(solution)/shard_map/ppermute | solution.py:396
  76.2 0.2 shard_map.80
  76.5 0.6 collective-permute-start.28
  77.1 0.5 collective-permute-start.24
  77.6 5.0 %collective-permute-done.21.refs_2_ = bf16[17,16,512]{2,1,0:T(8,128)(2,1)S(1)} collective-permute-done((bf16[17,16,512]{2,1,0:T(8,128)(2,1)S(1)}, bf16[17,16,512]{2,1,0:T(8,128)(2,1)S(1)}, u32[]{:S(2)}, u32[]{:S(2)}) %collective-permute-start.21) | collective-permute-done | bytes 278560 | tf_op jit(solution)/shard_map/ppermute | solution.py:396
  82.6 0.2 shard_map.78
  82.9 3.3 %collective-permute-start.22 = (bf16[17,16,512]{2,1,0:T(8,128)(2,1)S(1)}, bf16[17,16,512]{2,1,0:T(8,128)(2,1)S(1)}, u32[]{:S(2)}, u32[]{:S(2)}) collective-permute-start(bf16[17,16,512]{2,1,0:T(8,128)(2,1)S(1)} %shard_map.78), channel_id=1, source_target_pairs={{0,14},{2,0},{4,2},{6,4},{8,6},{10,8},{12,10},{14,12},{1,15},{3,1}... | collective-permute-start | bytes 835592 | tf_op jit(solution)/shard_map/ppermute | solution.py:396
  86.2 0.2 shard_map.81
  86.4 0.1 collective-permute-start.29
  86.5 0.1 collective-permute-start.15
  86.6 4.3 %collective-permute-done.22.refs_2_ = bf16[17,16,512]{2,1,0:T(8,128)(2,1)S(1)} collective-permute-done((bf16[17,16,512]{2,1,0:T(8,128)(2,1)S(1)}, bf16[17,16,512]{2,1,0:T(8,128)(2,1)S(1)}, u32[]{:S(2)}, u32[]{:S(2)}) %collective-permute-start.22) | collective-permute-done | bytes 278560 | tf_op jit(solution)/shard_map/ppermute | solution.py:396
  91.0 0.2 shard_map.79
  91.2 3.8 %collective-permute-start.23 = (bf16[17,16,512]{2,1,0:T(8,128)(2,1)S(1)}, bf16[17,16,512]{2,1,0:T(8,128)(2,1)S(1)}, u32[]{:S(2)}, u32[]{:S(2)}) collective-permute-start(bf16[17,16,512]{2,1,0:T(8,128)(2,1)S(1)} %shard_map.79), channel_id=1, source_target_pairs={{0,14},{2,0},{4,2},{6,4},{8,6},{10,8},{12,10},{14,12},{1,15},{3,1}... | collective-permute-start | bytes 835592 | tf_op jit(solution)/shard_map/ppermute | solution.py:396
  95.0 0.2 shard_map.82
  95.3 0.1 collective-permute-start.30
  95.4 3.7 %collective-permute-done.23.refs_2_ = bf16[17,16,512]{2,1,0:T(8,128)(2,1)S(1)} collective-permute-done((bf16[17,16,512]{2,1,0:T(8,128)(2,1)S(1)}, bf16[17,16,512]{2,1,0:T(8,128)(2,1)S(1)}, u32[]{:S(2)}, u32[]{:S(2)}) %collective-permute-start.23) | collective-permute-done | bytes 278560 | tf_op jit(solution)/shard_map/ppermute | solution.py:396
  99.1 4.0 %collective-permute-done.30.refs_3_ = bf16[17,16,512]{2,1,0:T(8,128)(2,1)S(1)} collective-permute-done((bf16[17,16,512]{2,1,0:T(8,128)(2,1)S(1)}, bf16[17,16,512]{2,1,0:T(8,128)(2,1)S(1)}, u32[]{:S(2)}, u32[]{:S(2)}) %collective-permute-start.30) | collective-permute-done | bytes 278560 | tf_op jit(solution)/shard_map/ppermute | solution.py:396
  103.1 0.9 shard_map.83
  104.0 10.9 %all_to_all.11.cache_ref = f32[16,2,1152]{2,1,0:T(2,128)S(1)} all-to-all(f32[16,2,1152]{2,1,0:T(2,128)S(1)} %shard_map.83), channel_id=1, replica_groups=mesh['pre'=16,'seq'=8,'dec'=2] {'pre'}, dimensions={0} | all-to-all | bytes 294912 | tf_op jit(solution)/shard_map/all_to_all | solution.py:413
  114.9 1.0 shard_map.84
  (26 shorter events, 0.1 us)
Async XLA Ops:
  15.5 12.4 %collective-permute-start = (bf16[16,16,576]{2,1,0:T(8,128)(2,1)S(1)}, bf16[16,16,576]{2,1,0:T(8,128)(2,1)S(1)}, u32[]{:S(2)}, u32[]{:S(2)}) collective-permute-start(bf16[16,16,576]{2,1,0:T(8,128)(2,1)S(1)} %all_to_all.10.refs_4_), channel_id=1, source_target_pairs={{0,2},{2,4},{4,6},{6,8},{8,10},{10,12},{12,14},{14,0},{1,3},{3,5},... | collective-permute-start | bytes 884744 | tf_op jit(solution)/shard_map/ppermute | solution.py:362
  17.4 0.7 copy-start.4
  18.1 0.7 copy-start.5
  18.7 0.7 copy-start.6
  21.1 10.7 %collective-permute-start.4 = (bf16[16,16,576]{2,1,0:T(8,128)(2,1)S(1)}, bf16[16,16,576]{2,1,0:T(8,128)(2,1)S(1)}, u32[]{:S(2)}, u32[]{:S(2)}) collective-permute-start(bf16[16,16,576]{2,1,0:T(8,128)(2,1)S(1)} %all_to_all.10.refs_4_), channel_id=1, source_target_pairs={{0,14},{2,0},{4,2},{6,4},{8,6},{10,8},{12,10},{14,12},{1,15},{3,1}... | collective-permute-start | bytes 884744 | tf_op jit(solution)/shard_map/ppermute | solution.py:364
  27.9 8.8 %collective-permute-start.1 = (bf16[16,16,576]{2,1,0:T(8,128)(2,1)S(1)}, bf16[16,16,576]{2,1,0:T(8,128)(2,1)S(1)}, u32[]{:S(2)}, u32[]{:S(2)}) collective-permute-start(bf16[16,16,576]{2,1,0:T(8,128)(2,1)S(1)} %collective-permute-done.refs_3_), channel_id=1, source_target_pairs={{0,2},{2,4},{4,6},{6,8},{8,10},{10,12},{12,14},{14,0},{1,3},{3,5},... | collective-permute-start | bytes 884744 | tf_op jit(solution)/shard_map/ppermute | solution.py:362
  27.9 1.2 %copy-start = (bf16[8,512,128]{2,1,0:T(8,128)(2,1)S(1)}, bf16[8,512,128]{2,1,0:T(8,128)(2,1)}, u32[]{:S(2)}) copy-start(bf16[8,512,128]{2,1,0:T(8,128)(2,1)} %refs_4_.1) | copy-start | bytes 3145732
  29.1 1.0 copy-start.2
  30.1 0.8 copy-start.3
  31.8 8.2 %collective-permute-start.5 = (bf16[16,16,576]{2,1,0:T(8,128)(2,1)S(1)}, bf16[16,16,576]{2,1,0:T(8,128)(2,1)S(1)}, u32[]{:S(2)}, u32[]{:S(2)}) collective-permute-start(bf16[16,16,576]{2,1,0:T(8,128)(2,1)S(1)} %collective-permute-done.4.refs_5_), channel_id=1, source_target_pairs={{0,14},{2,0},{4,2},{6,4},{8,6},{10,8},{12,10},{14,12},{1,15},{3,1}... | collective-permute-start | bytes 884744 | tf_op jit(solution)/shard_map/ppermute | solution.py:364
  36.7 8.5 %collective-permute-start.2 = (bf16[16,16,576]{2,1,0:T(8,128)(2,1)S(1)}, bf16[16,16,576]{2,1,0:T(8,128)(2,1)S(1)}, u32[]{:S(2)}, u32[]{:S(2)}) collective-permute-start(bf16[16,16,576]{2,1,0:T(8,128)(2,1)S(1)} %collective-permute-done.1.refs_2_), channel_id=1, source_target_pairs={{0,2},{2,4},{4,6},{6,8},{8,10},{10,12},{12,14},{14,0},{1,3},{3,5},... | collective-permute-start | bytes 884744 | tf_op jit(solution)/shard_map/ppermute | solution.py:362
  36.7 8.5 %collective-permute-start.11 = (bf16[16,16,576]{2,1,0:T(8,128)(2,1)S(1)}, bf16[16,16,576]{2,1,0:T(8,128)(2,1)S(1)}, u32[]{:S(2)}, u32[]{:S(2)}) collective-permute-start(bf16[16,16,576]{2,1,0:T(8,128)(2,1)S(1)} %all_to_all.10.refs_4_), channel_id=1, source_target_pairs={{0,1},{1,0},{2,3},{3,2},{4,5},{5,4},{6,7},{7,6},{8,9},{9,8},{10,11... | collective-permute-start | bytes 884744 | tf_op jit(solution)/shard_map/ppermute | solution.py:332
  36.7 8.5 %collective-permute-start.12 = (bf16[16,16,576]{2,1,0:T(8,128)(2,1)S(1)}, bf16[16,16,576]{2,1,0:T(8,128)(2,1)S(1)}, u32[]{:S(2)}, u32[]{:S(2)}) collective-permute-start(bf16[16,16,576]{2,1,0:T(8,128)(2,1)S(1)} %collective-permute-done.4.refs_5_), channel_id=1, source_target_pairs={{0,1},{1,0},{2,3},{3,2},{4,5},{5,4},{6,7},{7,6},{8,9},{9,8},{10,11... | collective-permute-start | bytes 884744 | tf_op jit(solution)/shard_map/ppermute | solution.py:332
  37.2 8.5 %collective-permute-start.10 = (bf16[16,16,576]{2,1,0:T(8,128)(2,1)S(1)}, bf16[16,16,576]{2,1,0:T(8,128)(2,1)S(1)}, u32[]{:S(2)}, u32[]{:S(2)}) collective-permute-start(bf16[16,16,576]{2,1,0:T(8,128)(2,1)S(1)} %collective-permute-done.refs_3_), channel_id=1, source_target_pairs={{0,1},{1,0},{2,3},{3,2},{4,5},{5,4},{6,7},{7,6},{8,9},{9,8},{10,11... | collective-permute-start | bytes 884744 | tf_op jit(solution)/shard_map/ppermute | solution.py:332
  40.0 8.3 %collective-permute-start.6 = (bf16[16,16,576]{2,1,0:T(8,128)(2,1)S(1)}, bf16[16,16,576]{2,1,0:T(8,128)(2,1)S(1)}, u32[]{:S(2)}, u32[]{:S(2)}) collective-permute-start(bf16[16,16,576]{2,1,0:T(8,128)(2,1)S(1)} %collective-permute-done.5.refs_6_), channel_id=1, source_target_pairs={{0,14},{2,0},{4,2},{6,4},{8,6},{10,8},{12,10},{14,12},{1,15},{3,1}... | collective-permute-start | bytes 884744 | tf_op jit(solution)/shard_map/ppermute | solution.py:364
  45.2 8.3 %collective-permute-start.3 = (bf16[16,16,576]{2,1,0:T(8,128)(2,1)S(1)}, bf16[16,16,576]{2,1,0:T(8,128)(2,1)S(1)}, u32[]{:S(2)}, u32[]{:S(2)}) collective-permute-start(bf16[16,16,576]{2,1,0:T(8,128)(2,1)S(1)} %collective-permute-done.2.refs_1_), channel_id=1, source_target_pairs={{0,2},{2,4},{4,6},{6,8},{8,10},{10,12},{12,14},{14,0},{1,3},{3,5},... | collective-permute-start | bytes 884744 | tf_op jit(solution)/shard_map/ppermute | solution.py:362
  45.2 8.3 %collective-permute-start.9 = (bf16[16,16,576]{2,1,0:T(8,128)(2,1)S(1)}, bf16[16,16,576]{2,1,0:T(8,128)(2,1)S(1)}, u32[]{:S(2)}, u32[]{:S(2)}) collective-permute-start(bf16[16,16,576]{2,1,0:T(8,128)(2,1)S(1)} %collective-permute-done.1.refs_2_), channel_id=1, source_target_pairs={{0,1},{1,0},{2,3},{3,2},{4,5},{5,4},{6,7},{7,6},{8,9},{9,8},{10,11... | collective-permute-start | bytes 884744 | tf_op jit(solution)/shard_map/ppermute | solution.py:332
  45.2 8.3 %collective-permute-start.13 = (bf16[16,16,576]{2,1,0:T(8,128)(2,1)S(1)}, bf16[16,16,576]{2,1,0:T(8,128)(2,1)S(1)}, u32[]{:S(2)}, u32[]{:S(2)}) collective-permute-start(bf16[16,16,576]{2,1,0:T(8,128)(2,1)S(1)} %collective-permute-done.5.refs_6_), channel_id=1, source_target_pairs={{0,1},{1,0},{2,3},{3,2},{4,5},{5,4},{6,7},{7,6},{8,9},{9,8},{10,11... | collective-permute-start | bytes 884744 | tf_op jit(solution)/shard_map/ppermute | solution.py:332
  45.7 7.8 %collective-permute-start.8 = (bf16[16,16,576]{2,1,0:T(8,128)(2,1)S(1)}, bf16[16,16,576]{2,1,0:T(8,128)(2,1)S(1)}, u32[]{:S(2)}, u32[]{:S(2)}) collective-permute-start(bf16[16,16,576]{2,1,0:T(8,128)(2,1)S(1)} %collective-permute-done.2.refs_1_), channel_id=1, source_target_pairs={{0,1},{1,0},{2,3},{3,2},{4,5},{5,4},{6,7},{7,6},{8,9},{9,8},{10,11... | collective-permute-start | bytes 884744 | tf_op jit(solution)/shard_map/ppermute | solution.py:332
  48.3 5.2 %collective-permute-start.14 = (bf16[16,16,576]{2,1,0:T(8,128)(2,1)S(1)}, bf16[16,16,576]{2,1,0:T(8,128)(2,1)S(1)}, u32[]{:S(2)}, u32[]{:S(2)}) collective-permute-start(bf16[16,16,576]{2,1,0:T(8,128)(2,1)S(1)} %collective-permute-done.6.refs_7_), channel_id=1, source_target_pairs={{0,1},{1,0},{2,3},{3,2},{4,5},{5,4},{6,7},{7,6},{8,9},{9,8},{10,11... | collective-permute-start | bytes 884744 | tf_op jit(solution)/shard_map/ppermute | solution.py:332
  53.5 1.6 %collective-permute-start.7 = (bf16[16,16,576]{2,1,0:T(8,128)(2,1)S(1)}, bf16[16,16,576]{2,1,0:T(8,128)(2,1)S(1)}, u32[]{:S(2)}, u32[]{:S(2)}) collective-permute-start(bf16[16,16,576]{2,1,0:T(8,128)(2,1)S(1)} %collective-permute-done.3.refs_0_), channel_id=1, source_target_pairs={{0,1},{1,0},{2,3},{3,2},{4,5},{5,4},{6,7},{7,6},{8,9},{9,8},{10,11... | collective-permute-start | bytes 884744 | tf_op jit(solution)/shard_map/ppermute | solution.py:332
  55.1 48.0 %copy-start.1 = (bf16[8,512,128]{2,1,0:T(8,128)(2,1)S(1)}, bf16[8,512,128]{2,1,0:T(8,128)(2,1)}, u32[]{:S(2)}) copy-start(bf16[8,512,128]{2,1,0:T(8,128)(2,1)} %refs_4_.1) | copy-start | bytes 3145732
  66.6 1.6 %collective-permute-start.19 = (bf16[17,16,512]{2,1,0:T(8,128)(2,1)S(1)}, bf16[17,16,512]{2,1,0:T(8,128)(2,1)S(1)}, u32[]{:S(2)}, u32[]{:S(2)}) collective-permute-start(bf16[17,16,512]{2,1,0:T(8,128)(2,1)S(1)} %get-tuple-element.39), channel_id=1, source_target_pairs={{0,1},{1,0},{2,3},{3,2},{4,5},{5,4},{6,7},{7,6},{8,9},{9,8},{10,11... | collective-permute-start | bytes 835592 | tf_op jit(solution)/shard_map/ppermute | solution.py:332
  66.9 3.7 %collective-permute-start.18 = (bf16[17,16,512]{2,1,0:T(8,128)(2,1)S(1)}, bf16[17,16,512]{2,1,0:T(8,128)(2,1)S(1)}, u32[]{:S(2)}, u32[]{:S(2)}) collective-permute-start(bf16[17,16,512]{2,1,0:T(8,128)(2,1)S(1)} %get-tuple-element.37), channel_id=1, source_target_pairs={{0,1},{1,0},{2,3},{3,2},{4,5},{5,4},{6,7},{7,6},{8,9},{9,8},{10,11... | collective-permute-start | bytes 835592 | tf_op jit(solution)/shard_map/ppermute | solution.py:332
  67.2 9.0 %collective-permute-start.26 = (bf16[17,16,512]{2,1,0:T(8,128)(2,1)S(1)}, bf16[17,16,512]{2,1,0:T(8,128)(2,1)S(1)}, u32[]{:S(2)}, u32[]{:S(2)}) collective-permute-start(bf16[17,16,512]{2,1,0:T(8,128)(2,1)S(1)} %get-tuple-element.46), channel_id=1, source_target_pairs={{0,1},{1,0},{2,3},{3,2},{4,5},{5,4},{6,7},{7,6},{8,9},{9,8},{10,11... | collective-permute-start | bytes 835592 | tf_op jit(solution)/shard_map/ppermute | solution.py:332
  68.5 6.0 %collective-permute-start.20 = (bf16[9,16,512]{2,1,0:T(8,128)(2,1)S(1)}, bf16[9,16,512]{2,1,0:T(8,128)(2,1)S(1)}, u32[]{:S(2)}, u32[]{:S(2)}) collective-permute-start(bf16[9,16,512]{2,1,0:T(8,128)(2,1)S(1)} %get-tuple-element.40), channel_id=1, source_target_pairs={{0,14},{2,0},{4,2},{6,4},{8,6},{10,8},{12,10},{14,12},{1,15},{3,1}... | collective-permute-start | bytes 442376 | tf_op jit(solution)/shard_map/ppermute | solution.py:396
  68.6 7.7 %collective-permute-start.27 = (bf16[9,16,512]{2,1,0:T(8,128)(2,1)S(1)}, bf16[9,16,512]{2,1,0:T(8,128)(2,1)S(1)}, u32[]{:S(2)}, u32[]{:S(2)}) collective-permute-start(bf16[9,16,512]{2,1,0:T(8,128)(2,1)S(1)} %get-tuple-element.47), channel_id=1, source_target_pairs={{0,2},{2,4},{4,6},{6,8},{8,10},{10,12},{12,14},{14,0},{1,3},{3,5},... | collective-permute-start | bytes 442376 | tf_op jit(solution)/shard_map/ppermute | solution.py:396
  70.6 6.5 %collective-permute-start.17 = (bf16[17,16,512]{2,1,0:T(8,128)(2,1)S(1)}, bf16[17,16,512]{2,1,0:T(8,128)(2,1)S(1)}, u32[]{:S(2)}, u32[]{:S(2)}) collective-permute-start(bf16[17,16,512]{2,1,0:T(8,128)(2,1)S(1)} %get-tuple-element.35), channel_id=1, source_target_pairs={{0,1},{1,0},{2,3},{3,2},{4,5},{5,4},{6,7},{7,6},{8,9},{9,8},{10,11... | collective-permute-start | bytes 835592 | tf_op jit(solution)/shard_map/ppermute | solution.py:332
  70.6 15.6 %collective-permute-start.25 = (bf16[17,16,512]{2,1,0:T(8,128)(2,1)S(1)}, bf16[17,16,512]{2,1,0:T(8,128)(2,1)S(1)}, u32[]{:S(2)}, u32[]{:S(2)}) collective-permute-start(bf16[17,16,512]{2,1,0:T(8,128)(2,1)S(1)} %get-tuple-element.44), channel_id=1, source_target_pairs={{0,1},{1,0},{2,3},{3,2},{4,5},{5,4},{6,7},{7,6},{8,9},{9,8},{10,11... | collective-permute-start | bytes 835592 | tf_op jit(solution)/shard_map/ppermute | solution.py:332
  74.7 7.9 %collective-permute-start.21 = (bf16[17,16,512]{2,1,0:T(8,128)(2,1)S(1)}, bf16[17,16,512]{2,1,0:T(8,128)(2,1)S(1)}, u32[]{:S(2)}, u32[]{:S(2)}) collective-permute-start(bf16[17,16,512]{2,1,0:T(8,128)(2,1)S(1)} %shard_map.77), channel_id=1, source_target_pairs={{0,14},{2,0},{4,2},{6,4},{8,6},{10,8},{12,10},{14,12},{1,15},{3,1}... | collective-permute-start | bytes 835592 | tf_op jit(solution)/shard_map/ppermute | solution.py:396
  76.5 9.7 %collective-permute-start.28 = (bf16[17,16,512]{2,1,0:T(8,128)(2,1)S(1)}, bf16[17,16,512]{2,1,0:T(8,128)(2,1)S(1)}, u32[]{:S(2)}, u32[]{:S(2)}) collective-permute-start(bf16[17,16,512]{2,1,0:T(8,128)(2,1)S(1)} %shard_map.80), channel_id=1, source_target_pairs={{0,2},{2,4},{4,6},{6,8},{8,10},{10,12},{12,14},{14,0},{1,3},{3,5},... | collective-permute-start | bytes 835592 | tf_op jit(solution)/shard_map/ppermute | solution.py:396
  77.1 9.6 %collective-permute-start.16 = (bf16[17,16,512]{2,1,0:T(8,128)(2,1)S(1)}, bf16[17,16,512]{2,1,0:T(8,128)(2,1)S(1)}, u32[]{:S(2)}, u32[]{:S(2)}) collective-permute-start(bf16[17,16,512]{2,1,0:T(8,128)(2,1)S(1)} %get-tuple-element.33), channel_id=1, source_target_pairs={{0,1},{1,0},{2,3},{3,2},{4,5},{5,4},{6,7},{7,6},{8,9},{9,8},{10,11... | collective-permute-start | bytes 835592 | tf_op jit(solution)/shard_map/ppermute | solution.py:332
  77.1 17.9 %collective-permute-start.24 = (bf16[17,16,512]{2,1,0:T(8,128)(2,1)S(1)}, bf16[17,16,512]{2,1,0:T(8,128)(2,1)S(1)}, u32[]{:S(2)}, u32[]{:S(2)}) collective-permute-start(bf16[17,16,512]{2,1,0:T(8,128)(2,1)S(1)} %get-tuple-element.42), channel_id=1, source_target_pairs={{0,1},{1,0},{2,3},{3,2},{4,5},{5,4},{6,7},{7,6},{8,9},{9,8},{10,11... | collective-permute-start | bytes 835592 | tf_op jit(solution)/shard_map/ppermute | solution.py:332
  82.9 8.1 %collective-permute-start.22 = (bf16[17,16,512]{2,1,0:T(8,128)(2,1)S(1)}, bf16[17,16,512]{2,1,0:T(8,128)(2,1)S(1)}, u32[]{:S(2)}, u32[]{:S(2)}) collective-permute-start(bf16[17,16,512]{2,1,0:T(8,128)(2,1)S(1)} %shard_map.78), channel_id=1, source_target_pairs={{0,14},{2,0},{4,2},{6,4},{8,6},{10,8},{12,10},{14,12},{1,15},{3,1}... | collective-permute-start | bytes 835592 | tf_op jit(solution)/shard_map/ppermute | solution.py:396
  86.4 8.6 %collective-permute-start.29 = (bf16[17,16,512]{2,1,0:T(8,128)(2,1)S(1)}, bf16[17,16,512]{2,1,0:T(8,128)(2,1)S(1)}, u32[]{:S(2)}, u32[]{:S(2)}) collective-permute-start(bf16[17,16,512]{2,1,0:T(8,128)(2,1)S(1)} %shard_map.81), channel_id=1, source_target_pairs={{0,2},{2,4},{4,6},{6,8},{8,10},{10,12},{12,14},{14,0},{1,3},{3,5},... | collective-permute-start | bytes 835592 | tf_op jit(solution)/shard_map/ppermute | solution.py:396
  86.5 8.8 %collective-permute-start.15 = (bf16[17,16,512]{2,1,0:T(8,128)(2,1)S(1)}, bf16[17,16,512]{2,1,0:T(8,128)(2,1)S(1)}, u32[]{:S(2)}, u32[]{:S(2)}) collective-permute-start(bf16[17,16,512]{2,1,0:T(8,128)(2,1)S(1)} %get-tuple-element.31), channel_id=1, source_target_pairs={{0,1},{1,0},{2,3},{3,2},{4,5},{5,4},{6,7},{7,6},{8,9},{9,8},{10,11... | collective-permute-start | bytes 835592 | tf_op jit(solution)/shard_map/ppermute | solution.py:332
  91.2 7.8 %collective-permute-start.23 = (bf16[17,16,512]{2,1,0:T(8,128)(2,1)S(1)}, bf16[17,16,512]{2,1,0:T(8,128)(2,1)S(1)}, u32[]{:S(2)}, u32[]{:S(2)}) collective-permute-start(bf16[17,16,512]{2,1,0:T(8,128)(2,1)S(1)} %shard_map.79), channel_id=1, source_target_pairs={{0,14},{2,0},{4,2},{6,4},{8,6},{10,8},{12,10},{14,12},{1,15},{3,1}... | collective-permute-start | bytes 835592 | tf_op jit(solution)/shard_map/ppermute | solution.py:396
  95.3 7.8 %collective-permute-start.30 = (bf16[17,16,512]{2,1,0:T(8,128)(2,1)S(1)}, bf16[17,16,512]{2,1,0:T(8,128)(2,1)S(1)}, u32[]{:S(2)}, u32[]{:S(2)}) collective-permute-start(bf16[17,16,512]{2,1,0:T(8,128)(2,1)S(1)} %shard_map.82), channel_id=1, source_target_pairs={{0,2},{2,4},{4,6},{6,8},{8,10},{10,12},{12,14},{14,0},{1,3},{3,5},... | collective-permute-start | bytes 835592 | tf_op jit(solution)/shard_map/ppermute | solution.py:396

commit v6 on v5

--- a/solution.py
+++ b/solution.py
@@ -395,7 +395,8 @@
         array, span = piece
         return [(lax.ppermute(array, "seq", way), span)]
 
-    halves = [(0, requests // 2), (requests // 2, requests)]
+    cut = requests * 5 // 8
+    halves = [(0, cut), (cut, requests)]
     low, high = combine(both[-far], halves)
     from_up, from_down = sent(low, down), sent(high, up)
     for s in range(far - 1, 0, -1):

time: 116 us -> 115 us (level)
  waiting for transfers between devices: 39.3 us -> 36.6 us
    ppermute x8, waiting for transfers between devices: 20.5 us -> 17.7 us  [sent(): return [(lax.ppermute(array, 'seq', way), span)]]
  transfers between devices with their start and end apart: 31 -> 31, of which waited for: 13 -> 12; matrix products, arithmetic and copies ran while one was open for 0% -> 0% of each run, Pallas kernels for 4% -> 4%
where the time goes in v6:
time: 115 us; the launch traced here: 114 us
  waiting for transfers between devices  36.6 us (32%)
  starting transfers between devices  28.3 us (25%)
  blocking collectives  26.2 us (23%)
  Pallas kernels  18.1 us (16%)
  local copies, waits for them, and re-layouts  4.94 us (4%)
    pallas_call x12, Pallas kernels, call(): pl.pallas_call(kernel, out_shape=out_shape, compiler_params=pltpu.Compile...  18.1 us
    ppermute x8, waiting for transfers between devices, sent(): return [(lax.ppermute(array, 'seq', way), span)]  17.7 us
    all_to_all x1, blocking collectives, shards(): lax.all_to_all(decode_q, 'pre', split_axis=0, concat_axis=0, tiled=True)  15.5 us
    ppermute x8, starting transfers between devices, sent(): return [(lax.ppermute(array, 'seq', way), span)]  12.4 us
    ppermute x4, waiting for transfers between devices, shards(): queries[-s] = lax.ppermute(queries[1 - s], 'seq', up)  11.1 us
    ppermute x3, starting transfers between devices, shards(): queries[s] = lax.ppermute(queries[s - 1], 'seq', down)  11 us
    all_to_all x1, blocking collectives, shards(): got = lax.all_to_all(values, 'pre', split_axis=0, concat_axis=0, tiled=True)  10.7 us
    ppermute x3, waiting for transfers between devices, shards(): queries[s] = lax.ppermute(queries[s - 1], 'seq', down)  5.22 us
  transfers between devices with their start and end apart: 31, of which 12 were waited for; matrix products, arithmetic and copies ran while one was open for 0% of the time, Pallas kernels for 4%

profile of v6, /device:TPU:2, one launch (start us, length us, event | category | flops | bytes accessed | tf_op | source)
XLA Modules:
  0.0 114.3 jit_solution(11708524934034642173)
XLA Ops:
  0.0 15.5 %all_to_all.10.refs_4_ = bf16[16,16,576]{2,1,0:T(8,128)(2,1)S(1)} all-to-all(bf16[16,16,576]{2,1,0:T(8,128)(2,1)} %bitcast.7), channel_id=1, replica_groups=mesh['pre'=16,'seq'=8,'dec'=2] {'pre'}, dimensions={0} | all-to-all | bytes 589824 | tf_op jit(solution)/shard_map/all_to_all | solution.py:335
  15.5 1.9 %collective-permute-start = (bf16[16,16,576]{2,1,0:T(8,128)(2,1)S(1)}, bf16[16,16,576]{2,1,0:T(8,128)(2,1)S(1)}, u32[]{:S(2)}, u32[]{:S(2)}) collective-permute-start(bf16[16,16,576]{2,1,0:T(8,128)(2,1)S(1)} %all_to_all.10.refs_4_), channel_id=1, source_target_pairs={{0,2},{2,4},{4,6},{6,8},{8,10},{10,12},{12,14},{14,0},{1,3},{3,5},... | collective-permute-start | bytes 884744 | tf_op jit(solution)/shard_map/ppermute | solution.py:362
  17.4 0.7 copy-done.4
  18.1 0.7 copy-done.5
  18.7 0.7 copy-done.6
  19.4 1.7 %shard_map.73.plan_ref = s32[16,11]{1,0:T(8,128)S(1)} custom-call(s32[1,16]{1,0:T(1,128)S(1)} %copy-done.4, s32[1,16]{1,0:T(1,128)S(1)} %copy-done.5, s32[1,1,1,128]{3,2,1,0:T(1,128)S(1)} %copy-done.6, s32[1]{0:T(128)} %bitcast.1.split_ref), custom_call_target="tpu_custom_call" | custom-call | tf_op jit(solution)/shard_map/pallas_call | solution.py:282
  21.1 4.0 %collective-permute-start.4 = (bf16[16,16,576]{2,1,0:T(8,128)(2,1)S(1)}, bf16[16,16,576]{2,1,0:T(8,128)(2,1)S(1)}, u32[]{:S(2)}, u32[]{:S(2)}) collective-permute-start(bf16[16,16,576]{2,1,0:T(8,128)(2,1)S(1)} %all_to_all.10.refs_4_), channel_id=1, source_target_pairs={{0,14},{2,0},{4,2},{6,4},{8,6},{10,8},{12,10},{14,12},{1,15},{3,1}... | collective-permute-start | bytes 884744 | tf_op jit(solution)/shard_map/ppermute | solution.py:364
  25.1 2.8 %collective-permute-done.refs_3_ = bf16[16,16,576]{2,1,0:T(8,128)(2,1)S(1)} collective-permute-done((bf16[16,16,576]{2,1,0:T(8,128)(2,1)S(1)}, bf16[16,16,576]{2,1,0:T(8,128)(2,1)S(1)}, u32[]{:S(2)}, u32[]{:S(2)}) %collective-permute-start) | collective-permute-done | bytes 294944 | tf_op jit(solution)/shard_map/ppermute | solution.py:362
  27.9 0.0 collective-permute-start.1
  27.9 1.2 %copy-done = bf16[8,512,128]{2,1,0:T(8,128)(2,1)S(1)} copy-done((bf16[8,512,128]{2,1,0:T(8,128)(2,1)S(1)}, bf16[8,512,128]{2,1,0:T(8,128)(2,1)}, u32[]{:S(2)}) %copy-start) | copy-done | bytes 1048600
  29.1 1.0 copy-done.2
  30.1 0.8 copy-done.3
  30.9 0.9 shard_map.74.new_ref
  31.8 3.3 %collective-permute-start.5 = (bf16[16,16,576]{2,1,0:T(8,128)(2,1)S(1)}, bf16[16,16,576]{2,1,0:T(8,128)(2,1)S(1)}, u32[]{:S(2)}, u32[]{:S(2)}) collective-permute-start(bf16[16,16,576]{2,1,0:T(8,128)(2,1)S(1)} %collective-permute-done.4.refs_5_), channel_id=1, source_target_pairs={{0,14},{2,0},{4,2},{6,4},{8,6},{10,8},{12,10},{14,12},{1,15},{3,1}... | collective-permute-start | bytes 884744 | tf_op jit(solution)/shard_map/ppermute | solution.py:364
  35.1 1.6 %collective-permute-done.1.refs_2_ = bf16[16,16,576]{2,1,0:T(8,128)(2,1)S(1)} collective-permute-done((bf16[16,16,576]{2,1,0:T(8,128)(2,1)S(1)}, bf16[16,16,576]{2,1,0:T(8,128)(2,1)S(1)}, u32[]{:S(2)}, u32[]{:S(2)}) %collective-permute-start.1) | collective-permute-done | bytes 294944 | tf_op jit(solution)/shard_map/ppermute | solution.py:362
  36.7 0.0 collective-permute-start.2
  36.7 0.0 collective-permute-start.11
  36.7 0.5 collective-permute-start.12
  37.2 0.0 collective-permute-start.10
  37.2 2.8 %collective-permute-done.5.refs_6_ = bf16[16,16,576]{2,1,0:T(8,128)(2,1)S(1)} collective-permute-done((bf16[16,16,576]{2,1,0:T(8,128)(2,1)S(1)}, bf16[16,16,576]{2,1,0:T(8,128)(2,1)S(1)}, u32[]{:S(2)}, u32[]{:S(2)}) %collective-permute-start.5) | collective-permute-done | bytes 294944 | tf_op jit(solution)/shard_map/ppermute | solution.py:364
  40.0 3.7 %collective-permute-start.6 = (bf16[16,16,576]{2,1,0:T(8,128)(2,1)S(1)}, bf16[16,16,576]{2,1,0:T(8,128)(2,1)S(1)}, u32[]{:S(2)}, u32[]{:S(2)}) collective-permute-start(bf16[16,16,576]{2,1,0:T(8,128)(2,1)S(1)} %collective-permute-done.5.refs_6_), channel_id=1, source_target_pairs={{0,14},{2,0},{4,2},{6,4},{8,6},{10,8},{12,10},{14,12},{1,15},{3,1}... | collective-permute-start | bytes 884744 | tf_op jit(solution)/shard_map/ppermute | solution.py:364
  43.7 1.5 %collective-permute-done.2.refs_1_ = bf16[16,16,576]{2,1,0:T(8,128)(2,1)S(1)} collective-permute-done((bf16[16,16,576]{2,1,0:T(8,128)(2,1)S(1)}, bf16[16,16,576]{2,1,0:T(8,128)(2,1)S(1)}, u32[]{:S(2)}, u32[]{:S(2)}) %collective-permute-start.2) | collective-permute-done | bytes 294944 | tf_op jit(solution)/shard_map/ppermute | solution.py:362
  45.2 0.0 collective-permute-start.3
  45.2 0.0 collective-permute-done.12.refs_13_
  45.2 0.5 collective-permute-start.13
  45.7 0.1 collective-permute-start.8
  45.8 2.5 %collective-permute-done.6.refs_7_ = bf16[16,16,576]{2,1,0:T(8,128)(2,1)S(1)} collective-permute-done((bf16[16,16,576]{2,1,0:T(8,128)(2,1)S(1)}, bf16[16,16,576]{2,1,0:T(8,128)(2,1)S(1)}, u32[]{:S(2)}, u32[]{:S(2)}) %collective-permute-start.6) | collective-permute-done | bytes 294944 | tf_op jit(solution)/shard_map/ppermute | solution.py:364
  48.3 0.0 collective-permute-start.14
  48.3 5.2 %collective-permute-done.3.refs_0_ = bf16[16,16,576]{2,1,0:T(8,128)(2,1)S(1)} collective-permute-done((bf16[16,16,576]{2,1,0:T(8,128)(2,1)S(1)}, bf16[16,16,576]{2,1,0:T(8,128)(2,1)S(1)}, u32[]{:S(2)}, u32[]{:S(2)}) %collective-permute-start.3) | collective-permute-done | bytes 294944 | tf_op jit(solution)/shard_map/ppermute | solution.py:362
  53.5 0.0 collective-permute-start.7
  53.5 0.0 collective-permute-done.14.refs_15_
  53.5 1.6 %collective-permute-done.7.refs_8_ = bf16[16,16,576]{2,1,0:T(8,128)(2,1)S(1)} collective-permute-done((bf16[16,16,576]{2,1,0:T(8,128)(2,1)S(1)}, bf16[16,16,576]{2,1,0:T(8,128)(2,1)S(1)}, u32[]{:S(2)}, u32[]{:S(2)}) %collective-permute-start.7) | collective-permute-done | bytes 294944 | tf_op jit(solution)/shard_map/ppermute | solution.py:332
  55.1 11.9 %shard_map.75 = (bf16[17,16,512]{2,1,0:T(8,128)(2,1)S(1)}, bf16[17,16,512]{2,1,0:T(8,128)(2,1)S(1)}, bf16[17,16,512]{2,1,0:T(8,128)(2,1)S(1)}, bf16[17,16,512]{2...) custom-call(s32[16,11]{1,0:T(8,128)S(1)} %shard_map.73.plan_ref, ...), custom_call_target="tpu_custom_call" | custom-call | tf_op jit(solution)/shard_map/pallas_call | solution.py:282
  67.0 0.2 collective-permute-start.19
  67.3 0.4 collective-permute-start.26
  67.6 0.1 collective-permute-start.18
  67.8 0.9 collective-permute-done.19.refs_1_
  68.7 0.2 shard_map.76
  68.9 0.1 collective-permute-start.20
  69.0 2.0 %collective-permute-start.27 = (bf16[7,16,512]{2,1,0:T(8,128)(2,1)S(1)}, bf16[7,16,512]{2,1,0:T(8,128)(2,1)S(1)}, u32[]{:S(2)}, u32[]{:S(2)}) collective-permute-start(bf16[7,16,512]{2,1,0:T(8,128)(2,1)S(1)} %get-tuple-element.47), channel_id=1, source_target_pairs={{0,2},{2,4},{4,6},{6,8},{8,10},{10,12},{12,14},{14,0},{1,3},{3,5},... | collective-permute-start | bytes 344072 | tf_op jit(solution)/shard_map/ppermute | solution.py:396
  71.0 0.0 collective-permute-start.17
  71.0 0.0 collective-permute-done.26.refs_1_
  71.0 0.5 collective-permute-start.25
  71.5 3.9 %collective-permute-done.27.refs_2_ = bf16[7,16,512]{2,1,0:T(8,128)(2,1)S(1)} collective-permute-done((bf16[7,16,512]{2,1,0:T(8,128)(2,1)S(1)}, bf16[7,16,512]{2,1,0:T(8,128)(2,1)S(1)}, u32[]{:S(2)}, u32[]{:S(2)}) %collective-permute-start.27) | collective-permute-done | bytes 114720 | tf_op jit(solution)/shard_map/ppermute | solution.py:396
  75.4 0.2 shard_map.80
  75.7 0.5 collective-permute-start.28
  76.2 0.0 collective-permute-done.18.refs_1_
  76.2 0.2 shard_map.77
  76.4 2.9 %collective-permute-start.21 = (bf16[17,16,512]{2,1,0:T(8,128)(2,1)S(1)}, bf16[17,16,512]{2,1,0:T(8,128)(2,1)S(1)}, u32[]{:S(2)}, u32[]{:S(2)}) collective-permute-start(bf16[17,16,512]{2,1,0:T(8,128)(2,1)S(1)} %shard_map.77), channel_id=1, source_target_pairs={{0,14},{2,0},{4,2},{6,4},{8,6},{10,8},{12,10},{14,12},{1,15},{3,1}... | collective-permute-start | bytes 835592 | tf_op jit(solution)/shard_map/ppermute | solution.py:396
  79.3 0.5 collective-permute-start.24
  79.8 5.0 %collective-permute-done.28.refs_2_ = bf16[17,16,512]{2,1,0:T(8,128)(2,1)S(1)} collective-permute-done((bf16[17,16,512]{2,1,0:T(8,128)(2,1)S(1)}, bf16[17,16,512]{2,1,0:T(8,128)(2,1)S(1)}, u32[]{:S(2)}, u32[]{:S(2)}) %collective-permute-start.28) | collective-permute-done | bytes 278560 | tf_op jit(solution)/shard_map/ppermute | solution.py:396
  84.8 0.2 shard_map.81
  85.1 0.3 collective-permute-start.29
  85.4 0.2 shard_map.78
  85.6 3.3 %collective-permute-start.22 = (bf16[17,16,512]{2,1,0:T(8,128)(2,1)S(1)}, bf16[17,16,512]{2,1,0:T(8,128)(2,1)S(1)}, u32[]{:S(2)}, u32[]{:S(2)}) collective-permute-start(bf16[17,16,512]{2,1,0:T(8,128)(2,1)S(1)} %shard_map.78), channel_id=1, source_target_pairs={{0,14},{2,0},{4,2},{6,4},{8,6},{10,8},{12,10},{14,12},{1,15},{3,1}... | collective-permute-start | bytes 835592 | tf_op jit(solution)/shard_map/ppermute | solution.py:396
  88.9 4.6 %collective-permute-done.29.refs_2_ = bf16[17,16,512]{2,1,0:T(8,128)(2,1)S(1)} collective-permute-done((bf16[17,16,512]{2,1,0:T(8,128)(2,1)S(1)}, bf16[17,16,512]{2,1,0:T(8,128)(2,1)S(1)}, u32[]{:S(2)}, u32[]{:S(2)}) %collective-permute-start.29) | collective-permute-done | bytes 278560 | tf_op jit(solution)/shard_map/ppermute | solution.py:396
  93.5 0.2 shard_map.82
  93.8 0.1 collective-permute-start.30
  93.9 0.2 shard_map.79
  94.1 3.3 %collective-permute-start.23 = (bf16[17,16,512]{2,1,0:T(8,128)(2,1)S(1)}, bf16[17,16,512]{2,1,0:T(8,128)(2,1)S(1)}, u32[]{:S(2)}, u32[]{:S(2)}) collective-permute-start(bf16[17,16,512]{2,1,0:T(8,128)(2,1)S(1)} %shard_map.79), channel_id=1, source_target_pairs={{0,14},{2,0},{4,2},{6,4},{8,6},{10,8},{12,10},{14,12},{1,15},{3,1}... | collective-permute-start | bytes 835592 | tf_op jit(solution)/shard_map/ppermute | solution.py:396
  97.4 4.2 %collective-permute-done.30.refs_3_ = bf16[17,16,512]{2,1,0:T(8,128)(2,1)S(1)} collective-permute-done((bf16[17,16,512]{2,1,0:T(8,128)(2,1)S(1)}, bf16[17,16,512]{2,1,0:T(8,128)(2,1)S(1)}, u32[]{:S(2)}, u32[]{:S(2)}) %collective-permute-start.30) | collective-permute-done | bytes 278560 | tf_op jit(solution)/shard_map/ppermute | solution.py:396
  101.6 0.9 shard_map.83
  102.6 10.7 %all_to_all.11.cache_ref = f32[16,2,1152]{2,1,0:T(2,128)S(1)} all-to-all(f32[16,2,1152]{2,1,0:T(2,128)S(1)} %shard_map.83), channel_id=1, replica_groups=mesh['pre'=16,'seq'=8,'dec'=2] {'pre'}, dimensions={0} | all-to-all | bytes 294912 | tf_op jit(solution)/shard_map/all_to_all | solution.py:414
  113.3 1.0 shard_map.84
  (26 shorter events, 0.1 us)
Async XLA Ops:
  15.5 12.4 %collective-permute-start = (bf16[16,16,576]{2,1,0:T(8,128)(2,1)S(1)}, bf16[16,16,576]{2,1,0:T(8,128)(2,1)S(1)}, u32[]{:S(2)}, u32[]{:S(2)}) collective-permute-start(bf16[16,16,576]{2,1,0:T(8,128)(2,1)S(1)} %all_to_all.10.refs_4_), channel_id=1, source_target_pairs={{0,2},{2,4},{4,6},{6,8},{8,10},{10,12},{12,14},{14,0},{1,3},{3,5},... | collective-permute-start | bytes 884744 | tf_op jit(solution)/shard_map/ppermute | solution.py:362
  17.4 0.7 copy-start.4
  18.1 0.7 copy-start.5
  18.7 0.7 copy-start.6
  21.1 10.7 %collective-permute-start.4 = (bf16[16,16,576]{2,1,0:T(8,128)(2,1)S(1)}, bf16[16,16,576]{2,1,0:T(8,128)(2,1)S(1)}, u32[]{:S(2)}, u32[]{:S(2)}) collective-permute-start(bf16[16,16,576]{2,1,0:T(8,128)(2,1)S(1)} %all_to_all.10.refs_4_), channel_id=1, source_target_pairs={{0,14},{2,0},{4,2},{6,4},{8,6},{10,8},{12,10},{14,12},{1,15},{3,1}... | collective-permute-start | bytes 884744 | tf_op jit(solution)/shard_map/ppermute | solution.py:364
  27.9 8.8 %collective-permute-start.1 = (bf16[16,16,576]{2,1,0:T(8,128)(2,1)S(1)}, bf16[16,16,576]{2,1,0:T(8,128)(2,1)S(1)}, u32[]{:S(2)}, u32[]{:S(2)}) collective-permute-start(bf16[16,16,576]{2,1,0:T(8,128)(2,1)S(1)} %collective-permute-done.refs_3_), channel_id=1, source_target_pairs={{0,2},{2,4},{4,6},{6,8},{8,10},{10,12},{12,14},{14,0},{1,3},{3,5},... | collective-permute-start | bytes 884744 | tf_op jit(solution)/shard_map/ppermute | solution.py:362
  27.9 1.2 %copy-start = (bf16[8,512,128]{2,1,0:T(8,128)(2,1)S(1)}, bf16[8,512,128]{2,1,0:T(8,128)(2,1)}, u32[]{:S(2)}) copy-start(bf16[8,512,128]{2,1,0:T(8,128)(2,1)} %refs_4_.1) | copy-start | bytes 3145732
  29.1 1.0 copy-start.2
  30.1 0.8 copy-start.3
  31.8 8.2 %collective-permute-start.5 = (bf16[16,16,576]{2,1,0:T(8,128)(2,1)S(1)}, bf16[16,16,576]{2,1,0:T(8,128)(2,1)S(1)}, u32[]{:S(2)}, u32[]{:S(2)}) collective-permute-start(bf16[16,16,576]{2,1,0:T(8,128)(2,1)S(1)} %collective-permute-done.4.refs_5_), channel_id=1, source_target_pairs={{0,14},{2,0},{4,2},{6,4},{8,6},{10,8},{12,10},{14,12},{1,15},{3,1}... | collective-permute-start | bytes 884744 | tf_op jit(solution)/shard_map/ppermute | solution.py:364
  36.7 8.5 %collective-permute-start.2 = (bf16[16,16,576]{2,1,0:T(8,128)(2,1)S(1)}, bf16[16,16,576]{2,1,0:T(8,128)(2,1)S(1)}, u32[]{:S(2)}, u32[]{:S(2)}) collective-permute-start(bf16[16,16,576]{2,1,0:T(8,128)(2,1)S(1)} %collective-permute-done.1.refs_2_), channel_id=1, source_target_pairs={{0,2},{2,4},{4,6},{6,8},{8,10},{10,12},{12,14},{14,0},{1,3},{3,5},... | collective-permute-start | bytes 884744 | tf_op jit(solution)/shard_map/ppermute | solution.py:362
  36.7 8.5 %collective-permute-start.11 = (bf16[16,16,576]{2,1,0:T(8,128)(2,1)S(1)}, bf16[16,16,576]{2,1,0:T(8,128)(2,1)S(1)}, u32[]{:S(2)}, u32[]{:S(2)}) collective-permute-start(bf16[16,16,576]{2,1,0:T(8,128)(2,1)S(1)} %all_to_all.10.refs_4_), channel_id=1, source_target_pairs={{0,1},{1,0},{2,3},{3,2},{4,5},{5,4},{6,7},{7,6},{8,9},{9,8},{10,11... | collective-permute-start | bytes 884744 | tf_op jit(solution)/shard_map/ppermute | solution.py:332
  36.7 8.5 %collective-permute-start.12 = (bf16[16,16,576]{2,1,0:T(8,128)(2,1)S(1)}, bf16[16,16,576]{2,1,0:T(8,128)(2,1)S(1)}, u32[]{:S(2)}, u32[]{:S(2)}) collective-permute-start(bf16[16,16,576]{2,1,0:T(8,128)(2,1)S(1)} %collective-permute-done.4.refs_5_), channel_id=1, source_target_pairs={{0,1},{1,0},{2,3},{3,2},{4,5},{5,4},{6,7},{7,6},{8,9},{9,8},{10,11... | collective-permute-start | bytes 884744 | tf_op jit(solution)/shard_map/ppermute | solution.py:332
  37.2 8.5 %collective-permute-start.10 = (bf16[16,16,576]{2,1,0:T(8,128)(2,1)S(1)}, bf16[16,16,576]{2,1,0:T(8,128)(2,1)S(1)}, u32[]{:S(2)}, u32[]{:S(2)}) collective-permute-start(bf16[16,16,576]{2,1,0:T(8,128)(2,1)S(1)} %collective-permute-done.refs_3_), channel_id=1, source_target_pairs={{0,1},{1,0},{2,3},{3,2},{4,5},{5,4},{6,7},{7,6},{8,9},{9,8},{10,11... | collective-permute-start | bytes 884744 | tf_op jit(solution)/shard_map/ppermute | solution.py:332
  40.0 8.3 %collective-permute-start.6 = (bf16[16,16,576]{2,1,0:T(8,128)(2,1)S(1)}, bf16[16,16,576]{2,1,0:T(8,128)(2,1)S(1)}, u32[]{:S(2)}, u32[]{:S(2)}) collective-permute-start(bf16[16,16,576]{2,1,0:T(8,128)(2,1)S(1)} %collective-permute-done.5.refs_6_), channel_id=1, source_target_pairs={{0,14},{2,0},{4,2},{6,4},{8,6},{10,8},{12,10},{14,12},{1,15},{3,1}... | collective-permute-start | bytes 884744 | tf_op jit(solution)/shard_map/ppermute | solution.py:364
  45.2 8.3 %collective-permute-start.3 = (bf16[16,16,576]{2,1,0:T(8,128)(2,1)S(1)}, bf16[16,16,576]{2,1,0:T(8,128)(2,1)S(1)}, u32[]{:S(2)}, u32[]{:S(2)}) collective-permute-start(bf16[16,16,576]{2,1,0:T(8,128)(2,1)S(1)} %collective-permute-done.2.refs_1_), channel_id=1, source_target_pairs={{0,2},{2,4},{4,6},{6,8},{8,10},{10,12},{12,14},{14,0},{1,3},{3,5},... | collective-permute-start | bytes 884744 | tf_op jit(solution)/shard_map/ppermute | solution.py:362
  45.2 8.3 %collective-permute-start.9 = (bf16[16,16,576]{2,1,0:T(8,128)(2,1)S(1)}, bf16[16,16,576]{2,1,0:T(8,128)(2,1)S(1)}, u32[]{:S(2)}, u32[]{:S(2)}) collective-permute-start(bf16[16,16,576]{2,1,0:T(8,128)(2,1)S(1)} %collective-permute-done.1.refs_2_), channel_id=1, source_target_pairs={{0,1},{1,0},{2,3},{3,2},{4,5},{5,4},{6,7},{7,6},{8,9},{9,8},{10,11... | collective-permute-start | bytes 884744 | tf_op jit(solution)/shard_map/ppermute | solution.py:332
  45.2 8.3 %collective-permute-start.13 = (bf16[16,16,576]{2,1,0:T(8,128)(2,1)S(1)}, bf16[16,16,576]{2,1,0:T(8,128)(2,1)S(1)}, u32[]{:S(2)}, u32[]{:S(2)}) collective-permute-start(bf16[16,16,576]{2,1,0:T(8,128)(2,1)S(1)} %collective-permute-done.5.refs_6_), channel_id=1, source_target_pairs={{0,1},{1,0},{2,3},{3,2},{4,5},{5,4},{6,7},{7,6},{8,9},{9,8},{10,11... | collective-permute-start | bytes 884744 | tf_op jit(solution)/shard_map/ppermute | solution.py:332
  45.7 7.8 %collective-permute-start.8 = (bf16[16,16,576]{2,1,0:T(8,128)(2,1)S(1)}, bf16[16,16,576]{2,1,0:T(8,128)(2,1)S(1)}, u32[]{:S(2)}, u32[]{:S(2)}) collective-permute-start(bf16[16,16,576]{2,1,0:T(8,128)(2,1)S(1)} %collective-permute-done.2.refs_1_), channel_id=1, source_target_pairs={{0,1},{1,0},{2,3},{3,2},{4,5},{5,4},{6,7},{7,6},{8,9},{9,8},{10,11... | collective-permute-start | bytes 884744 | tf_op jit(solution)/shard_map/ppermute | solution.py:332
  48.3 5.2 %collective-permute-start.14 = (bf16[16,16,576]{2,1,0:T(8,128)(2,1)S(1)}, bf16[16,16,576]{2,1,0:T(8,128)(2,1)S(1)}, u32[]{:S(2)}, u32[]{:S(2)}) collective-permute-start(bf16[16,16,576]{2,1,0:T(8,128)(2,1)S(1)} %collective-permute-done.6.refs_7_), channel_id=1, source_target_pairs={{0,1},{1,0},{2,3},{3,2},{4,5},{5,4},{6,7},{7,6},{8,9},{9,8},{10,11... | collective-permute-start | bytes 884744 | tf_op jit(solution)/shard_map/ppermute | solution.py:332
  53.5 1.6 %collective-permute-start.7 = (bf16[16,16,576]{2,1,0:T(8,128)(2,1)S(1)}, bf16[16,16,576]{2,1,0:T(8,128)(2,1)S(1)}, u32[]{:S(2)}, u32[]{:S(2)}) collective-permute-start(bf16[16,16,576]{2,1,0:T(8,128)(2,1)S(1)} %collective-permute-done.3.refs_0_), channel_id=1, source_target_pairs={{0,1},{1,0},{2,3},{3,2},{4,5},{5,4},{6,7},{7,6},{8,9},{9,8},{10,11... | collective-permute-start | bytes 884744 | tf_op jit(solution)/shard_map/ppermute | solution.py:332
  55.1 46.5 %copy-start.1 = (bf16[8,512,128]{2,1,0:T(8,128)(2,1)S(1)}, bf16[8,512,128]{2,1,0:T(8,128)(2,1)}, u32[]{:S(2)}) copy-start(bf16[8,512,128]{2,1,0:T(8,128)(2,1)} %refs_4_.1) | copy-start | bytes 3145732
  67.0 1.6 %collective-permute-start.19 = (bf16[17,16,512]{2,1,0:T(8,128)(2,1)S(1)}, bf16[17,16,512]{2,1,0:T(8,128)(2,1)S(1)}, u32[]{:S(2)}, u32[]{:S(2)}) collective-permute-start(bf16[17,16,512]{2,1,0:T(8,128)(2,1)S(1)} %get-tuple-element.39), channel_id=1, source_target_pairs={{0,1},{1,0},{2,3},{3,2},{4,5},{5,4},{6,7},{7,6},{8,9},{9,8},{10,11... | collective-permute-start | bytes 835592 | tf_op jit(solution)/shard_map/ppermute | solution.py:332
  67.3 3.7 %collective-permute-start.26 = (bf16[17,16,512]{2,1,0:T(8,128)(2,1)S(1)}, bf16[17,16,512]{2,1,0:T(8,128)(2,1)S(1)}, u32[]{:S(2)}, u32[]{:S(2)}) collective-permute-start(bf16[17,16,512]{2,1,0:T(8,128)(2,1)S(1)} %get-tuple-element.46), channel_id=1, source_target_pairs={{0,1},{1,0},{2,3},{3,2},{4,5},{5,4},{6,7},{7,6},{8,9},{9,8},{10,11... | collective-permute-start | bytes 835592 | tf_op jit(solution)/shard_map/ppermute | solution.py:332
  67.6 8.5 %collective-permute-start.18 = (bf16[17,16,512]{2,1,0:T(8,128)(2,1)S(1)}, bf16[17,16,512]{2,1,0:T(8,128)(2,1)S(1)}, u32[]{:S(2)}, u32[]{:S(2)}) collective-permute-start(bf16[17,16,512]{2,1,0:T(8,128)(2,1)S(1)} %get-tuple-element.37), channel_id=1, source_target_pairs={{0,1},{1,0},{2,3},{3,2},{4,5},{5,4},{6,7},{7,6},{8,9},{9,8},{10,11... | collective-permute-start | bytes 835592 | tf_op jit(solution)/shard_map/ppermute | solution.py:332
  68.9 7.3 %collective-permute-start.20 = (bf16[11,16,512]{2,1,0:T(8,128)(2,1)S(1)}, bf16[11,16,512]{2,1,0:T(8,128)(2,1)S(1)}, u32[]{:S(2)}, u32[]{:S(2)}) collective-permute-start(bf16[11,16,512]{2,1,0:T(8,128)(2,1)S(1)} %get-tuple-element.40), channel_id=1, source_target_pairs={{0,14},{2,0},{4,2},{6,4},{8,6},{10,8},{12,10},{14,12},{1,15},{3,1}... | collective-permute-start | bytes 540680 | tf_op jit(solution)/shard_map/ppermute | solution.py:396
  69.0 6.5 %collective-permute-start.27 = (bf16[7,16,512]{2,1,0:T(8,128)(2,1)S(1)}, bf16[7,16,512]{2,1,0:T(8,128)(2,1)S(1)}, u32[]{:S(2)}, u32[]{:S(2)}) collective-permute-start(bf16[7,16,512]{2,1,0:T(8,128)(2,1)S(1)} %get-tuple-element.47), channel_id=1, source_target_pairs={{0,2},{2,4},{4,6},{6,8},{8,10},{10,12},{12,14},{14,0},{1,3},{3,5},... | collective-permute-start | bytes 344072 | tf_op jit(solution)/shard_map/ppermute | solution.py:396
  71.0 14.4 %collective-permute-start.17 = (bf16[17,16,512]{2,1,0:T(8,128)(2,1)S(1)}, bf16[17,16,512]{2,1,0:T(8,128)(2,1)S(1)}, u32[]{:S(2)}, u32[]{:S(2)}) collective-permute-start(bf16[17,16,512]{2,1,0:T(8,128)(2,1)S(1)} %get-tuple-element.35), channel_id=1, source_target_pairs={{0,1},{1,0},{2,3},{3,2},{4,5},{5,4},{6,7},{7,6},{8,9},{9,8},{10,11... | collective-permute-start | bytes 835592 | tf_op jit(solution)/shard_map/ppermute | solution.py:332
  71.0 8.3 %collective-permute-start.25 = (bf16[17,16,512]{2,1,0:T(8,128)(2,1)S(1)}, bf16[17,16,512]{2,1,0:T(8,128)(2,1)S(1)}, u32[]{:S(2)}, u32[]{:S(2)}) collective-permute-start(bf16[17,16,512]{2,1,0:T(8,128)(2,1)S(1)} %get-tuple-element.44), channel_id=1, source_target_pairs={{0,1},{1,0},{2,3},{3,2},{4,5},{5,4},{6,7},{7,6},{8,9},{9,8},{10,11... | collective-permute-start | bytes 835592 | tf_op jit(solution)/shard_map/ppermute | solution.py:332
  75.7 9.2 %collective-permute-start.28 = (bf16[17,16,512]{2,1,0:T(8,128)(2,1)S(1)}, bf16[17,16,512]{2,1,0:T(8,128)(2,1)S(1)}, u32[]{:S(2)}, u32[]{:S(2)}) collective-permute-start(bf16[17,16,512]{2,1,0:T(8,128)(2,1)S(1)} %shard_map.80), channel_id=1, source_target_pairs={{0,2},{2,4},{4,6},{6,8},{8,10},{10,12},{12,14},{14,0},{1,3},{3,5},... | collective-permute-start | bytes 835592 | tf_op jit(solution)/shard_map/ppermute | solution.py:396
  76.4 9.0 %collective-permute-start.21 = (bf16[17,16,512]{2,1,0:T(8,128)(2,1)S(1)}, bf16[17,16,512]{2,1,0:T(8,128)(2,1)S(1)}, u32[]{:S(2)}, u32[]{:S(2)}) collective-permute-start(bf16[17,16,512]{2,1,0:T(8,128)(2,1)S(1)} %shard_map.77), channel_id=1, source_target_pairs={{0,14},{2,0},{4,2},{6,4},{8,6},{10,8},{12,10},{14,12},{1,15},{3,1}... | collective-permute-start | bytes 835592 | tf_op jit(solution)/shard_map/ppermute | solution.py:396
  79.3 14.6 %collective-permute-start.16 = (bf16[17,16,512]{2,1,0:T(8,128)(2,1)S(1)}, bf16[17,16,512]{2,1,0:T(8,128)(2,1)S(1)}, u32[]{:S(2)}, u32[]{:S(2)}) collective-permute-start(bf16[17,16,512]{2,1,0:T(8,128)(2,1)S(1)} %get-tuple-element.33), channel_id=1, source_target_pairs={{0,1},{1,0},{2,3},{3,2},{4,5},{5,4},{6,7},{7,6},{8,9},{9,8},{10,11... | collective-permute-start | bytes 835592 | tf_op jit(solution)/shard_map/ppermute | solution.py:332
  79.3 9.7 %collective-permute-start.24 = (bf16[17,16,512]{2,1,0:T(8,128)(2,1)S(1)}, bf16[17,16,512]{2,1,0:T(8,128)(2,1)S(1)}, u32[]{:S(2)}, u32[]{:S(2)}) collective-permute-start(bf16[17,16,512]{2,1,0:T(8,128)(2,1)S(1)} %get-tuple-element.42), channel_id=1, source_target_pairs={{0,1},{1,0},{2,3},{3,2},{4,5},{5,4},{6,7},{7,6},{8,9},{9,8},{10,11... | collective-permute-start | bytes 835592 | tf_op jit(solution)/shard_map/ppermute | solution.py:332
  85.1 8.5 %collective-permute-start.29 = (bf16[17,16,512]{2,1,0:T(8,128)(2,1)S(1)}, bf16[17,16,512]{2,1,0:T(8,128)(2,1)S(1)}, u32[]{:S(2)}, u32[]{:S(2)}) collective-permute-start(bf16[17,16,512]{2,1,0:T(8,128)(2,1)S(1)} %shard_map.81), channel_id=1, source_target_pairs={{0,2},{2,4},{4,6},{6,8},{8,10},{10,12},{12,14},{14,0},{1,3},{3,5},... | collective-permute-start | bytes 835592 | tf_op jit(solution)/shard_map/ppermute | solution.py:396
  85.6 8.2 %collective-permute-start.22 = (bf16[17,16,512]{2,1,0:T(8,128)(2,1)S(1)}, bf16[17,16,512]{2,1,0:T(8,128)(2,1)S(1)}, u32[]{:S(2)}, u32[]{:S(2)}) collective-permute-start(bf16[17,16,512]{2,1,0:T(8,128)(2,1)S(1)} %shard_map.78), channel_id=1, source_target_pairs={{0,14},{2,0},{4,2},{6,4},{8,6},{10,8},{12,10},{14,12},{1,15},{3,1}... | collective-permute-start | bytes 835592 | tf_op jit(solution)/shard_map/ppermute | solution.py:396
  88.9 8.5 %collective-permute-start.15 = (bf16[17,16,512]{2,1,0:T(8,128)(2,1)S(1)}, bf16[17,16,512]{2,1,0:T(8,128)(2,1)S(1)}, u32[]{:S(2)}, u32[]{:S(2)}) collective-permute-start(bf16[17,16,512]{2,1,0:T(8,128)(2,1)S(1)} %get-tuple-element.31), channel_id=1, source_target_pairs={{0,1},{1,0},{2,3},{3,2},{4,5},{5,4},{6,7},{7,6},{8,9},{9,8},{10,11... | collective-permute-start | bytes 835592 | tf_op jit(solution)/shard_map/ppermute | solution.py:332
  93.8 7.8 %collective-permute-start.30 = (bf16[17,16,512]{2,1,0:T(8,128)(2,1)S(1)}, bf16[17,16,512]{2,1,0:T(8,128)(2,1)S(1)}, u32[]{:S(2)}, u32[]{:S(2)}) collective-permute-start(bf16[17,16,512]{2,1,0:T(8,128)(2,1)S(1)} %shard_map.82), channel_id=1, source_target_pairs={{0,2},{2,4},{4,6},{6,8},{8,10},{10,12},{12,14},{14,0},{1,3},{3,5},... | collective-permute-start | bytes 835592 | tf_op jit(solution)/shard_map/ppermute | solution.py:396
  94.1 7.5 %collective-permute-start.23 = (bf16[17,16,512]{2,1,0:T(8,128)(2,1)S(1)}, bf16[17,16,512]{2,1,0:T(8,128)(2,1)S(1)}, u32[]{:S(2)}, u32[]{:S(2)}) collective-permute-start(bf16[17,16,512]{2,1,0:T(8,128)(2,1)S(1)} %shard_map.79), channel_id=1, source_target_pairs={{0,14},{2,0},{4,2},{6,4},{8,6},{10,8},{12,10},{14,12},{1,15},{3,1}... | collective-permute-start | bytes 835592 | tf_op jit(solution)/shard_map/ppermute | solution.py:396
